TPU v7x, 32 devices: a whole 2x2x4 slice. The times are simulated.
32 devices in a mesh: req: 8 (over z, y), mlp: 4 (over x, core).
Axes of the slice: x: 2, y: 2, z: 4, core: 2. Of those that a mesh axis runs over, the one named last changes fastest.
Arguments:
- queries: bfloat16 [1024, 5120], P('req', 'mlp'), may hold values from -6 to 6
- leaf_keys: bfloat16 [1024, 1024], P('req', 'mlp'), may hold values from -6 to 6
- leaf_token_values: bfloat16 [1024, 1024], P('req', 'mlp'), may hold values from -6 to 6
- key_value_pages: bfloat16 [256, 64, 2, 1024], P('req', None, None, 'mlp'), may hold values from -6 to 6
- page_holder: int32 [8, 6, 4], replicated, may hold values from 0 to 7, as said below
- page_slot: int32 [8, 6, 4], replicated, may hold values from 0 to 31
- segment_ids: int32 [1024], P('req'), may hold values from 0 to 7, as said below
- req_parent: int32 [8, 8], P('req'), may hold values from 0 to 3
- mid_parent: int32 [8, 4], P('req'), may hold values from 0 to 1
- node_len: int32 [8, 6], P('req'), may hold values from 1 to 256
- residual: bfloat16 [1024, 5120], P('req'), may hold values from -6 to 6
- out_proj: bfloat16 [5120, 5120], P('mlp'), may hold values from -0.078125 to 0.078125
- norm_gain: float32 [5120], replicated, may hold values from 0.5 to 1.5
- gate_proj: bfloat16 [5120, 13824], P(None, ('req', 'mlp')), may hold values from -0.078125 to 0.078125
- up_proj: bfloat16 [5120, 13824], P(None, ('req', 'mlp')), may hold values from -0.078125 to 0.078125
- down_proj: bfloat16 [13824, 5120], P(('req', 'mlp')), may hold values from -0.0546875 to 0.0546875
- next_gain: float32 [5120], replicated, may hold values from 0.5 to 1.5
- qkv_proj: bfloat16 [5120, 7168], P(None, 'mlp'), may hold values from -0.078125 to 0.078125
- qkv_bias: float32 [7168], P('mlp'), may hold values from -3 to 3
Outputs:
- layer_out: bfloat16 [1024, 5120], P(('req', 'mlp'))
- qkv_out: bfloat16 [1024, 7168], P('req', 'mlp')
Inputs may be any that keep to these rules, and one draw needn't show every extreme that they name: `segment_ids`: within each block of 128 tokens of one group the ids never fall, start at 0, and every id 0 to 7 occurs. `page_holder`: in each row (one group's prefix pages) exactly half of the entries name the row's own group; the other entries name other groups, no group more than 2 times in a row, and some group exactly 2 times.
All inputs are finite; a program needn't handle non-finite values.
Results may differ from a plain program's by a relative error of at most 0.02.
Values may be sent and summed in bfloat16 or wider, within the bound.
No kernel may reach another device: no remote copies, remote signals or barrier semaphores. Data moves between devices by JAX's collectives and lax.ppermute only.
A program may use at most 192 MiB of HBM per device.

v0:
```python
import math

import jax
import jax.numpy as jnp
from jax import lax
from jax.sharding import PartitionSpec as P

HEAD_SIZE = 128
QUERY_PER_KV = 5
REQ_DEV = 8
ROOT_DEV = 2
MID_DEV = 4
NODES_DEV = 6
NODE_MAX = 256


EPS = 1e-06


def rms_norm(stream, gain):
    values = stream.astype(jnp.float32)
    mean_sq = jnp.mean(values * values, axis=-1, keepdims=True)
    return (values * lax.rsqrt(mean_sq + EPS) * gain).astype(jnp.bfloat16)


def attend(
    queries,
    leaf_keys,
    leaf_token_values,
    prefix_keys,
    prefix_values,
    segments,
    parents,
    roots,
    lengths,
):
    tokens = queries.shape[0]
    heads_kv = leaf_keys.shape[1] // HEAD_SIZE
    query_rows = queries.reshape(tokens, heads_kv, QUERY_PER_KV, HEAD_SIZE)
    keys = jnp.concatenate(
        [
            prefix_keys.reshape(-1, heads_kv, HEAD_SIZE),
            leaf_keys.reshape(tokens, heads_kv, HEAD_SIZE),
        ],
        0,
    )
    values = jnp.concatenate(
        [
            prefix_values.reshape(-1, heads_kv, HEAD_SIZE),
            leaf_token_values.reshape(tokens, heads_kv, HEAD_SIZE),
        ],
        0,
    )
    middle = jnp.sum((segments[:, None] == jnp.arange(REQ_DEV)[None, :]) * parents[None, :], axis=1)
    root = jnp.sum((middle[:, None] == jnp.arange(MID_DEV)[None, :]) * roots[None, :], axis=1)
    node = jnp.arange(NODES_DEV * NODE_MAX) // NODE_MAX
    inside = (jnp.arange(NODE_MAX)[None, :] < lengths[:, None]).reshape(-1)
    prefix_mask = (
        (node[None, :] == root[:, None]) | (node[None, :] == ROOT_DEV + middle[:, None])
    ) & inside[None, :]
    place = jnp.arange(tokens)
    leaf_mask = (segments[None, :] == segments[:, None]) & (place[None, :] <= place[:, None])
    mask = jnp.concatenate([prefix_mask, leaf_mask], 1)
    score = jnp.einsum(
        "tkgd,skd->tkgs", query_rows, keys, preferred_element_type=jnp.float32
    ) / math.sqrt(HEAD_SIZE)
    score = jnp.where(mask[:, None, None, :], score, -1e30)
    top = jnp.max(score, axis=-1, keepdims=True)
    expo = jnp.where(mask[:, None, None, :], jnp.exp(score - top), 0.0)
    total = jnp.sum(expo, axis=-1, keepdims=True)
    weights = expo.astype(jnp.bfloat16)
    summed = jnp.einsum("tkgs,skd->tkgd", weights, values, preferred_element_type=jnp.float32)
    return (summed / total).astype(jnp.bfloat16).reshape(tokens, -1)


def fetch_prefix(key_value_pages, page_holder, page_slot):
    groups = lax.axis_size("req")
    myself = lax.axis_index("req")
    holders = page_holder.reshape(groups, -1)
    slots = page_slot.reshape(groups, -1)
    token_count = holders.shape[1]
    room = (token_count // 2 + groups - 2) // (groups - 1)
    earlier = jnp.arange(token_count)[None, :] < jnp.arange(token_count)[:, None]
    same = holders[:, :, None] == holders[:, None, :]
    rank = jnp.sum(same & earlier[None, :, :], axis=-1)
    asked = (holders == myself) & (jnp.arange(groups)[:, None] != myself)
    picked = asked[:, None, :] & (rank[:, None, :] == jnp.arange(room)[None, :, None])
    send_slot = jnp.sum(jnp.where(picked, slots[:, None, :], 0), axis=-1)
    outgoing = key_value_pages[send_slot]
    incoming = lax.all_to_all(outgoing, "req", split_axis=0, concat_axis=0, tiled=True)
    flat_in = incoming.reshape((groups * room,) + incoming.shape[2:])
    own_holders = lax.dynamic_index_in_dim(holders, myself, 0, keepdims=False)
    own_slots = lax.dynamic_index_in_dim(slots, myself, 0, keepdims=False)
    own_rank = lax.dynamic_index_in_dim(rank, myself, 0, keepdims=False)
    remote = flat_in[own_holders * room + jnp.minimum(own_rank, room - 1)]
    local = key_value_pages[own_slots]
    pages = jnp.where((own_holders == myself)[:, None, None, None], local, remote)
    return pages.reshape(NODES_DEV * NODE_MAX, 2, -1)


def body(
    queries,
    leaf_keys,
    leaf_token_values,
    key_value_pages,
    page_holder,
    page_slot,
    segment_ids,
    req_parent,
    mid_parent,
    node_len,
    residual,
    out_proj,
    norm_gain,
    gate_proj,
    up_proj,
    down_proj,
    next_gain,
    qkv_proj,
    qkv_bias,
):
    prefix = fetch_prefix(key_value_pages, page_holder, page_slot)
    attention = attend(
        queries,
        leaf_keys,
        leaf_token_values,
        prefix[:, 0],
        prefix[:, 1],
        segment_ids,
        req_parent[0],
        mid_parent[0],
        node_len[0],
    )
    projected = jnp.dot(attention, out_proj, preferred_element_type=jnp.float32)
    group_tokens = queries.shape[0]
    groups = lax.axis_size("req")
    members = lax.axis_size("mlp")
    rows_mlp = group_tokens // members
    first_row = lax.axis_index("mlp") * rows_mlp
    head_part = lax.psum_scatter(
        projected.astype(jnp.bfloat16), "mlp", scatter_dimension=0, tiled=True
    ).astype(jnp.float32)
    own_resid = lax.dynamic_slice_in_dim(residual, first_row, rows_mlp, 0)
    stream = (own_resid.astype(jnp.float32) + head_part).astype(jnp.bfloat16)
    normed = rms_norm(stream, norm_gain)
    piece = lax.all_gather(normed, ("req", "mlp"), axis=0, tiled=True)
    gate = jnp.dot(piece, gate_proj, preferred_element_type=jnp.float32)
    upper = jnp.dot(piece, up_proj, preferred_element_type=jnp.float32)
    hidden_all = (jax.nn.silu(gate) * upper).astype(jnp.bfloat16)
    blocks = hidden_all.reshape(groups, members, rows_mlp, -1)
    regrouped = lax.all_to_all(blocks, "mlp", split_axis=1, concat_axis=3, tiled=True)
    hidden = regrouped.reshape(groups * rows_mlp, -1)
    mixed_all = jnp.dot(
        hidden,
        lax.all_gather(down_proj, "mlp", axis=0, tiled=True),
        preferred_element_type=jnp.float32,
    )
    mixed = lax.psum_scatter(
        mixed_all.astype(jnp.bfloat16), "req", scatter_dimension=0, tiled=True
    ).astype(jnp.float32)
    layer_out = (stream.astype(jnp.float32) + mixed).astype(jnp.bfloat16)
    next_rows = rms_norm(layer_out, next_gain)
    next_normed = lax.all_gather(next_rows, "mlp", axis=0, tiled=True)
    qkv_out = (
        jnp.dot(next_normed, qkv_proj, preferred_element_type=jnp.float32) + qkv_bias
    ).astype(jnp.bfloat16)
    return (layer_out, qkv_out)


def solution(mesh):
    placed = (
        P("req", "mlp"),
        P("req", "mlp"),
        P("req", "mlp"),
        P("req", None, None, "mlp"),
        P(),
        P(),
        P("req"),
        P("req", None),
        P("req", None),
        P("req", None),
        P("req", None),
        P("mlp", None),
        P(),
        P(None, ("req", "mlp")),
        P(None, ("req", "mlp")),
        P(("req", "mlp"), None),
        P(),
        P(None, "mlp"),
        P("mlp"),
    )
    return jax.shard_map(
        body,
        mesh=mesh,
        in_specs=placed,
        out_specs=(P(("req", "mlp"), None), P("req", "mlp")),
        check_vma=False,
    )
```

profile of v0, /device:TPU:0, one launch (start us, length us, event | category | flops | bytes accessed | tf_op | source)
XLA Modules:
  0.0 428.7 jit_solution(16138540161181441922)
XLA Ops:
  10.3 2.7 gather_fusion.1
  13.0 1.2 copy.102
  14.2 7.3 %all-to-all-start = ((bf16[8,2,64,2,256]{4,2,3,1,0:T(8,128)(2,1)}), bf16[8,2,64,2,256]{4,2,3,1,0:T(8,128)(2,1)S(1)}, u32[]{:S(2)}, u32[]{:S(2)}) async-start(bf16[8,2,64,2,256]{4,2,3,1,0:T(8,128)(2,1)} %copy.102), calls=%async_computation | async-start | bytes 2097152 | tf_op jit(solution)/shard_map/all_to_all | solution.py:90
  21.9 6.0 %gather_fusion = bf16[24,64,2,256]{3,2,1,0:T(2,128)(2,1)} fusion(bf16[32,64,2,256]{3,2,1,0:T(2,128)(2,1)S(1)} %copy-done, s32[1024]{0:T(1024)S(1)} %pad_clamp_fusion.2), kind=kCustom, calls=%fused_computation | custom fusion | bytes 3145824 | tf_op jit(solution)/shard_map/gather | solution.py:96
  27.9 1.8 copy.96
  31.9 15.3 %all-to-all-done = bf16[8,2,64,2,256]{4,2,3,1,0:T(8,128)(2,1)S(1)} async-done(((bf16[8,2,64,2,256]{4,2,3,1,0:T(8,128)(2,1)}), bf16[8,2,64,2,256]{4,2,3,1,0:T(8,128)(2,1)S(1)}, u32[]{:S(2)}, u32[]{:S(2)}) %all-to-all-start) | async-done | bytes 1048608 | tf_op jit(solution)/shard_map/all_to_all | solution.py:90
  47.2 1.9 gather_fusion.2
  49.1 1.5 copy.103
  52.2 5.5 %fusion.48 = (f32[128,2,5]{0,2,1:T(8,128)S(1)}, bf16[128,2,5,1664]{0,3,2,1:T(8,128)(2,1)}) fusion(pred[128,1664]{0,1:T(8,128)(4,1)S(1)} %pad_add_fusion, bf16[128,2,5,128]{0,3,2,1:T(8,128)(2,1)S(1)} %bitcast.97, bf16[128,2,128]{2,0,1:T(8,128)(2,1)S(1)} %copy.109, bf16[1536,2,128]{2,0,1:T(8,128)(2,1)S(1)} %copy.108), kind=kOutput, calls=%fused_computation.87 | convolution fusion | flops 559744640 | bytes 5657600 | tf_op jit(solution)/shard_map/sub | solution.py:69
  57.8 3.1 fusion.14
  60.9 7.7 %convolution_convert_fusion.1 = bf16[128,5120]{1,0:T(8,128)(2,1)} fusion(bf16[128,1280]{0,1:T(8,128)(2,1)S(1)} %bitcast.96, bf16[1280,5120]{1,0:T(8,128)(2,1)} %param.30), kind=kOutput, calls=%fused_computation.8 | convolution fusion | flops 1678376960 | bytes 14745600 | tf_op jit(solution)/shard_map/dot_general | solution.py:134
  68.7 25.6 %reduce-scatter.3.cloned.1.call-done = bf16[32,5120]{1,0:T(8,128)(2,1)} async-done(((bf16[128,5120]{1,0:T(8,128)(2,1)}), bf16[32,5120]{1,0:T(8,128)(2,1)}) %reduce-scatter.3.cloned.1.call-update) | async-done | bytes 327696 | tf_op jit(solution)/shard_map/reduce_scatter | solution.py:140
  94.3 1.3 fusion.24
  97.5 87.4 %all-gather.4.cloned.1.call-done = bf16[1024,5120]{1,0:T(8,128)(2,1)} async-done(((bf16[32,5120]{1,0:T(8,128)(2,1)}), bf16[1024,5120]{1,0:T(8,128)(2,1)}) %all-gather.4.cloned.1.call-update) | async-done | bytes 10485776 | tf_op jit(solution)/shard_map/all_gather | solution.py:146
  184.9 8.9 %fusion.49 = f32[1024,432]{0,1:T(8,128)S(1)} fusion(bf16[1024,5120]{1,0:T(8,128)(2,1)} %all-gather.4.cloned.1.call-done, bf16[5120,432]{0,1:T(8,128)(2,1)} %param.32), kind=kOutput, calls=%fused_computation.88 | convolution fusion | flops 4529848320 | bytes 16678912 | tf_op jit(solution)/shard_map/dot_general | solution.py:147
  194.5 8.0 %multiply_convert_fusion = bf16[1024,432]{0,1:T(8,128)(2,1)S(1)} fusion(f32[1024,432]{0,1:T(8,128)S(1)} %fusion.49, bf16[1024,5120]{1,0:T(8,128)(2,1)S(1)} %copy-done.11, bf16[5120,432]{0,1:T(8,128)(2,1)} %param.33), kind=kOutput, calls=%fused_computation.16 | convolution fusion | flops 4532502528 | bytes 17563648 | tf_op jit(solution)/shard_map/dot_general | solution.py:148
  203.1 28.4 %all_to_all.20 = bf16[8,4,32,432]{3,2,0,1:T(8,128)(2,1)S(1)} all-to-all(bf16[8,4,32,432]{3,2,0,1:T(8,128)(2,1)S(1)} %copy.114), channel_id=1, replica_groups=mesh['req'=8,'mlp'=4] {'mlp'}, dimensions={1} | all-to-all | bytes 1769472 | tf_op jit(solution)/shard_map/all_to_all | solution.py:151
  232.4 1.2 reshape.225
  233.6 76.2 %all-gather.6.cloned.1.call-done = bf16[1728,5120]{1,0:T(8,128)(2,1)} async-done(((bf16[432,5120]{1,0:T(8,128)(2,1)}), bf16[1728,5120]{1,0:T(8,128)(2,1)}) %all-gather.6.cloned.1.call-update) | async-done | bytes 17694736 | tf_op jit(solution)/shard_map/all_gather | solution.py:155
  309.8 12.2 %convolution_convert_fusion = bf16[256,5120]{1,0:T(8,128)(2,1)} fusion(bf16[256,1728]{1,0:T(8,128)(2,1)S(1)} %reshape.225, bf16[1728,5120]{1,0:T(8,128)(2,1)} %all-gather.6.cloned.1.call-done), kind=kOutput, calls=%fused_computation.6 | convolution fusion | flops 4531159040 | bytes 21200896 | tf_op jit(solution)/shard_map/dot_general | solution.py:153
  322.4 70.3 %reduce-scatter.5.cloned.1.call-done = bf16[32,5120]{1,0:T(8,128)(2,1)} async-done(((bf16[256,5120]{1,0:T(8,128)(2,1)}), bf16[32,5120]{1,0:T(8,128)(2,1)}) %reduce-scatter.5.cloned.1.call-update) | async-done | bytes 327696 | tf_op jit(solution)/shard_map/reduce_scatter | solution.py:158
  392.7 1.2 fusion.21
  394.8 17.3 %all-gather.8.cloned.1.call-done = bf16[128,5120]{1,0:T(8,128)(2,1)} async-done(((bf16[32,5120]{1,0:T(8,128)(2,1)}), bf16[128,5120]{1,0:T(8,128)(2,1)}) %all-gather.8.cloned.1.call-update) | async-done | bytes 1310736 | tf_op jit(solution)/shard_map/all_gather | solution.py:163
  412.1 10.1 %fusion.7 = bf16[128,1792]{1,0:T(8,128)(2,1)} fusion(bf16[128,5120]{1,0:T(8,128)(2,1)} %all-gather.8.cloned.1.call-done, bf16[5120,1792]{1,0:T(8,128)(2,1)} %param.36, f32[1792]{0:T(1024)S(1)} %copy-done.8), kind=kOutput, calls=%fused_computation.15 | convolution fusion | flops 2349268992 | bytes 20126720 | tf_op jit(solution)/shard_map/dot_general | solution.py:165
  (82 shorter events, 12.5 us)
Async XLA Ops:
  7.2 3.2 copy-start
  14.2 33.0 %all-to-all-start = ((bf16[8,2,64,2,256]{4,2,3,1,0:T(8,128)(2,1)}), bf16[8,2,64,2,256]{4,2,3,1,0:T(8,128)(2,1)S(1)}, u32[]{:S(2)}, u32[]{:S(2)}) async-start(bf16[8,2,64,2,256]{4,2,3,1,0:T(8,128)(2,1)} %copy.102), calls=%async_computation | async-start | bytes 2097152 | tf_op jit(solution)/shard_map/all_to_all | solution.py:90
  21.5 72.9 %reduce-scatter.3.cloned.1.call-start = ((), (), s32[]{:S(2)}) async-start(), calls=%async_computation.4 | async-start | bytes 1638400 | tf_op jit(solution)/shard_map/reduce_scatter | solution.py:140
  21.9 7.8 %copy-start.10 = (s32[1,6]{1,0:T(1,128)S(1)}, s32[1,6]{1,0:T(1,128)}, u32[]{:S(2)}) copy-start(s32[1,6]{1,0:T(1,128)} %param.28) | copy-start | bytes 76
  21.9 7.9 %copy-start.3 = (bf16[128,1280]{1,0:T(8,128)(2,1)S(1)}, bf16[128,1280]{1,0:T(8,128)(2,1)}, u32[]{:S(2)}) copy-start(bf16[128,1280]{1,0:T(8,128)(2,1)} %param.19) | copy-start | bytes 983044
  27.9 2.1 copy-start.4
  27.9 2.4 copy-start.5
  27.9 2.6 copy-start.9
  27.9 2.6 copy-start.12
  27.9 2.7 copy-start.13
  60.9 34.8 %copy-start.6 = (f32[5120]{0:T(1024)S(1)}, f32[5120]{0:T(1024)}, u32[]{:S(2)}) copy-start(f32[5120]{0:T(1024)} %param.31) | copy-start | bytes 61444
  68.6 116.3 %all-gather.4.cloned.1.call-start = ((), (), s32[]{:S(2)}) async-start(), calls=%async_computation.5 | async-start | bytes 10813440 | tf_op jit(solution)/shard_map/all_gather | solution.py:146
  96.5 213.3 %all-gather.6.cloned.1.call-start = ((), (), s32[]{:S(2)}) async-start(), calls=%async_computation.6 | async-start | bytes 22118400 | tf_op jit(solution)/shard_map/all_gather | solution.py:155
  97.3 295.4 %reduce-scatter.5.cloned.1.call-start = ((), (), s32[]{:S(2)}) async-start(), calls=%async_computation.7 | async-start | bytes 2949120 | tf_op jit(solution)/shard_map/reduce_scatter | solution.py:158
  184.9 9.6 %copy-start.11 = (bf16[1024,5120]{1,0:T(8,128)(2,1)S(1)}, bf16[1024,5120]{1,0:T(8,128)(2,1)}, u32[]{:S(2)}) copy-start(bf16[1024,5120]{1,0:T(8,128)(2,1)} %all-gather.4.cloned.1.call-done) | copy-start | bytes 31457284
  322.0 71.9 %copy-start.7 = (f32[5120]{0:T(1024)S(1)}, f32[5120]{0:T(1024)}, u32[]{:S(2)}) copy-start(f32[5120]{0:T(1024)} %param.35) | copy-start | bytes 61444
  322.0 90.0 %copy-start.8 = (f32[1792]{0:T(1024)S(1)}, f32[1792]{0:T(1024)}, u32[]{:S(2)}) copy-start(f32[1792]{0:T(1024)} %param.37) | copy-start | bytes 21508
  322.1 90.0 %all-gather.8.cloned.1.call-start = ((), (), s32[]{:S(2)}) async-start(), calls=%async_computation.8 | async-start | bytes 1638400 | tf_op jit(solution)/shard_map/all_gather | solution.py:163
  393.9 28.3 %copy-start.2 = (bf16[32,5120]{1,0:T(8,128)(2,1)}, bf16[32,5120]{1,0:T(8,128)(2,1)S(1)}, u32[]{:S(2)}) copy-start(bf16[32,5120]{1,0:T(8,128)(2,1)S(1)} %get-tuple-element.3) | copy-start | bytes 983044
  412.1 10.1 %copy-start.1 = (bf16[32,64,2,256]{3,2,1,0:T(2,128)(2,1)S(1)}, bf16[32,64,2,256]{3,2,1,0:T(2,128)(2,1)}, u32[]{:S(2)}) copy-start(bf16[32,64,2,256]{3,2,1,0:T(2,128)(2,1)} %param.22) | copy-start | bytes 6291460
Sparse Core Ops, SparseCore 0:
  68.7 25.5 reduce-scatter.2
  98.1 86.7 all-gather.3
  186.6 123.2 all-gather.5
  322.2 70.4 reduce-scatter.4
  394.9 17.1 all-gather.7
where the time goes:
time: 429 us
  waiting for transfers between devices  293 us (68%)
  matrix products  55.5 us (13%)
  blocking collectives  28.4 us (7%)
  local copies, waits for them, and re-layouts  22 us (5%)
  between operations  14.1 us (3%)
  starting transfers between devices  8.14 us (2%)
  other arithmetic  7.49 us (2%)
    all_gather x1, waiting for transfers between devices, body(): piece = lax.all_gather(normed, ('req', 'mlp'), axis=0, tiled=True)  87.4 us
    all_gather x1, waiting for transfers between devices, body(): lax.all_gather(down_proj, 'mlp', axis=0, tiled=True)  76.2 us
    reduce_scatter x1, waiting for transfers between devices, body(): lax.psum_scatter(mixed_all.astype(jnp.bfloat16), 'req', scatter_dimension...  70.3 us
    all_to_all x1, blocking collectives, body(): lax.all_to_all(blocks, 'mlp', split_axis=1, concat_axis=3, tiled=True)  28.4 us
    reduce_scatter x1, waiting for transfers between devices, body(): lax.psum_scatter(projected.astype(jnp.bfloat16), 'mlp', scatter_dimension...  25.6 us
    all_gather x1, waiting for transfers between devices, body(): next_normed = lax.all_gather(next_rows, 'mlp', axis=0, tiled=True)  17.3 us
    all_to_all x1, waiting for transfers between devices, fetch_prefix(): lax.all_to_all(outgoing, 'req', split_axis=0, concat_axis=0, tiled=True)  15.3 us
    dot_general x1, matrix products, body(): jnp.dot(hidden, lax.all_gather(down_proj, 'mlp', axis=0, tiled=True), pre...  12.2 us
  transfers between devices with their start and end apart: 6, of which 6 were waited for; matrix products, arithmetic and copies ran while one was open for 7% of the time, Pallas kernels for 0%

commit v1 on v0

--- a/solution.py
+++ b/solution.py
@@ -12,6 +12,8 @@
 MID_DEV = 4
 NODES_DEV = 6
 NODE_MAX = 256
+OUTER = 4
+CHUNKS = 2
 
 
 EPS = 1e-06
@@ -23,8 +25,14 @@
     return (values * lax.rsqrt(mean_sq + EPS) * gain).astype(jnp.bfloat16)
 
 
+def swap(array, axis, step):
+    return lax.ppermute(array, axis, [(i, i ^ step) for i in range(lax.axis_size(axis))])
+
+
 def attend(
     queries,
+    places,
+    query_segments,
     leaf_keys,
     leaf_token_values,
     prefix_keys,
@@ -35,31 +43,35 @@
     lengths,
 ):
     tokens = queries.shape[0]
+    leaf_tokens = leaf_keys.shape[0]
     heads_kv = leaf_keys.shape[1] // HEAD_SIZE
     query_rows = queries.reshape(tokens, heads_kv, QUERY_PER_KV, HEAD_SIZE)
     keys = jnp.concatenate(
         [
             prefix_keys.reshape(-1, heads_kv, HEAD_SIZE),
-            leaf_keys.reshape(tokens, heads_kv, HEAD_SIZE),
+            leaf_keys.reshape(leaf_tokens, heads_kv, HEAD_SIZE),
         ],
         0,
     )
     values = jnp.concatenate(
         [
             prefix_values.reshape(-1, heads_kv, HEAD_SIZE),
-            leaf_token_values.reshape(tokens, heads_kv, HEAD_SIZE),
+            leaf_token_values.reshape(leaf_tokens, heads_kv, HEAD_SIZE),
         ],
         0,
     )
-    middle = jnp.sum((segments[:, None] == jnp.arange(REQ_DEV)[None, :]) * parents[None, :], axis=1)
+    middle = jnp.sum(
+        (query_segments[:, None] == jnp.arange(REQ_DEV)[None, :]) * parents[None, :], axis=1
+    )
     root = jnp.sum((middle[:, None] == jnp.arange(MID_DEV)[None, :]) * roots[None, :], axis=1)
     node = jnp.arange(NODES_DEV * NODE_MAX) // NODE_MAX
     inside = (jnp.arange(NODE_MAX)[None, :] < lengths[:, None]).reshape(-1)
     prefix_mask = (
         (node[None, :] == root[:, None]) | (node[None, :] == ROOT_DEV + middle[:, None])
     ) & inside[None, :]
-    place = jnp.arange(tokens)
-    leaf_mask = (segments[None, :] == segments[:, None]) & (place[None, :] <= place[:, None])
+    leaf_mask = (segments[None, :] == query_segments[:, None]) & (
+        jnp.arange(leaf_tokens)[None, :] <= places[:, None]
+    )
     mask = jnp.concatenate([prefix_mask, leaf_mask], 1)
     score = jnp.einsum(
         "tkgd,skd->tkgs", query_rows, keys, preferred_element_type=jnp.float32
@@ -98,6 +110,86 @@
     return pages.reshape(NODES_DEV * NODE_MAX, 2, -1)
 
 
+def gather_tokens(rows):
+    inner = lax.axis_size("req") // OUTER
+    across = lax.axis_size("mlp") // 2
+    column = jnp.concatenate(
+        [rows] + [swap(rows, "req", k * inner) for k in range(1, OUTER)], 0
+    )
+    half = column.shape[0] // 2
+    by_x = {k: swap(column, "mlp", 2 * k) for k in range(1, across)}
+    by_y = {l: swap(column, "req", l) for l in range(1, inner)}
+    blocks = [column] + list(by_x.values()) + list(by_y.values())
+    for k in range(1, across):
+        for l in range(1, inner):
+            blocks.append(swap(by_y[l][:half], "mlp", 2 * k))
+            blocks.append(swap(by_x[k][half:], "req", l))
+    return jnp.concatenate(blocks, 0)
+
+
+def scatter_sum(partial, rows):
+    inner = lax.axis_size("req") // OUTER
+    across = lax.axis_size("mlp") // 2
+    size = OUTER * rows
+    half = size // 2
+    blocks = [partial[i * size : (i + 1) * size] for i in range(across * inner)]
+    wide = jnp.float32
+    column = blocks[0].astype(wide)
+    by_x = {k: blocks[k].astype(wide) for k in range(1, across)}
+    by_y = {l: blocks[across - 1 + l].astype(wide) for l in range(1, inner)}
+    at = across + inner - 1
+    for k in range(1, across):
+        for l in range(1, inner):
+            first = swap(blocks[at][:half], "mlp", 2 * k).astype(wide)
+            second = swap(blocks[at][half:], "req", l).astype(wide)
+            by_y[l] = jnp.concatenate([by_y[l][:half] + first, by_y[l][half:]], 0)
+            by_x[k] = jnp.concatenate([by_x[k][:half], by_x[k][half:] + second], 0)
+            at += 1
+    for k in range(1, across):
+        column = column + swap(by_x[k].astype(jnp.bfloat16), "mlp", 2 * k).astype(wide)
+    for l in range(1, inner):
+        column = column + swap(by_y[l].astype(jnp.bfloat16), "req", l).astype(wide)
+    total = column[:rows]
+    for k in range(1, OUTER):
+        part = column[k * rows : (k + 1) * rows].astype(jnp.bfloat16)
+        total = total + swap(part, "req", k * inner).astype(wide)
+    return total
+
+
+def sum_heads(projected, rows):
+    members = lax.axis_size("mlp")
+    wide = jnp.float32
+    blocks = [projected[j * rows : (j + 1) * rows] for j in range(members)]
+    odd = jnp.concatenate(blocks[1::2], 0).astype(jnp.bfloat16)
+    even = jnp.concatenate(blocks[0::2], 0) + swap(odd, "mlp", 1).astype(wide)
+    total = even[:rows]
+    for k in range(1, members // 2):
+        part = even[k * rows : (k + 1) * rows].astype(jnp.bfloat16)
+        total = total + swap(part, "mlp", 2 * k).astype(wide)
+    return total
+
+
+def gather_heads(rows):
+    members = lax.axis_size("mlp")
+    place = lax.axis_index("mlp")
+    blocks = [rows] + [swap(rows, "mlp", 2 * k) for k in range(1, members // 2)]
+    near = jnp.concatenate(blocks, 0)
+    far = swap(near, "mlp", 1)
+    size = rows.shape[0]
+    near = near.reshape(members // 2, size, -1)
+    far = far.reshape(members // 2, size, -1)
+    core = place % 2
+    low = jnp.where(core == 0, near, far)
+    high = jnp.where(core == 0, far, near)
+    pairs = jnp.stack([low, high], 1)
+    for bit in range((members // 2).bit_length() - 1):
+        shaped = pairs.reshape((-1, 2, 1 << bit) + pairs.shape[1:])
+        swapped = shaped[:, ::-1]
+        shaped = jnp.where(((place // 2) >> bit) % 2 == 0, shaped, swapped)
+        pairs = shaped.reshape(pairs.shape)
+    return pairs.reshape(members, size, -1)
+
+
 def body(
     queries,
     leaf_keys,
@@ -119,48 +211,64 @@
     qkv_proj,
     qkv_bias,
 ):
+    group_tokens = queries.shape[0]
+    members = lax.axis_size("mlp")
+    place = lax.axis_index("mlp")
+    owned = group_tokens // members
+    rows = owned // CHUNKS
+    gates = [gate_proj, swap(gate_proj, "mlp", 1)]
+    uppers = [up_proj, swap(up_proj, "mlp", 1)]
+    downs = [down_proj, swap(down_proj, "mlp", 1)]
     prefix = fetch_prefix(key_value_pages, page_holder, page_slot)
-    attention = attend(
-        queries,
-        leaf_keys,
-        leaf_token_values,
-        prefix[:, 0],
-        prefix[:, 1],
-        segment_ids,
-        req_parent[0],
-        mid_parent[0],
-        node_len[0],
-    )
-    projected = jnp.dot(attention, out_proj, preferred_element_type=jnp.float32)
-    group_tokens = queries.shape[0]
-    groups = lax.axis_size("req")
-    members = lax.axis_size("mlp")
-    rows_mlp = group_tokens // members
-    first_row = lax.axis_index("mlp") * rows_mlp
-    head_part = lax.psum_scatter(
-        projected.astype(jnp.bfloat16), "mlp", scatter_dimension=0, tiled=True
-    ).astype(jnp.float32)
-    own_resid = lax.dynamic_slice_in_dim(residual, first_row, rows_mlp, 0)
-    stream = (own_resid.astype(jnp.float32) + head_part).astype(jnp.bfloat16)
-    normed = rms_norm(stream, norm_gain)
-    piece = lax.all_gather(normed, ("req", "mlp"), axis=0, tiled=True)
-    gate = jnp.dot(piece, gate_proj, preferred_element_type=jnp.float32)
-    upper = jnp.dot(piece, up_proj, preferred_element_type=jnp.float32)
-    hidden_all = (jax.nn.silu(gate) * upper).astype(jnp.bfloat16)
-    blocks = hidden_all.reshape(groups, members, rows_mlp, -1)
-    regrouped = lax.all_to_all(blocks, "mlp", split_axis=1, concat_axis=3, tiled=True)
-    hidden = regrouped.reshape(groups * rows_mlp, -1)
-    mixed_all = jnp.dot(
-        hidden,
-        lax.all_gather(down_proj, "mlp", axis=0, tiled=True),
-        preferred_element_type=jnp.float32,
-    )
-    mixed = lax.psum_scatter(
-        mixed_all.astype(jnp.bfloat16), "req", scatter_dimension=0, tiled=True
-    ).astype(jnp.float32)
-    layer_out = (stream.astype(jnp.float32) + mixed).astype(jnp.bfloat16)
-    next_rows = rms_norm(layer_out, next_gain)
-    next_normed = lax.all_gather(next_rows, "mlp", axis=0, tiled=True)
+
+    def attention_of(chunk):
+        starts = [(place ^ j) * owned + chunk * rows for j in range(members)]
+
+        def picked(array):
+            return jnp.concatenate(
+                [lax.dynamic_slice_in_dim(array, s, rows, 0) for s in starts], 0
+            )
+
+        places = jnp.concatenate([s + jnp.arange(rows) for s in starts], 0)
+        attention = attend(
+            picked(queries),
+            places,
+            picked(segment_ids),
+            leaf_keys,
+            leaf_token_values,
+            prefix[:, 0],
+            prefix[:, 1],
+            segment_ids,
+            req_parent[0],
+            mid_parent[0],
+            node_len[0],
+        )
+        return jnp.dot(attention, out_proj, preferred_element_type=jnp.float32)
+
+    def stream_of(chunk, projected):
+        own = lax.dynamic_slice_in_dim(residual, place * owned + chunk * rows, rows, 0)
+        return (own.astype(jnp.float32) + sum_heads(projected, rows)).astype(jnp.bfloat16)
+
+    def mixed_of(tokens):
+        total = None
+        for gate_w, up_w, down_w in zip(gates, uppers, downs):
+            gate = jnp.dot(tokens, gate_w, preferred_element_type=jnp.float32)
+            upper = jnp.dot(tokens, up_w, preferred_element_type=jnp.float32)
+            hidden = (jax.nn.silu(gate) * upper).astype(jnp.bfloat16)
+            part = jnp.dot(hidden, down_w, preferred_element_type=jnp.float32)
+            total = part if total is None else total + part
+        return total.astype(jnp.bfloat16)
+
+    layer_rows, next_rows = [], []
+    for chunk in range(CHUNKS):
+        stream = stream_of(chunk, attention_of(chunk))
+        tokens = gather_tokens(rms_norm(stream, norm_gain))
+        mixed = scatter_sum(mixed_of(tokens), rows)
+        layer = (stream.astype(jnp.float32) + mixed).astype(jnp.bfloat16)
+        layer_rows.append(layer)
+        next_rows.append(gather_heads(rms_norm(layer, next_gain)))
+    layer_out = jnp.concatenate(layer_rows, 0)
+    next_normed = jnp.concatenate(next_rows, 1).reshape(group_tokens, -1)
     qkv_out = (
         jnp.dot(next_normed, qkv_proj, preferred_element_type=jnp.float32) + qkv_bias
     ).astype(jnp.bfloat16)

time: 429 us -> 309 us (0.72); the launches traced: 429 us -> 303 us
  waiting for transfers between devices: 293 us -> 110 us
  starting transfers between devices: 8.14 us -> 49.7 us
  matrix products: 55.5 us -> 95.1 us
  blocking collectives: 28.4 us -> 0 us
  local copies, waits for them, and re-layouts: 22 us -> 34.3 us
  between operations: 14.1 us -> 2.22 us
    all_gather x3 -> x0, waiting for transfers between devices: 181 us -> none  [the longest x1 87.4 us: body(): piece = lax.all_gather(normed, ('req', 'mlp'), axis=0, tiled=True)]
    ppermute x0 -> x39, waiting for transfers between devices: none -> 103 us  [swap(): lax.ppermute(array, axis, [(i, i ^ step) for i in range(lax.axis_size(axi...]
    reduce_scatter x2 -> x0, waiting for transfers between devices: 96 us -> none  [the longest x1 70.3 us: body(): lax.psum_scatter(mixed_all.astype(jnp.bfloat16), 'req', scatter_dimension...]
    ppermute x0 -> x39, starting transfers between devices: none -> 42.4 us  [swap(): lax.ppermute(array, axis, [(i, i ^ step) for i in range(lax.axis_size(axi...]
    dot_general x4 -> x10, matrix products: 36.8 us -> 74.1 us  [the longest x4 49.1 us: mixed_of(): part = jnp.dot(hidden, down_w, preferred_element_type=jnp.float32)]
    all_to_all x1 -> x0, blocking collectives: 28.4 us -> none  [body(): lax.all_to_all(blocks, 'mlp', split_axis=1, concat_axis=3, tiled=True)]
    all_to_all x1, waiting for transfers between devices: 15.3 us -> 7.35 us  [fetch_prefix(): lax.all_to_all(outgoing, 'req', split_axis=0, concat_axis=0, tiled=True)]
    unnamed x31 -> x78, local copies, waits for them, and re-layouts: 1.14 us -> 7.07 us
  transfers between devices with their start and end apart: 6 -> 40, of which waited for: 6 -> 21; matrix products, arithmetic and copies ran while one was open for 7% -> 26% of each run, Pallas kernels for 0% -> 0%
where the time goes in v1:
time: 309 us; the launch traced here: 303 us
  waiting for transfers between devices  110 us (36%)
  matrix products  95.1 us (31%)
  starting transfers between devices  49.7 us (16%)
  local copies, waits for them, and re-layouts  34.3 us (11%)
  other arithmetic  11.5 us (4%)
    ppermute x39, waiting for transfers between devices, swap(): lax.ppermute(array, axis, [(i, i ^ step) for i in range(lax.axis_size(axi...  103 us
    dot_general x4, matrix products, mixed_of(): part = jnp.dot(hidden, down_w, preferred_element_type=jnp.float32)  49.1 us
    ppermute x39, starting transfers between devices, swap(): lax.ppermute(array, axis, [(i, i ^ step) for i in range(lax.axis_size(axi...  42.4 us
    dot_general x4, matrix products, mixed_of(): gate = jnp.dot(tokens, gate_w, preferred_element_type=jnp.float32)  15.2 us
    dot_general x2, matrix products, attention_of(): return jnp.dot(attention, out_proj, preferred_element_type=jnp.float32)  9.81 us
    dot_general x1, matrix products, body(): jnp.dot(next_normed, qkv_proj, preferred_element_type=jnp.float32)  9.71 us
    gather x2, local copies, waits for them, and re-layouts, fetch_prefix(): local = key_value_pages[own_slots]  8.37 us
    all_to_all x1, waiting for transfers between devices, fetch_prefix(): lax.all_to_all(outgoing, 'req', split_axis=0, concat_axis=0, tiled=True)  7.35 us
  transfers between devices with their start and end apart: 40, of which 21 were waited for; matrix products, arithmetic and copies ran while one was open for 26% of the time, Pallas kernels for 0%

profile of v1, /device:TPU:0, one launch (start us, length us, event | category | flops | bytes accessed | tf_op | source)
XLA Modules:
  0.0 303.1 jit_solution(1895355729357623365)
XLA Ops:
  8.3 7.3 %all-to-all-start = ((bf16[8,2,64,2,256]{4,2,3,1,0:T(8,128)(2,1)}), bf16[8,2,64,2,256]{4,2,3,1,0:T(8,128)(2,1)S(1)}, u32[]{:S(2)}, u32[]{:S(2)}) async-start(bf16[8,2,64,2,256]{4,2,3,1,0:T(8,128)(2,1)} %copy.132), calls=%async_computation | async-start | bytes 2097152 | tf_op jit(solution)/shard_map/all_to_all | solution.py:102
  25.0 6.7 %gather_fusion = bf16[24,64,2,256]{3,2,1,0:T(2,128)(2,1)} fusion(bf16[32,64,2,256]{3,2,1,0:T(2,128)(2,1)S(1)} %copy-done, s32[1024]{0:T(1024)} %get-tuple-element.95), kind=kCustom, calls=%fused_computation | custom fusion | bytes 3145824 | tf_op jit(solution)/shard_map/gather | solution.py:108
  34.0 7.3 %all-to-all-done = bf16[8,2,64,2,256]{4,2,3,1,0:T(8,128)(2,1)S(1)} async-done(((bf16[8,2,64,2,256]{4,2,3,1,0:T(8,128)(2,1)}), bf16[8,2,64,2,256]{4,2,3,1,0:T(8,128)(2,1)S(1)}, u32[]{:S(2)}, u32[]{:S(2)}) %all-to-all-start) | async-done | bytes 1048608 | tf_op jit(solution)/shard_map/all_to_all | solution.py:102
  58.9 7.3 %fusion.125 = (bf16[64,5120]{1,0:T(8,128)(2,1)S(1)}, f32[64,5120]{1,0:T(8,128)S(1)}) fusion(bf16[64,1280]{1,0:T(8,128)(2,1)S(1)} %reshape.345, bf16[1280,5120]{1,0:T(8,128)(2,1)} %param.30), kind=kOutput, calls=%fused_computation.235 | convolution fusion | flops 839188480 | bytes 15237120 | tf_op jit(solution)/shard_map/dot_general | solution.py:246
  73.3 4.0 %collective-permute-done.20 = bf16[16,5120]{1,0:T(8,128)(2,1)S(1)} collective-permute-done((bf16[16,5120]{1,0:T(8,128)(2,1)S(1)}, bf16[16,5120]{1,0:T(8,128)(2,1)S(1)}, u32[]{:S(2)}, u32[]{:S(2)}) %collective-permute-start.20) | collective-permute-done | bytes 163872 | tf_op jit(solution)/shard_map/ppermute | solution.py:29
  87.4 4.1 %collective-permute-done.23 = bf16[16,5120]{1,0:T(8,128)(2,1)S(1)} collective-permute-done((bf16[16,5120]{1,0:T(8,128)(2,1)S(1)}, bf16[16,5120]{1,0:T(8,128)(2,1)S(1)}, u32[]{:S(2)}, u32[]{:S(2)}) %collective-permute-start.23) | collective-permute-done | bytes 163872 | tf_op jit(solution)/shard_map/ppermute | solution.py:29
  92.6 11.4 %collective-permute-done.22 = bf16[16,5120]{1,0:T(8,128)(2,1)S(1)} collective-permute-done((bf16[16,5120]{1,0:T(8,128)(2,1)S(1)}, bf16[16,5120]{1,0:T(8,128)(2,1)S(1)}, u32[]{:S(2)}, u32[]{:S(2)}) %collective-permute-start.22) | collective-permute-done | bytes 163872 | tf_op jit(solution)/shard_map/ppermute | solution.py:29
  108.7 3.4 %collective-permute-done.3 = bf16[16,5120]{1,0:T(8,128)(2,1)S(1)} collective-permute-done((bf16[16,5120]{1,0:T(8,128)(2,1)S(1)}, bf16[16,5120]{1,0:T(8,128)(2,1)S(1)}, u32[]{:S(2)}, u32[]{:S(2)}) %collective-permute-start.3) | collective-permute-done | bytes 163872 | tf_op jit(solution)/shard_map/ppermute | solution.py:29
  116.4 11.6 %collective-permute-done.24 = bf16[64,5120]{1,0:T(8,128)(2,1)S(1)} collective-permute-done((bf16[64,5120]{1,0:T(8,128)(2,1)S(1)}, bf16[64,5120]{1,0:T(8,128)(2,1)S(1)}, u32[]{:S(2)}, u32[]{:S(2)}) %collective-permute-start.24) | collective-permute-done | bytes 655392 | tf_op jit(solution)/shard_map/ppermute | solution.py:29
  132.9 12.8 %collective-permute-done.5 = bf16[64,5120]{1,0:T(8,128)(2,1)S(1)} collective-permute-done((bf16[64,5120]{1,0:T(8,128)(2,1)S(1)}, bf16[64,5120]{1,0:T(8,128)(2,1)S(1)}, u32[]{:S(2)}, u32[]{:S(2)}) %collective-permute-start.5) | collective-permute-done | bytes 655392 | tf_op jit(solution)/shard_map/ppermute | solution.py:29
  157.1 3.6 %fusion.136 = f32[256,432]{0,1:T(8,128)S(1)} fusion(bf16[256,5120]{1,0:T(8,128)(2,1)S(1)} %constant_dynamic-update-slice_fusion.8, bf16[5120,432]{0,1:T(8,128)(2,1)} %param.32), kind=kOutput, calls=%fused_computation.242 | convolution fusion | flops 1132462080 | bytes 7487488 | tf_op jit(solution)/shard_map/dot_general | solution.py:255
  162.3 3.6 %fusion.134 = f32[256,432]{0,1:T(8,128)S(1)} fusion(bf16[256,5120]{1,0:T(8,128)(2,1)S(1)} %constant_dynamic-update-slice_fusion, bf16[5120,432]{0,1:T(8,128)(2,1)} %param.32), kind=kOutput, calls=%fused_computation.240 | convolution fusion | flops 1132462080 | bytes 7487488 | tf_op jit(solution)/shard_map/dot_general | solution.py:255
  165.9 11.9 %fusion.61 = f32[256,5120]{1,0:T(8,128)} fusion(bf16[432,5120]{1,0:T(8,128)(2,1)} %param.34, f32[256,432]{0,1:T(8,128)S(1)} %fusion.134, bf16[256,5120]{1,0:T(8,128)(2,1)} %copy-done.6, bf16[5120,432]{0,1:T(8,128)(2,1)} %param.33), kind=kOutput, calls=%fused_computation.112 | convolution fusion | flops 2265587712 | bytes 17154048 | tf_op jit(solution)/shard_map/dot_general | solution.py:258
  177.7 12.0 %fusion.62 = f32[256,5120]{1,0:T(8,128)} fusion(bf16[432,5120]{1,0:T(8,128)(2,1)} %param.34, f32[256,432]{0,1:T(8,128)S(1)} %fusion.136, bf16[256,5120]{1,0:T(8,128)(2,1)} %copy-done.3, bf16[5120,432]{0,1:T(8,128)(2,1)} %param.33), kind=kOutput, calls=%fused_computation.113 | convolution fusion | flops 2265587712 | bytes 17154048 | tf_op jit(solution)/shard_map/dot_general | solution.py:258
  189.8 4.4 %fusion.135 = f32[256,432]{0,1:T(8,128)S(1)} fusion(bf16[256,5120]{1,0:T(8,128)(2,1)} %copy-done.6, bf16[5120,432]{0,1:T(8,128)(2,1)} %collective-permute-done.9), kind=kOutput, calls=%fused_computation.241 | convolution fusion | flops 1132462080 | bytes 7487488 | tf_op jit(solution)/shard_map/dot_general | solution.py:255
  194.2 12.5 %fusion.2 = bf16[256,5120]{1,0:T(8,128)(2,1)} fusion(f32[256,5120]{1,0:T(8,128)} %fusion.61, bf16[432,5120]{1,0:T(8,128)(2,1)} %collective-permute-done.11, f32[256,432]{0,1:T(8,128)S(1)} %fusion.135, bf16[256,5120]{1,0:T(8,128)(2,1)} %copy-done.6, bf16[5120,432]{0,1:T(8,128)(2,1)} %collective-permute-done.10), kind=kOutput, calls=%fused_computation.7 | convolution fusion | flops 2268209152 | bytes 19775488 | tf_op jit(solution)/shard_map/dot_general | solution.py:258
  212.6 3.6 %fusion.137 = f32[256,432]{0,1:T(8,128)S(1)} fusion(bf16[256,5120]{1,0:T(8,128)(2,1)S(1)} %copy-done.4, bf16[5120,432]{0,1:T(8,128)(2,1)} %collective-permute-done.9), kind=kOutput, calls=%fused_computation.243 | convolution fusion | flops 1132462080 | bytes 7487488 | tf_op jit(solution)/shard_map/dot_general | solution.py:255
  216.2 12.7 %fusion.3 = bf16[256,5120]{1,0:T(8,128)(2,1)} fusion(f32[256,5120]{1,0:T(8,128)} %fusion.62, bf16[432,5120]{1,0:T(8,128)(2,1)} %collective-permute-done.11, f32[256,432]{0,1:T(8,128)S(1)} %fusion.137, bf16[256,5120]{1,0:T(8,128)(2,1)} %copy-done.3, bf16[5120,432]{0,1:T(8,128)(2,1)} %collective-permute-done.10), kind=kOutput, calls=%fused_computation.8 | convolution fusion | flops 2268209152 | bytes 19775488 | tf_op jit(solution)/shard_map/dot_general | solution.py:258
  235.0 6.2 %collective-permute-done.30 = bf16[32,5120]{1,0:T(8,128)(2,1)S(1)} collective-permute-done((bf16[32,5120]{1,0:T(8,128)(2,1)S(1)}, bf16[32,5120]{1,0:T(8,128)(2,1)S(1)}, u32[]{:S(2)}, u32[]{:S(2)}) %collective-permute-start.30) | collective-permute-done | bytes 327712 | tf_op jit(solution)/shard_map/ppermute | solution.py:29
  243.6 12.1 %collective-permute-done.15 = bf16[64,5120]{1,0:T(8,128)(2,1)S(1)} collective-permute-done((bf16[64,5120]{1,0:T(8,128)(2,1)S(1)}, bf16[64,5120]{1,0:T(8,128)(2,1)S(1)}, u32[]{:S(2)}, u32[]{:S(2)}) %collective-permute-start.15) | collective-permute-done | bytes 655392 | tf_op jit(solution)/shard_map/ppermute | solution.py:29
  259.6 5.6 %collective-permute-done.31 = bf16[64,5120]{1,0:T(8,128)(2,1)S(1)} collective-permute-done((bf16[64,5120]{1,0:T(8,128)(2,1)S(1)}, bf16[64,5120]{1,0:T(8,128)(2,1)S(1)}, u32[]{:S(2)}, u32[]{:S(2)}) %collective-permute-start.31) | collective-permute-done | bytes 655392 | tf_op jit(solution)/shard_map/ppermute | solution.py:29
  269.0 8.0 %collective-permute-done.17 = bf16[16,5120]{1,0:T(8,128)(2,1)S(1)} collective-permute-done((bf16[16,5120]{1,0:T(8,128)(2,1)S(1)}, bf16[16,5120]{1,0:T(8,128)(2,1)S(1)}, u32[]{:S(2)}, u32[]{:S(2)}) %collective-permute-start.17) | collective-permute-done | bytes 163872 | tf_op jit(solution)/shard_map/ppermute | solution.py:29
  277.3 4.8 %collective-permute-done.33 = bf16[16,5120]{1,0:T(8,128)(2,1)S(1)} collective-permute-done((bf16[16,5120]{1,0:T(8,128)(2,1)S(1)}, bf16[16,5120]{1,0:T(8,128)(2,1)S(1)}, u32[]{:S(2)}, u32[]{:S(2)}) %collective-permute-start.33) | collective-permute-done | bytes 163872 | tf_op jit(solution)/shard_map/ppermute | solution.py:29
  292.9 9.7 %fusion.6 = bf16[128,1792]{1,0:T(8,128)(2,1)} fusion(bf16[128,5120]{1,0:T(8,128)(2,1)S(1)} %bitcast.122, bf16[5120,1792]{1,0:T(8,128)(2,1)} %param.36, f32[1792]{0:T(1024)S(1)} %copy-done.19), kind=kOutput, calls=%fused_computation.16 | convolution fusion | flops 2349268992 | bytes 20126720 | tf_op jit(solution)/shard_map/dot_general | solution.py:273
  (261 shorter events, 114.2 us)
Async XLA Ops:
  8.3 33.0 %all-to-all-start = ((bf16[8,2,64,2,256]{4,2,3,1,0:T(8,128)(2,1)}), bf16[8,2,64,2,256]{4,2,3,1,0:T(8,128)(2,1)S(1)}, u32[]{:S(2)}, u32[]{:S(2)}) async-start(bf16[8,2,64,2,256]{4,2,3,1,0:T(8,128)(2,1)} %copy.132), calls=%async_computation | async-start | bytes 2097152 | tf_op jit(solution)/shard_map/all_to_all | solution.py:102
  83.7 20.4 %collective-permute-start.22 = (bf16[16,5120]{1,0:T(8,128)(2,1)S(1)}, bf16[16,5120]{1,0:T(8,128)(2,1)S(1)}, u32[]{:S(2)}, u32[]{:S(2)}) collective-permute-start(bf16[16,5120]{1,0:T(8,128)(2,1)S(1)} %get-tuple-element.67), channel_id=1, source_target_pairs={{0,16},{4,20},{8,24},{12,28},{16,0},{20,4},{24,8},{28,12},{1,17},{... | collective-permute-start | bytes 491528 | tf_op jit(solution)/shard_map/ppermute | solution.py:29
  83.7 20.4 %collective-permute-start.21 = (bf16[16,5120]{1,0:T(8,128)(2,1)S(1)}, bf16[16,5120]{1,0:T(8,128)(2,1)S(1)}, u32[]{:S(2)}, u32[]{:S(2)}) collective-permute-start(bf16[16,5120]{1,0:T(8,128)(2,1)S(1)} %get-tuple-element.67), channel_id=1, source_target_pairs={{0,8},{4,12},{8,0},{12,4},{16,24},{20,28},{24,16},{28,20},{1,9},{5... | collective-permute-start | bytes 491528 | tf_op jit(solution)/shard_map/ppermute | solution.py:29
  86.9 102.8 %collective-permute-start.9 = (bf16[5120,432]{0,1:T(8,128)(2,1)}, bf16[5120,432]{0,1:T(8,128)(2,1)}, u32[]{:S(2)}, u32[]{:S(2)}) collective-permute-start(bf16[5120,432]{0,1:T(8,128)(2,1)} %param.32), channel_id=1, source_target_pairs={{0,1},{1,0},{2,3},{3,2},{4,5},{5,4},{6,7},{7,6},{8,9},{9,8},{10,11... | collective-permute-start | bytes 13271048 | tf_op jit(solution)/shard_map/ppermute | solution.py:29
  86.9 107.2 %collective-permute-start.10 = (bf16[5120,432]{0,1:T(8,128)(2,1)}, bf16[5120,432]{0,1:T(8,128)(2,1)}, u32[]{:S(2)}, u32[]{:S(2)}) collective-permute-start(bf16[5120,432]{0,1:T(8,128)(2,1)} %param.33), channel_id=1, source_target_pairs={{0,1},{1,0},{2,3},{3,2},{4,5},{5,4},{6,7},{7,6},{8,9},{9,8},{10,11... | collective-permute-start | bytes 13271048 | tf_op jit(solution)/shard_map/ppermute | solution.py:29
  91.5 14.7 %collective-permute-start.4 = (bf16[16,5120]{1,0:T(8,128)(2,1)S(1)}, bf16[16,5120]{1,0:T(8,128)(2,1)S(1)}, u32[]{:S(2)}, u32[]{:S(2)}) collective-permute-start(bf16[16,5120]{1,0:T(8,128)(2,1)S(1)} %get-tuple-element.13), channel_id=1, source_target_pairs={{0,24},{4,28},{8,16},{12,20},{16,8},{20,12},{24,0},{28,4},{1,25},{... | collective-permute-start | bytes 491528 | tf_op jit(solution)/shard_map/ppermute | solution.py:29
  106.3 23.4 %collective-permute-start.25 = (bf16[64,5120]{1,0:T(8,128)(2,1)S(1)}, bf16[64,5120]{1,0:T(8,128)(2,1)S(1)}, u32[]{:S(2)}, u32[]{:S(2)}) collective-permute-start(bf16[64,5120]{1,0:T(8,128)(2,1)S(1)} %pad_maximum_fusion.4), channel_id=1, source_target_pairs={{0,4},{4,0},{8,12},{12,8},{16,20},{20,16},{24,28},{28,24},{1,5},{5... | collective-permute-start | bytes 1966088 | tf_op jit(solution)/shard_map/ppermute | solution.py:29
  112.2 15.9 %collective-permute-start.24 = (bf16[64,5120]{1,0:T(8,128)(2,1)S(1)}, bf16[64,5120]{1,0:T(8,128)(2,1)S(1)}, u32[]{:S(2)}, u32[]{:S(2)}) collective-permute-start(bf16[64,5120]{1,0:T(8,128)(2,1)S(1)} %pad_maximum_fusion.4), channel_id=1, source_target_pairs={{0,2},{1,3},{2,0},{3,1},{4,6},{5,7},{6,4},{7,5},{8,10},{9,11},{10,... | collective-permute-start | bytes 1966088 | tf_op jit(solution)/shard_map/ppermute | solution.py:29
  113.7 17.7 %collective-permute-start.6 = (bf16[64,5120]{1,0:T(8,128)(2,1)S(1)}, bf16[64,5120]{1,0:T(8,128)(2,1)S(1)}, u32[]{:S(2)}, u32[]{:S(2)}) collective-permute-start(bf16[64,5120]{1,0:T(8,128)(2,1)S(1)} %pad_maximum_fusion.1), channel_id=1, source_target_pairs={{0,4},{4,0},{8,12},{12,8},{16,20},{20,16},{24,28},{28,24},{1,5},{5... | collective-permute-start | bytes 1966088 | tf_op jit(solution)/shard_map/ppermute | solution.py:29
  128.0 17.7 %collective-permute-start.5 = (bf16[64,5120]{1,0:T(8,128)(2,1)S(1)}, bf16[64,5120]{1,0:T(8,128)(2,1)S(1)}, u32[]{:S(2)}, u32[]{:S(2)}) collective-permute-start(bf16[64,5120]{1,0:T(8,128)(2,1)S(1)} %pad_maximum_fusion.1), channel_id=1, source_target_pairs={{0,2},{1,3},{2,0},{3,1},{4,6},{5,7},{6,4},{7,5},{8,10},{9,11},{10,... | collective-permute-start | bytes 1966088 | tf_op jit(solution)/shard_map/ppermute | solution.py:29
  129.6 64.5 %collective-permute-start.11 = (bf16[432,5120]{1,0:T(8,128)(2,1)}, bf16[432,5120]{1,0:T(8,128)(2,1)}, u32[]{:S(2)}, u32[]{:S(2)}) collective-permute-start(bf16[432,5120]{1,0:T(8,128)(2,1)} %param.34), channel_id=1, source_target_pairs={{0,1},{1,0},{2,3},{3,2},{4,5},{5,4},{6,7},{7,6},{8,9},{9,8},{10,11... | collective-permute-start | bytes 13271048 | tf_op jit(solution)/shard_map/ppermute | solution.py:29
  131.4 18.7 %collective-permute-start.26 = (bf16[32,5120]{1,0:T(8,128)(2,1)S(1)}, bf16[32,5120]{1,0:T(8,128)(2,1)S(1)}, u32[]{:S(2)}, u32[]{:S(2)}) collective-permute-start(bf16[32,5120]{1,0:T(8,128)(2,1)S(1)} %slice.245), channel_id=1, source_target_pairs={{0,2},{1,3},{2,0},{3,1},{4,6},{5,7},{6,4},{7,5},{8,10},{9,11},{10,... | collective-permute-start | bytes 983048 | tf_op jit(solution)/shard_map/ppermute | solution.py:29
  208.2 22.8 %collective-permute-start.14 = (bf16[32,5120]{1,0:T(8,128)(2,1)S(1)}, bf16[32,5120]{1,0:T(8,128)(2,1)S(1)}, u32[]{:S(2)}, u32[]{:S(2)}) collective-permute-start(bf16[32,5120]{1,0:T(8,128)(2,1)S(1)} %get-tuple-element.24), channel_id=1, source_target_pairs={{0,2},{1,3},{2,0},{3,1},{4,6},{5,7},{6,4},{7,5},{8,10},{9,11},{10,... | collective-permute-start | bytes 983048 | tf_op jit(solution)/shard_map/ppermute | solution.py:29
  210.1 21.0 %collective-permute-start.12 = (bf16[32,5120]{1,0:T(8,128)(2,1)S(1)}, bf16[32,5120]{1,0:T(8,128)(2,1)S(1)}, u32[]{:S(2)}, u32[]{:S(2)}) collective-permute-start(bf16[32,5120]{1,0:T(8,128)(2,1)S(1)} %get-tuple-element.25), channel_id=1, source_target_pairs={{0,4},{4,0},{8,12},{12,8},{16,20},{20,16},{24,28},{28,24},{1,5},{5... | collective-permute-start | bytes 983048 | tf_op jit(solution)/shard_map/ppermute | solution.py:29
  230.4 10.7 %collective-permute-start.30 = (bf16[32,5120]{1,0:T(8,128)(2,1)S(1)}, bf16[32,5120]{1,0:T(8,128)(2,1)S(1)}, u32[]{:S(2)}, u32[]{:S(2)}) collective-permute-start(bf16[32,5120]{1,0:T(8,128)(2,1)S(1)} %get-tuple-element.30), channel_id=1, source_target_pairs={{0,2},{1,3},{2,0},{3,1},{4,6},{5,7},{6,4},{7,5},{8,10},{9,11},{10,... | collective-permute-start | bytes 983048 | tf_op jit(solution)/shard_map/ppermute | solution.py:29
  231.3 24.4 %collective-permute-start.15 = (bf16[64,5120]{1,0:T(8,128)(2,1)S(1)}, bf16[64,5120]{1,0:T(8,128)(2,1)S(1)}, u32[]{:S(2)}, u32[]{:S(2)}) collective-permute-start(bf16[64,5120]{1,0:T(8,128)(2,1)S(1)} %pad_maximum_fusion.3), channel_id=1, source_target_pairs={{0,4},{4,0},{8,12},{12,8},{16,20},{20,16},{24,28},{28,24},{1,5},{5... | collective-permute-start | bytes 1966088 | tf_op jit(solution)/shard_map/ppermute | solution.py:29
  233.4 22.3 %collective-permute-start.13 = (bf16[64,5120]{1,0:T(8,128)(2,1)S(1)}, bf16[64,5120]{1,0:T(8,128)(2,1)S(1)}, u32[]{:S(2)}, u32[]{:S(2)}) collective-permute-start(bf16[64,5120]{1,0:T(8,128)(2,1)S(1)} %pad_maximum_fusion.2), channel_id=1, source_target_pairs={{0,2},{1,3},{2,0},{3,1},{4,6},{5,7},{6,4},{7,5},{8,10},{9,11},{10,... | collective-permute-start | bytes 1966088 | tf_op jit(solution)/shard_map/ppermute | solution.py:29
  241.9 23.3 %collective-permute-start.31 = (bf16[64,5120]{1,0:T(8,128)(2,1)S(1)}, bf16[64,5120]{1,0:T(8,128)(2,1)S(1)}, u32[]{:S(2)}, u32[]{:S(2)}) collective-permute-start(bf16[64,5120]{1,0:T(8,128)(2,1)S(1)} %pad_maximum_fusion.6), channel_id=1, source_target_pairs={{0,4},{4,0},{8,12},{12,8},{16,20},{20,16},{24,28},{28,24},{1,5},{5... | collective-permute-start | bytes 1966088 | tf_op jit(solution)/shard_map/ppermute | solution.py:29
  242.0 23.1 %collective-permute-start.29 = (bf16[64,5120]{1,0:T(8,128)(2,1)S(1)}, bf16[64,5120]{1,0:T(8,128)(2,1)S(1)}, u32[]{:S(2)}, u32[]{:S(2)}) collective-permute-start(bf16[64,5120]{1,0:T(8,128)(2,1)S(1)} %pad_maximum_fusion.5), channel_id=1, source_target_pairs={{0,2},{1,3},{2,0},{3,1},{4,6},{5,7},{6,4},{7,5},{8,10},{9,11},{10,... | collective-permute-start | bytes 1966088 | tf_op jit(solution)/shard_map/ppermute | solution.py:29
  256.1 12.9 %collective-permute-start.18 = (bf16[16,5120]{1,0:T(8,128)(2,1)S(1)}, bf16[16,5120]{1,0:T(8,128)(2,1)S(1)}, u32[]{:S(2)}, u32[]{:S(2)}) collective-permute-start(bf16[16,5120]{1,0:T(8,128)(2,1)S(1)} %get-tuple-element.47), channel_id=1, source_target_pairs={{0,24},{4,28},{8,16},{12,20},{16,8},{20,12},{24,0},{28,4},{1,25},{... | collective-permute-start | bytes 491528 | tf_op jit(solution)/shard_map/ppermute | solution.py:29
  257.1 20.0 %collective-permute-start.17 = (bf16[16,5120]{1,0:T(8,128)(2,1)S(1)}, bf16[16,5120]{1,0:T(8,128)(2,1)S(1)}, u32[]{:S(2)}, u32[]{:S(2)}) collective-permute-start(bf16[16,5120]{1,0:T(8,128)(2,1)S(1)} %get-tuple-element.48), channel_id=1, source_target_pairs={{0,16},{4,20},{8,24},{12,28},{16,0},{20,4},{24,8},{28,12},{1,17},{... | collective-permute-start | bytes 491528 | tf_op jit(solution)/shard_map/ppermute | solution.py:29
  265.5 11.9 %collective-permute-start.32 = (bf16[16,5120]{1,0:T(8,128)(2,1)S(1)}, bf16[16,5120]{1,0:T(8,128)(2,1)S(1)}, u32[]{:S(2)}, u32[]{:S(2)}) collective-permute-start(bf16[16,5120]{1,0:T(8,128)(2,1)S(1)} %get-tuple-element.51), channel_id=1, source_target_pairs={{0,8},{4,12},{8,0},{12,4},{16,24},{20,28},{24,16},{28,20},{1,9},{5... | collective-permute-start | bytes 491528 | tf_op jit(solution)/shard_map/ppermute | solution.py:29
  265.5 11.8 %collective-permute-start.34 = (bf16[16,5120]{1,0:T(8,128)(2,1)S(1)}, bf16[16,5120]{1,0:T(8,128)(2,1)S(1)}, u32[]{:S(2)}, u32[]{:S(2)}) collective-permute-start(bf16[16,5120]{1,0:T(8,128)(2,1)S(1)} %get-tuple-element.52), channel_id=1, source_target_pairs={{0,24},{4,28},{8,16},{12,20},{16,8},{20,12},{24,0},{28,4},{1,25},{... | collective-permute-start | bytes 491528 | tf_op jit(solution)/shard_map/ppermute | solution.py:29
  266.5 15.7 %collective-permute-start.33 = (bf16[16,5120]{1,0:T(8,128)(2,1)S(1)}, bf16[16,5120]{1,0:T(8,128)(2,1)S(1)}, u32[]{:S(2)}, u32[]{:S(2)}) collective-permute-start(bf16[16,5120]{1,0:T(8,128)(2,1)S(1)} %get-tuple-element.53), channel_id=1, source_target_pairs={{0,16},{4,20},{8,24},{12,28},{16,0},{20,4},{24,8},{28,12},{1,17},{... | collective-permute-start | bytes 491528 | tf_op jit(solution)/shard_map/ppermute | solution.py:29
  (48 other events, 371.2 us)

commit v2 on v1

v2 whole, which is shorter than its diff:
```python
import math

import jax
import jax.numpy as jnp
from jax import lax
from jax.experimental import pallas as pl
from jax.experimental.pallas import tpu as pltpu
from jax.sharding import PartitionSpec as P

HEAD_SIZE = 128
QUERY_PER_KV = 5
REQ_DEV = 8
ROOT_DEV = 2
MID_DEV = 4
NODES_DEV = 6
NODE_MAX = 256
OUTER = 4
CHUNKS = 2


EPS = 1e-06


def rms_norm(stream, gain):
    values = stream.astype(jnp.float32)
    mean_sq = jnp.mean(values * values, axis=-1, keepdims=True)
    return (values * lax.rsqrt(mean_sq + EPS) * gain).astype(jnp.bfloat16)


def swap(array, axis, step):
    return lax.ppermute(array, axis, [(i, i ^ step) for i in range(lax.axis_size(axis))])


def attend_kernel(
    local_ref,
    entry_ref,
    queries_ref,
    limits_ref,
    query_segments_ref,
    places_ref,
    segments_ref,
    own_pages_ref,
    sent_pages_ref,
    leaf_keys_ref,
    leaf_values_ref,
    out_ref,
    keys,
    values,
    mask,
):
    tokens = queries_ref.shape[0]
    page = own_pages_ref.shape[2]
    pages = own_pages_ref.shape[0]
    prefix = pages * page
    node_tokens = prefix // NODES_DEV
    leaf_tokens = leaf_keys_ref.shape[0]
    heads_kv = leaf_keys_ref.shape[1] // HEAD_SIZE
    for p in range(pages):
        span = pl.ds(p * page, page)

        @pl.when(local_ref[p] == 1)
        def _():
            keys[span] = own_pages_ref[p, 0]
            values[span] = own_pages_ref[p, 1]

        @pl.when(local_ref[p] == 0)
        def _():
            keys[span] = sent_pages_ref[entry_ref[p], 0]
            values[span] = sent_pages_ref[entry_ref[p], 1]

    keys[pl.ds(prefix, leaf_tokens)] = leaf_keys_ref[...]
    values[pl.ds(prefix, leaf_tokens)] = leaf_values_ref[...]
    at = lax.broadcasted_iota(jnp.int32, (tokens, node_tokens), 1)
    for n in range(NODES_DEV):
        seen = at < limits_ref[:, n : n + 1]
        mask[:, n * node_tokens : (n + 1) * node_tokens] = jnp.where(seen, 0.0, -1e30)
    at = lax.broadcasted_iota(jnp.int32, (tokens, leaf_tokens), 1)
    seen = (segments_ref[...] == query_segments_ref[...]) & (at <= places_ref[...])
    mask[:, prefix:] = jnp.where(seen, 0.0, -1e30)
    scale = 1.0 / math.sqrt(HEAD_SIZE)
    for h in range(heads_kv * QUERY_PER_KV):
        group = pl.ds(h // QUERY_PER_KV * HEAD_SIZE, HEAD_SIZE)
        head = pl.ds(h * HEAD_SIZE, HEAD_SIZE)
        score = lax.dot_general(
            queries_ref[:, head],
            keys[:, group],
            (((1,), (1,)), ((), ())),
            preferred_element_type=jnp.float32,
        )
        score = score * scale + mask[...]
        top = jnp.max(score, axis=1, keepdims=True)
        expo = jnp.exp(score - top)
        total = jnp.sum(expo, axis=1, keepdims=True)
        summed = jnp.dot(
            expo.astype(jnp.bfloat16), values[:, group], preferred_element_type=jnp.float32
        )
        out_ref[:, head] = (summed / total).astype(jnp.bfloat16)


def attend(
    queries, places, query_segments, leaf_keys, leaf_values, fetched, segments, parents, roots, lengths
):
    is_local, entry, own_pages, sent_pages = fetched
    tokens, leaf_tokens = queries.shape[0], leaf_keys.shape[0]
    middle = jnp.sum(
        (query_segments[:, None] == jnp.arange(REQ_DEV)[None, :]) * parents[None, :], axis=1
    )
    root = jnp.sum((middle[:, None] == jnp.arange(MID_DEV)[None, :]) * roots[None, :], axis=1)
    node = jnp.arange(NODES_DEV)[None, :]
    on_path = (node == root[:, None]) | (node == ROOT_DEV + middle[:, None])
    limits = jnp.where(on_path, lengths[None, :], 0)
    key_count = NODES_DEV * NODE_MAX + leaf_tokens
    scalars = pl.BlockSpec(memory_space=pltpu.SMEM)
    whole = pl.BlockSpec(memory_space=pltpu.VMEM)
    columns = leaf_keys.shape[1]
    heads = queries.shape[1] // HEAD_SIZE
    return pl.pallas_call(
        attend_kernel,
        in_specs=[scalars] * 2 + [whole] * 9,
        out_specs=whole,
        out_shape=jax.ShapeDtypeStruct(queries.shape, jnp.bfloat16),
        scratch_shapes=[
            pltpu.VMEM((key_count, columns), jnp.bfloat16),
            pltpu.VMEM((key_count, columns), jnp.bfloat16),
            pltpu.VMEM((tokens, key_count), jnp.float32),
        ],
        compiler_params=pltpu.CompilerParams(vmem_limit_bytes=20 * 1024 * 1024),
        cost_estimate=pl.CostEstimate(
            flops=4 * tokens * heads * HEAD_SIZE * key_count,
            bytes_accessed=8 * key_count * columns,
            transcendentals=tokens * heads * key_count,
        ),
        name="attend",
    )(
        is_local,
        entry,
        queries,
        limits,
        query_segments[:, None],
        places[:, None],
        segments[None, :],
        own_pages,
        sent_pages,
        leaf_keys,
        leaf_values,
    )


def fetch_prefix(key_value_pages, page_holder, page_slot):
    groups = lax.axis_size("req")
    myself = lax.axis_index("req")
    holders = page_holder.reshape(groups, -1)
    slots = page_slot.reshape(groups, -1)
    token_count = holders.shape[1]
    room = (token_count // 2 + groups - 2) // (groups - 1)
    earlier = jnp.arange(token_count)[None, :] < jnp.arange(token_count)[:, None]
    same = holders[:, :, None] == holders[:, None, :]
    rank = jnp.sum(same & earlier[None, :, :], axis=-1)
    asked = (holders == myself) & (jnp.arange(groups)[:, None] != myself)
    picked = asked[:, None, :] & (rank[:, None, :] == jnp.arange(room)[None, :, None])
    send_slot = jnp.sum(jnp.where(picked, slots[:, None, :], 0), axis=-1)
    outgoing = jnp.swapaxes(key_value_pages[send_slot.reshape(-1)], 1, 2)
    incoming = lax.all_to_all(outgoing, "req", split_axis=0, concat_axis=0, tiled=True)
    own_holders = lax.dynamic_index_in_dim(holders, myself, 0, keepdims=False)
    own_slots = lax.dynamic_index_in_dim(slots, myself, 0, keepdims=False)
    own_rank = lax.dynamic_index_in_dim(rank, myself, 0, keepdims=False)
    entry = own_holders * room + jnp.minimum(own_rank, room - 1)
    local = jnp.swapaxes(key_value_pages[own_slots], 1, 2)
    return (own_holders == myself).astype(jnp.int32), entry, local, incoming


def gather_tokens(rows):
    inner = lax.axis_size("req") // OUTER
    across = lax.axis_size("mlp") // 2
    column = jnp.concatenate(
        [rows] + [swap(rows, "req", k * inner) for k in range(1, OUTER)], 0
    )
    half = column.shape[0] // 2
    by_x = {k: swap(column, "mlp", 2 * k) for k in range(1, across)}
    by_y = {l: swap(column, "req", l) for l in range(1, inner)}
    blocks = [column] + list(by_x.values()) + list(by_y.values())
    for k in range(1, across):
        for l in range(1, inner):
            blocks.append(swap(by_y[l][:half], "mlp", 2 * k))
            blocks.append(swap(by_x[k][half:], "req", l))
    return jnp.concatenate(blocks, 0)


def scatter_sum(partial, rows):
    inner = lax.axis_size("req") // OUTER
    across = lax.axis_size("mlp") // 2
    size = OUTER * rows
    half = size // 2
    blocks = [partial[i * size : (i + 1) * size] for i in range(across * inner)]
    wide = jnp.float32
    column = blocks[0].astype(wide)
    by_x = {k: blocks[k].astype(wide) for k in range(1, across)}
    by_y = {l: blocks[across - 1 + l].astype(wide) for l in range(1, inner)}
    at = across + inner - 1
    for k in range(1, across):
        for l in range(1, inner):
            first = swap(blocks[at][:half], "mlp", 2 * k).astype(wide)
            second = swap(blocks[at][half:], "req", l).astype(wide)
            by_y[l] = jnp.concatenate([by_y[l][:half] + first, by_y[l][half:]], 0)
            by_x[k] = jnp.concatenate([by_x[k][:half], by_x[k][half:] + second], 0)
            at += 1
    for k in range(1, across):
        column = column + swap(by_x[k].astype(jnp.bfloat16), "mlp", 2 * k).astype(wide)
    for l in range(1, inner):
        column = column + swap(by_y[l].astype(jnp.bfloat16), "req", l).astype(wide)
    total = column[:rows]
    for k in range(1, OUTER):
        part = column[k * rows : (k + 1) * rows].astype(jnp.bfloat16)
        total = total + swap(part, "req", k * inner).astype(wide)
    return total


def sum_cores(projected, rows):
    members = lax.axis_size("mlp")
    wide = jnp.float32
    blocks = [projected[j * rows : (j + 1) * rows] for j in range(members)]
    odd = jnp.concatenate(blocks[1::2], 0).astype(jnp.bfloat16)
    return jnp.concatenate(blocks[0::2], 0) + swap(odd, "mlp", 1).astype(wide)


def sum_across(even, rows):
    members = lax.axis_size("mlp")
    wide = jnp.float32
    total = even[:rows]
    for k in range(1, members // 2):
        part = even[k * rows : (k + 1) * rows].astype(jnp.bfloat16)
        total = total + swap(part, "mlp", 2 * k).astype(wide)
    return total


def gather_heads(rows):
    members = lax.axis_size("mlp")
    place = lax.axis_index("mlp")
    size = rows.shape[0]
    near = [rows] + [swap(rows, "mlp", 2 * k) for k in range(1, members // 2)]
    far = swap(jnp.concatenate(near, 0), "mlp", 1)
    blocks = []
    for k, block in enumerate(near):
        blocks += [block, far[k * size : (k + 1) * size]]
    step = 1
    while step < members:
        flip = (place // step) % 2 == 1
        blocks = [
            jnp.where(flip, blocks[j ^ step], blocks[j]) for j in range(members)
        ]
        step *= 2
    return blocks


def feed_forward_kernel(
    steps_in, x_ref, g0_ref, g1_ref, u0_ref, u1_ref, d0_ref, d1_ref, out_ref, acc, hidden
):
    step = pl.program_id(0)
    wide = jnp.float32

    @pl.when(step < steps_in)
    def _():
        x = x_ref[...]
        parts = [
            lax.dot_general(x, w[...], (((1,), (1,)), ((), ())), preferred_element_type=wide)
            for w in (g0_ref, g1_ref, u0_ref, u1_ref)
        ]

        @pl.when(step == 0)
        def _():
            for n, part in enumerate(parts):
                acc[n] = part

        @pl.when(step > 0)
        def _():
            for n, part in enumerate(parts):
                acc[n] += part

    @pl.when(step == steps_in - 1)
    def _():
        for n in range(2):
            gate = acc[n]
            hidden[n] = (gate / (1.0 + jnp.exp(-gate)) * acc[2 + n]).astype(jnp.bfloat16)

    @pl.when(step >= steps_in)
    def _():
        total = jnp.dot(hidden[0], d0_ref[...], preferred_element_type=wide)
        total += jnp.dot(hidden[1], d1_ref[...], preferred_element_type=wide)
        out_ref[...] = total.astype(jnp.bfloat16)


def feed_forward(tokens, gates, uppers, downs):
    rows, width = tokens.shape
    units = gates[0].shape[0]
    steps_in, steps_out = 4, 4
    depth, span = width // steps_in, width // steps_out

    def inner(i):
        return jnp.minimum(i, steps_in - 1)

    def outer(i):
        return jnp.maximum(i - steps_in, 0)

    weight = pl.BlockSpec((units, depth), lambda i: (0, inner(i)))
    down = pl.BlockSpec((units, span), lambda i: (0, outer(i)))
    return pl.pallas_call(
        lambda *refs: feed_forward_kernel(steps_in, *refs),
        grid=(steps_in + steps_out,),
        in_specs=[pl.BlockSpec((rows, depth), lambda i: (0, inner(i)))]
        + [weight] * 4
        + [down] * 2,
        out_specs=pl.BlockSpec((rows, span), lambda i: (0, outer(i))),
        out_shape=jax.ShapeDtypeStruct((rows, width), jnp.bfloat16),
        scratch_shapes=[
            pltpu.VMEM((4, rows, units), jnp.float32),
            pltpu.VMEM((2, rows, units), jnp.bfloat16),
        ],
        compiler_params=pltpu.CompilerParams(vmem_limit_bytes=24 * 1024 * 1024),
        cost_estimate=pl.CostEstimate(
            flops=12 * rows * width * units,
            bytes_accessed=12 * width * units + 4 * rows * width,
            transcendentals=2 * rows * units,
        ),
        name="feed_forward",
    )(tokens, *gates, *uppers, *downs)


def body(
    queries,
    leaf_keys,
    leaf_token_values,
    key_value_pages,
    page_holder,
    page_slot,
    segment_ids,
    req_parent,
    mid_parent,
    node_len,
    residual,
    out_proj,
    norm_gain,
    gate_proj,
    up_proj,
    down_proj,
    next_gain,
    qkv_proj,
    qkv_bias,
):
    group_tokens = queries.shape[0]
    members = lax.axis_size("mlp")
    place = lax.axis_index("mlp")
    owned = group_tokens // members
    rows = owned // CHUNKS
    gate_rows, up_rows = gate_proj.T, up_proj.T
    gates = [gate_rows, swap(gate_rows, "mlp", 1)]
    uppers = [up_rows, swap(up_rows, "mlp", 1)]
    downs = [down_proj, swap(down_proj, "mlp", 1)]
    fetched = fetch_prefix(key_value_pages, page_holder, page_slot)
    starts = [
        (place ^ j) * owned + chunk * rows for chunk in range(CHUNKS) for j in range(members)
    ]

    def picked(array):
        return jnp.concatenate([lax.dynamic_slice_in_dim(array, s, rows, 0) for s in starts], 0)

    places = jnp.concatenate([s + jnp.arange(rows) for s in starts], 0)
    asked, fetched, gates, uppers, downs = lax.optimization_barrier(
        (picked(queries), fetched, gates, uppers, downs)
    )
    attention = attend(
        asked,
        places,
        picked(segment_ids),
        leaf_keys,
        leaf_token_values,
        fetched,
        segment_ids,
        req_parent[0],
        mid_parent[0],
        node_len[0],
    )
    projected = jnp.dot(attention, out_proj, preferred_element_type=jnp.float32)
    span = members * rows
    evens = [sum_cores(projected[c * span : (c + 1) * span], rows) for c in range(CHUNKS)]
    streams, mixed = [], []
    for chunk in range(CHUNKS):
        own = lax.dynamic_slice_in_dim(residual, place * owned + chunk * rows, rows, 0)
        summed = sum_across(evens[chunk], rows)
        streams.append((own.astype(jnp.float32) + summed).astype(jnp.bfloat16))
    for chunk in range(CHUNKS):
        tokens = gather_tokens(rms_norm(streams[chunk], norm_gain))
        mixed.append(feed_forward(tokens, gates, uppers, downs))
    layer_rows, next_rows = [], []
    for chunk in range(CHUNKS):
        summed = scatter_sum(mixed[chunk], rows)
        layer = (streams[chunk].astype(jnp.float32) + summed).astype(jnp.bfloat16)
        layer_rows.append(layer)
        next_rows.append(gather_heads(rms_norm(layer, next_gain)))
    layer_out = jnp.concatenate(layer_rows, 0)
    next_normed = jnp.concatenate(
        [next_rows[c][j] for j in range(members) for c in range(CHUNKS)], 0
    )
    qkv_out = (
        jnp.dot(next_normed, qkv_proj, preferred_element_type=jnp.float32) + qkv_bias
    ).astype(jnp.bfloat16)
    return (layer_out, qkv_out)


def solution(mesh):
    placed = (
        P("req", "mlp"),
        P("req", "mlp"),
        P("req", "mlp"),
        P("req", None, None, "mlp"),
        P(),
        P(),
        P("req"),
        P("req", None),
        P("req", None),
        P("req", None),
        P("req", None),
        P("mlp", None),
        P(),
        P(None, ("req", "mlp")),
        P(None, ("req", "mlp")),
        P(("req", "mlp"), None),
        P(),
        P(None, "mlp"),
        P("mlp"),
    )
    return jax.shard_map(
        body,
        mesh=mesh,
        in_specs=placed,
        out_specs=(P(("req", "mlp"), None), P("req", "mlp")),
        check_vma=False,
    )
```

time: 309 us -> 233 us (0.75); the launches traced: 303 us -> 232 us
  matrix products: 95.1 us -> 16.3 us
  Pallas kernels: 0 us -> 35.1 us
  waiting for transfers between devices: 110 us -> 82.5 us
  starting transfers between devices: 49.7 us -> 58.2 us
  local copies, waits for them, and re-layouts: 34.3 us -> 26.4 us
    dot_general x12 -> x1, matrix products: 78.7 us -> 6.6 us  [body(): projected = jnp.dot(attention, out_proj, preferred_element_type=jnp.float32)]
    pallas_call x0 -> x3, Pallas kernels: none -> 35.1 us  [the longest x2 29 us: feed_forward(): pl.pallas_call(lambda *refs: feed_forward_kernel(steps_in, *refs), grid=(...]
    ppermute x39, waiting for transfers between devices: 103 us -> 69.7 us  [swap(): lax.ppermute(array, axis, [(i, i ^ step) for i in range(lax.axis_size(axi...]
    ppermute x39, starting transfers between devices: 42.4 us -> 51.2 us  [swap(): lax.ppermute(array, axis, [(i, i ^ step) for i in range(lax.axis_size(axi...]
    sub x2 -> x0, matrix products: 6.62 us -> none  [attend(): expo = jnp.where(mask[:, None, None, :], jnp.exp(score - top), 0.0)]
    all_to_all x1, waiting for transfers between devices: 7.35 us -> 12.8 us  [fetch_prefix(): lax.all_to_all(outgoing, 'req', split_axis=0, concat_axis=0, tiled=True)]
    unnamed x78 -> x77, local copies, waits for them, and re-layouts: 7.07 us -> 12 us
    gather x6 -> x4, local copies, waits for them, and re-layouts: 15.7 us -> 11.6 us  [the longest x2 7.75 us: fetch_prefix(): local = jnp.swapaxes(key_value_pages[own_slots], 1, 2)]
  transfers between devices with their start and end apart: 40 -> 40, of which waited for: 21 -> 19; matrix products, arithmetic and copies ran while one was open for 26% -> 12% of each run, Pallas kernels for 0% -> 12%
where the time goes in v2:
time: 233 us; the launch traced here: 232 us
  waiting for transfers between devices  82.5 us (35%)
  starting transfers between devices  58.2 us (25%)
  Pallas kernels  35.1 us (15%)
  local copies, waits for them, and re-layouts  26.4 us (11%)
  matrix products  16.3 us (7%)
  other arithmetic  11.8 us (5%)
    ppermute x39, waiting for transfers between devices, swap(): lax.ppermute(array, axis, [(i, i ^ step) for i in range(lax.axis_size(axi...  69.7 us
    ppermute x39, starting transfers between devices, swap(): lax.ppermute(array, axis, [(i, i ^ step) for i in range(lax.axis_size(axi...  51.2 us
    pallas_call x2, Pallas kernels, feed_forward(): pl.pallas_call(lambda *refs: feed_forward_kernel(steps_in, *refs), grid=(...  29 us
    all_to_all x1, waiting for transfers between devices, fetch_prefix(): lax.all_to_all(outgoing, 'req', split_axis=0, concat_axis=0, tiled=True)  12.8 us
    unnamed x77, local copies, waits for them, and re-layouts  12 us
    dot_general x1, matrix products, body(): jnp.dot(next_normed, qkv_proj, preferred_element_type=jnp.float32)  9.71 us
    gather x2, local copies, waits for them, and re-layouts, fetch_prefix(): local = jnp.swapaxes(key_value_pages[own_slots], 1, 2)  7.75 us
    all_to_all x1, starting transfers between devices, fetch_prefix(): lax.all_to_all(outgoing, 'req', split_axis=0, concat_axis=0, tiled=True)  7.04 us
  transfers between devices with their start and end apart: 40, of which 19 were waited for; matrix products, arithmetic and copies ran while one was open for 12% of the time, Pallas kernels for 12%

profile of v2, /device:TPU:0, one launch (start us, length us, event | category | flops | bytes accessed | tf_op | source)
XLA Modules:
  0.0 231.8 jit_solution(15194248150699101609)
XLA Ops:
  4.7 2.7 %gather_fusion.1 = bf16[16,64,2,256]{3,2,1,0:T(2,128)(2,1)S(1)} fusion(bf16[32,64,2,256]{3,2,1,0:T(2,128)(2,1)S(1)} %copy-done, s32[1024]{0:T(1024)S(1)} %get-tuple-element.82), kind=kCustom, calls=%fused_computation.1 | custom fusion | bytes 2097216 | tf_op jit(solution)/shard_map/gather | solution.py:162
  8.6 7.0 %all-to-all-start = ((bf16[16,2,64,256]{3,2,1,0:T(8,128)(2,1)}), bf16[16,2,64,256]{3,2,1,0:T(8,128)(2,1)S(1)}, u32[]{:S(2)}, u32[]{:S(2)}) async-start(bf16[16,2,64,256]{3,2,1,0:T(8,128)(2,1)} %bitcast.44), calls=%async_computation | async-start | bytes 2097152 | tf_op jit(solution)/shard_map/all_to_all | solution.py:163
  20.0 6.0 %gather_fusion = bf16[24,64,2,256]{3,2,1,0:T(2,128)(2,1)} fusion(bf16[32,64,2,256]{3,2,1,0:T(2,128)(2,1)S(1)} %copy-done, s32[1024]{0:T(1024)S(1)} %get-tuple-element.83), kind=kCustom, calls=%fused_computation | custom fusion | bytes 3145824 | tf_op jit(solution)/shard_map/gather | solution.py:168
  29.2 12.8 %all-to-all-done.sent_pages_ref = bf16[16,2,64,256]{3,2,1,0:T(8,128)(2,1)S(1)} async-done(((bf16[16,2,64,256]{3,2,1,0:T(8,128)(2,1)}), bf16[16,2,64,256]{3,2,1,0:T(8,128)(2,1)S(1)}, u32[]{:S(2)}, u32[]{:S(2)}) %all-to-all-start) | async-done | bytes 1048608 | tf_op jit(solution)/shard_map/all_to_all | solution.py:163
  42.8 6.1 %attend.1 = bf16[128,1280]{1,0:T(8,128)(2,1)S(1)} custom-call(s32[24]{0:T(128)S(1)} %fusion.26.local_ref, s32[24]{0:T(128)S(1)} %fusion.32.entry_ref, bf16[128,1280]{1,0:T(8,128)(2,1)S(1)} %constant_dynamic-update-slice_fusion.queries_ref, s32[128,6]{1,0:T(8,128)S(1)} %fusion.24.limits_ref, s32[128,1]{1,0:T(8,128)S(1)} %copy.56.query_segments_ref, ...), custom_call_target="tpu_custom_call" | custom-call | flops 1090519040 | bytes 3407872 | tf_op jit(solution)/shard_map/attend/pallas_call | solution.py:117
  49.0 6.6 %fusion.48 = (bf16[128,5120]{1,0:T(8,128)(2,1)S(1)}, f32[128,5120]{1,0:T(8,128)S(1)}) fusion(bf16[128,1280]{1,0:T(8,128)(2,1)S(1)} %attend.1, bf16[1280,5120]{1,0:T(8,128)(2,1)} %param.30), kind=kOutput, calls=%fused_computation.155 | convolution fusion | flops 1678376960 | bytes 17367040 | tf_op jit(solution)/shard_map/dot_general | solution.py:382
  59.8 4.9 %collective-permute-done.4 = bf16[16,5120]{1,0:T(8,128)(2,1)S(1)} collective-permute-done((bf16[16,5120]{1,0:T(8,128)(2,1)S(1)}, bf16[16,5120]{1,0:T(8,128)(2,1)S(1)}, u32[]{:S(2)}, u32[]{:S(2)}) %collective-permute-start.4) | collective-permute-done | bytes 163872 | tf_op jit(solution)/shard_map/ppermute | solution.py:31
  64.6 2.7 %collective-permute-done.20 = bf16[16,5120]{1,0:T(8,128)(2,1)S(1)} collective-permute-done((bf16[16,5120]{1,0:T(8,128)(2,1)S(1)}, bf16[16,5120]{1,0:T(8,128)(2,1)S(1)}, u32[]{:S(2)}, u32[]{:S(2)}) %collective-permute-start.20) | collective-permute-done | bytes 163872 | tf_op jit(solution)/shard_map/ppermute | solution.py:31
  69.5 2.7 %collective-permute-start.22 = (bf16[16,5120]{1,0:T(8,128)(2,1)S(1)}, bf16[16,5120]{1,0:T(8,128)(2,1)}, u32[]{:S(2)}, u32[]{:S(2)}) collective-permute-start(bf16[16,5120]{1,0:T(8,128)(2,1)S(1)} %get-tuple-element.71), channel_id=1, source_target_pairs={{0,16},{4,20},{8,24},{12,28},{16,0},{20,4},{24,8},{28,12},{1,17},{... | collective-permute-start | bytes 491528 | tf_op jit(solution)/shard_map/ppermute | solution.py:31
  73.9 2.7 %collective-permute-start.6 = (bf16[16,5120]{1,0:T(8,128)(2,1)S(1)}, bf16[16,5120]{1,0:T(8,128)(2,1)S(1)}, u32[]{:S(2)}, u32[]{:S(2)}) collective-permute-start(bf16[16,5120]{1,0:T(8,128)(2,1)S(1)} %get-tuple-element.31), channel_id=1, source_target_pairs={{0,16},{4,20},{8,24},{12,28},{16,0},{20,4},{24,8},{28,12},{1,17},{... | collective-permute-start | bytes 491528 | tf_op jit(solution)/shard_map/ppermute | solution.py:31
  76.6 2.9 %collective-permute-done.21 = bf16[16,5120]{1,0:T(8,128)(2,1)} collective-permute-done((bf16[16,5120]{1,0:T(8,128)(2,1)S(1)}, bf16[16,5120]{1,0:T(8,128)(2,1)}, u32[]{:S(2)}, u32[]{:S(2)}) %collective-permute-start.21) | collective-permute-done | bytes 163872 | tf_op jit(solution)/shard_map/ppermute | solution.py:31
  81.8 2.9 %collective-permute-done.22 = bf16[16,5120]{1,0:T(8,128)(2,1)} collective-permute-done((bf16[16,5120]{1,0:T(8,128)(2,1)S(1)}, bf16[16,5120]{1,0:T(8,128)(2,1)}, u32[]{:S(2)}, u32[]{:S(2)}) %collective-permute-start.22) | collective-permute-done | bytes 163872 | tf_op jit(solution)/shard_map/ppermute | solution.py:31
  88.9 9.7 %collective-permute-done.6 = bf16[16,5120]{1,0:T(8,128)(2,1)S(1)} collective-permute-done((bf16[16,5120]{1,0:T(8,128)(2,1)S(1)}, bf16[16,5120]{1,0:T(8,128)(2,1)S(1)}, u32[]{:S(2)}, u32[]{:S(2)}) %collective-permute-start.6) | collective-permute-done | bytes 163872 | tf_op jit(solution)/shard_map/ppermute | solution.py:31
  105.8 12.0 %collective-permute-done.9 = bf16[64,5120]{1,0:T(8,128)(2,1)S(1)} collective-permute-done((bf16[64,5120]{1,0:T(8,128)(2,1)S(1)}, bf16[64,5120]{1,0:T(8,128)(2,1)S(1)}, u32[]{:S(2)}, u32[]{:S(2)}) %collective-permute-start.9) | collective-permute-done | bytes 655392 | tf_op jit(solution)/shard_map/ppermute | solution.py:31
  120.0 3.3 %collective-permute-done.26 = bf16[32,5120]{1,0:T(8,128)(2,1)S(1)} collective-permute-done((bf16[32,5120]{1,0:T(8,128)(2,1)S(1)}, bf16[32,5120]{1,0:T(8,128)(2,1)S(1)}, u32[]{:S(2)}, u32[]{:S(2)}) %collective-permute-start.26) | collective-permute-done | bytes 327712 | tf_op jit(solution)/shard_map/ppermute | solution.py:31
  129.3 14.3 %feed_forward.3 = bf16[256,5120]{1,0:T(8,128)(2,1)S(1)} custom-call(bf16[256,5120]{1,0:T(8,128)(2,1)S(1)} %constant_dynamic-update-slice_fusion.16.refs_0_, bf16[432,5120]{1,0:T(8,128)(2,1)S(1)} %bitcast.35, bf16[432,5120]{1,0:T(8,128)(2,1)} %collective-permute-done.refs_2_, bf16[432,5120]{1,0:T(8,128)(2,1)S(1)} %bitcast.38, ...), custom_call_target="tpu_custom_call" | custom-call | flops 6794772480 | bytes 31784960 | tf_op jit(solution)/shard_map/feed_forward/pallas_call | solution.py:306
  147.7 14.6 %feed_forward.2 = bf16[256,5120]{1,0:T(8,128)(2,1)S(1)} custom-call(bf16[256,5120]{1,0:T(8,128)(2,1)S(1)} %constant_dynamic-update-slice_fusion.8.refs_0_, bf16[432,5120]{1,0:T(8,128)(2,1)S(1)} %bitcast.36, bf16[432,5120]{1,0:T(8,128)(2,1)} %collective-permute-done.refs_2_, bf16[432,5120]{1,0:T(8,128)(2,1)S(1)} %bitcast.41, ...), custom_call_target="tpu_custom_call" | custom-call | flops 6794772480 | bytes 31784960 | tf_op jit(solution)/shard_map/feed_forward/pallas_call | solution.py:306
  167.0 6.2 %collective-permute-done.12 = bf16[32,5120]{1,0:T(8,128)(2,1)S(1)} collective-permute-done((bf16[32,5120]{1,0:T(8,128)(2,1)S(1)}, bf16[32,5120]{1,0:T(8,128)(2,1)S(1)}, u32[]{:S(2)}, u32[]{:S(2)}) %collective-permute-start.12) | collective-permute-done | bytes 327712 | tf_op jit(solution)/shard_map/ppermute | solution.py:31
  177.0 9.2 %collective-permute-done.31 = bf16[64,5120]{1,0:T(8,128)(2,1)S(1)} collective-permute-done((bf16[64,5120]{1,0:T(8,128)(2,1)S(1)}, bf16[64,5120]{1,0:T(8,128)(2,1)S(1)}, u32[]{:S(2)}, u32[]{:S(2)}) %collective-permute-start.31) | collective-permute-done | bytes 655392 | tf_op jit(solution)/shard_map/ppermute | solution.py:31
  189.5 6.8 %collective-permute-start.33 = (bf16[16,5120]{1,0:T(8,128)(2,1)S(1)}, bf16[16,5120]{1,0:T(8,128)(2,1)S(1)}, u32[]{:S(2)}, u32[]{:S(2)}) collective-permute-start(bf16[16,5120]{1,0:T(8,128)(2,1)S(1)} %get-tuple-element.67), channel_id=1, source_target_pairs={{0,16},{4,20},{8,24},{12,28},{16,0},{20,4},{24,8},{28,12},{1,17},{... | collective-permute-start | bytes 491528 | tf_op jit(solution)/shard_map/ppermute | solution.py:31
  198.1 5.2 %collective-permute-start.17 = (bf16[16,5120]{1,0:T(8,128)(2,1)S(1)}, bf16[16,5120]{1,0:T(8,128)(2,1)S(1)}, u32[]{:S(2)}, u32[]{:S(2)}) collective-permute-start(bf16[16,5120]{1,0:T(8,128)(2,1)S(1)} %get-tuple-element.64), channel_id=1, source_target_pairs={{0,16},{4,20},{8,24},{12,28},{16,0},{20,4},{24,8},{28,12},{1,17},{... | collective-permute-start | bytes 491528 | tf_op jit(solution)/shard_map/ppermute | solution.py:31
  205.2 3.1 %collective-permute-done.33 = bf16[16,5120]{1,0:T(8,128)(2,1)S(1)} collective-permute-done((bf16[16,5120]{1,0:T(8,128)(2,1)S(1)}, bf16[16,5120]{1,0:T(8,128)(2,1)S(1)}, u32[]{:S(2)}, u32[]{:S(2)}) %collective-permute-start.33) | collective-permute-done | bytes 163872 | tf_op jit(solution)/shard_map/ppermute | solution.py:31
  208.5 3.2 %collective-permute-done.17 = bf16[16,5120]{1,0:T(8,128)(2,1)S(1)} collective-permute-done((bf16[16,5120]{1,0:T(8,128)(2,1)S(1)}, bf16[16,5120]{1,0:T(8,128)(2,1)S(1)}, u32[]{:S(2)}, u32[]{:S(2)}) %collective-permute-start.17) | collective-permute-done | bytes 163872 | tf_op jit(solution)/shard_map/ppermute | solution.py:31
  222.1 9.7 %fusion = bf16[128,1792]{1,0:T(8,128)(2,1)} fusion(bf16[128,5120]{1,0:T(8,128)(2,1)S(1)} %select_dynamic-update-slice_fusion, bf16[5120,1792]{1,0:T(8,128)(2,1)} %param.36, f32[1792]{0:T(1024)S(1)} %copy-done.14), kind=kOutput, calls=%fused_computation.3 | convolution fusion | flops 2349268992 | bytes 20126720 | tf_op jit(solution)/shard_map/dot_general | solution.py:404
  (221 shorter events, 73.1 us)
Async XLA Ops:
  0.6 41.3 %collective-permute-start = (bf16[432,5120]{1,0:T(8,128)(2,1)}, bf16[432,5120]{1,0:T(8,128)(2,1)}, u32[]{:S(2)}, u32[]{:S(2)}) collective-permute-start(bf16[432,5120]{1,0:T(8,128)(2,1)} %bitcast.32), channel_id=1, source_target_pairs={{0,1},{1,0},{2,3},{3,2},{4,5},{5,4},{6,7},{7,6},{8,9},{9,8},{10,11... | collective-permute-start | bytes 13271048 | tf_op jit(solution)/shard_map/ppermute | solution.py:31
  1.2 40.8 %collective-permute-start.1 = (bf16[432,5120]{1,0:T(8,128)(2,1)}, bf16[432,5120]{1,0:T(8,128)(2,1)}, u32[]{:S(2)}, u32[]{:S(2)}) collective-permute-start(bf16[432,5120]{1,0:T(8,128)(2,1)} %bitcast.37), channel_id=1, source_target_pairs={{0,1},{1,0},{2,3},{3,2},{4,5},{5,4},{6,7},{7,6},{8,9},{9,8},{10,11... | collective-permute-start | bytes 13271048 | tf_op jit(solution)/shard_map/ppermute | solution.py:31
  1.2 40.7 %collective-permute-start.2 = (bf16[432,5120]{1,0:T(8,128)(2,1)}, bf16[432,5120]{1,0:T(8,128)(2,1)}, u32[]{:S(2)}, u32[]{:S(2)}) collective-permute-start(bf16[432,5120]{1,0:T(8,128)(2,1)} %refs_5_.1), channel_id=1, source_target_pairs={{0,1},{1,0},{2,3},{3,2},{4,5},{5,4},{6,7},{7,6},{8,9},{9,8},{10,11... | collective-permute-start | bytes 13271048 | tf_op jit(solution)/shard_map/ppermute | solution.py:31
  8.6 33.4 %all-to-all-start = ((bf16[16,2,64,256]{3,2,1,0:T(8,128)(2,1)}), bf16[16,2,64,256]{3,2,1,0:T(8,128)(2,1)S(1)}, u32[]{:S(2)}, u32[]{:S(2)}) async-start(bf16[16,2,64,256]{3,2,1,0:T(8,128)(2,1)} %bitcast.44), calls=%async_computation | async-start | bytes 2097152 | tf_op jit(solution)/shard_map/all_to_all | solution.py:163
  69.5 15.2 %collective-permute-start.22 = (bf16[16,5120]{1,0:T(8,128)(2,1)S(1)}, bf16[16,5120]{1,0:T(8,128)(2,1)}, u32[]{:S(2)}, u32[]{:S(2)}) collective-permute-start(bf16[16,5120]{1,0:T(8,128)(2,1)S(1)} %get-tuple-element.71), channel_id=1, source_target_pairs={{0,16},{4,20},{8,24},{12,28},{16,0},{20,4},{24,8},{28,12},{1,17},{... | collective-permute-start | bytes 491528 | tf_op jit(solution)/shard_map/ppermute | solution.py:31
  73.8 15.0 %collective-permute-start.5 = (bf16[16,5120]{1,0:T(8,128)(2,1)S(1)}, bf16[16,5120]{1,0:T(8,128)(2,1)S(1)}, u32[]{:S(2)}, u32[]{:S(2)}) collective-permute-start(bf16[16,5120]{1,0:T(8,128)(2,1)S(1)} %get-tuple-element.31), channel_id=1, source_target_pairs={{0,8},{4,12},{8,0},{12,4},{16,24},{20,28},{24,16},{28,20},{1,9},{5... | collective-permute-start | bytes 491528 | tf_op jit(solution)/shard_map/ppermute | solution.py:31
  73.9 24.7 %collective-permute-start.6 = (bf16[16,5120]{1,0:T(8,128)(2,1)S(1)}, bf16[16,5120]{1,0:T(8,128)(2,1)S(1)}, u32[]{:S(2)}, u32[]{:S(2)}) collective-permute-start(bf16[16,5120]{1,0:T(8,128)(2,1)S(1)} %get-tuple-element.31), channel_id=1, source_target_pairs={{0,16},{4,20},{8,24},{12,28},{16,0},{20,4},{24,8},{28,12},{1,17},{... | collective-permute-start | bytes 491528 | tf_op jit(solution)/shard_map/ppermute | solution.py:31
  79.4 19.1 %collective-permute-start.7 = (bf16[16,5120]{1,0:T(8,128)(2,1)S(1)}, bf16[16,5120]{1,0:T(8,128)(2,1)S(1)}, u32[]{:S(2)}, u32[]{:S(2)}) collective-permute-start(bf16[16,5120]{1,0:T(8,128)(2,1)S(1)} %get-tuple-element.31), channel_id=1, source_target_pairs={{0,24},{4,28},{8,16},{12,20},{16,8},{20,12},{24,0},{28,4},{1,25},{... | collective-permute-start | bytes 491528 | tf_op jit(solution)/shard_map/ppermute | solution.py:31
  85.8 19.1 %collective-permute-start.24 = (bf16[64,5120]{1,0:T(8,128)(2,1)S(1)}, bf16[64,5120]{1,0:T(8,128)(2,1)S(1)}, u32[]{:S(2)}, u32[]{:S(2)}) collective-permute-start(bf16[64,5120]{1,0:T(8,128)(2,1)S(1)} %pad_maximum_fusion.3), channel_id=1, source_target_pairs={{0,2},{1,3},{2,0},{3,1},{4,6},{5,7},{6,4},{7,5},{8,10},{9,11},{10,... | collective-permute-start | bytes 1966088 | tf_op jit(solution)/shard_map/ppermute | solution.py:31
  87.3 16.9 %collective-permute-start.25 = (bf16[64,5120]{1,0:T(8,128)(2,1)S(1)}, bf16[64,5120]{1,0:T(8,128)(2,1)S(1)}, u32[]{:S(2)}, u32[]{:S(2)}) collective-permute-start(bf16[64,5120]{1,0:T(8,128)(2,1)S(1)} %pad_maximum_fusion.3), channel_id=1, source_target_pairs={{0,4},{4,0},{8,12},{12,8},{16,20},{20,16},{24,28},{28,24},{1,5},{5... | collective-permute-start | bytes 1966088 | tf_op jit(solution)/shard_map/ppermute | solution.py:31
  98.6 19.9 %collective-permute-start.8 = (bf16[64,5120]{1,0:T(8,128)(2,1)S(1)}, bf16[64,5120]{1,0:T(8,128)(2,1)S(1)}, u32[]{:S(2)}, u32[]{:S(2)}) collective-permute-start(bf16[64,5120]{1,0:T(8,128)(2,1)S(1)} %pad_maximum_fusion), channel_id=1, source_target_pairs={{0,2},{1,3},{2,0},{3,1},{4,6},{5,7},{6,4},{7,5},{8,10},{9,11},{10,... | collective-permute-start | bytes 1966088 | tf_op jit(solution)/shard_map/ppermute | solution.py:31
  100.1 17.7 %collective-permute-start.9 = (bf16[64,5120]{1,0:T(8,128)(2,1)S(1)}, bf16[64,5120]{1,0:T(8,128)(2,1)S(1)}, u32[]{:S(2)}, u32[]{:S(2)}) collective-permute-start(bf16[64,5120]{1,0:T(8,128)(2,1)S(1)} %pad_maximum_fusion), channel_id=1, source_target_pairs={{0,4},{4,0},{8,12},{12,8},{16,20},{20,16},{24,28},{28,24},{1,5},{5... | collective-permute-start | bytes 1966088 | tf_op jit(solution)/shard_map/ppermute | solution.py:31
  104.3 19.1 %collective-permute-start.26 = (bf16[32,5120]{1,0:T(8,128)(2,1)S(1)}, bf16[32,5120]{1,0:T(8,128)(2,1)S(1)}, u32[]{:S(2)}, u32[]{:S(2)}) collective-permute-start(bf16[32,5120]{1,0:T(8,128)(2,1)S(1)} %slice.257), channel_id=1, source_target_pairs={{0,2},{1,3},{2,0},{3,1},{4,6},{5,7},{6,4},{7,5},{8,10},{9,11},{10,... | collective-permute-start | bytes 983048 | tf_op jit(solution)/shard_map/ppermute | solution.py:31
  104.9 19.8 %collective-permute-start.27 = (bf16[32,5120]{1,0:T(8,128)(2,1)S(1)}, bf16[32,5120]{1,0:T(8,128)(2,1)S(1)}, u32[]{:S(2)}, u32[]{:S(2)}) collective-permute-start(bf16[32,5120]{1,0:T(8,128)(2,1)S(1)} %slice.258), channel_id=1, source_target_pairs={{0,4},{4,0},{8,12},{12,8},{16,20},{20,16},{24,28},{28,24},{1,5},{5... | collective-permute-start | bytes 983048 | tf_op jit(solution)/shard_map/ppermute | solution.py:31
  117.8 27.5 %collective-permute-start.10 = (bf16[32,5120]{1,0:T(8,128)(2,1)S(1)}, bf16[32,5120]{1,0:T(8,128)(2,1)S(1)}, u32[]{:S(2)}, u32[]{:S(2)}) collective-permute-start(bf16[32,5120]{1,0:T(8,128)(2,1)S(1)} %slice.238), channel_id=1, source_target_pairs={{0,2},{1,3},{2,0},{3,1},{4,6},{5,7},{6,4},{7,5},{8,10},{9,11},{10,... | collective-permute-start | bytes 983048 | tf_op jit(solution)/shard_map/ppermute | solution.py:31
  118.5 27.0 %collective-permute-start.11 = (bf16[32,5120]{1,0:T(8,128)(2,1)S(1)}, bf16[32,5120]{1,0:T(8,128)(2,1)S(1)}, u32[]{:S(2)}, u32[]{:S(2)}) collective-permute-start(bf16[32,5120]{1,0:T(8,128)(2,1)S(1)} %slice.239), channel_id=1, source_target_pairs={{0,4},{4,0},{8,12},{12,8},{16,20},{20,16},{24,28},{28,24},{1,5},{5... | collective-permute-start | bytes 983048 | tf_op jit(solution)/shard_map/ppermute | solution.py:31
  143.8 21.2 %collective-permute-start.28 = (bf16[32,5120]{1,0:T(8,128)(2,1)S(1)}, bf16[32,5120]{1,0:T(8,128)(2,1)S(1)}, u32[]{:S(2)}, u32[]{:S(2)}) collective-permute-start(bf16[32,5120]{1,0:T(8,128)(2,1)S(1)} %get-tuple-element.53), channel_id=1, source_target_pairs={{0,4},{4,0},{8,12},{12,8},{16,20},{20,16},{24,28},{28,24},{1,5},{5... | collective-permute-start | bytes 983048 | tf_op jit(solution)/shard_map/ppermute | solution.py:31
  144.8 20.2 %collective-permute-start.30 = (bf16[32,5120]{1,0:T(8,128)(2,1)S(1)}, bf16[32,5120]{1,0:T(8,128)(2,1)S(1)}, u32[]{:S(2)}, u32[]{:S(2)}) collective-permute-start(bf16[32,5120]{1,0:T(8,128)(2,1)S(1)} %get-tuple-element.52), channel_id=1, source_target_pairs={{0,2},{1,3},{2,0},{3,1},{4,6},{5,7},{6,4},{7,5},{8,10},{9,11},{10,... | collective-permute-start | bytes 983048 | tf_op jit(solution)/shard_map/ppermute | solution.py:31
  165.2 21.0 %collective-permute-start.31 = (bf16[64,5120]{1,0:T(8,128)(2,1)S(1)}, bf16[64,5120]{1,0:T(8,128)(2,1)S(1)}, u32[]{:S(2)}, u32[]{:S(2)}) collective-permute-start(bf16[64,5120]{1,0:T(8,128)(2,1)S(1)} %pad_maximum_fusion.5), channel_id=1, source_target_pairs={{0,4},{4,0},{8,12},{12,8},{16,20},{20,16},{24,28},{28,24},{1,5},{5... | collective-permute-start | bytes 1966088 | tf_op jit(solution)/shard_map/ppermute | solution.py:31
  166.3 20.3 %collective-permute-start.29 = (bf16[64,5120]{1,0:T(8,128)(2,1)S(1)}, bf16[64,5120]{1,0:T(8,128)(2,1)S(1)}, u32[]{:S(2)}, u32[]{:S(2)}) collective-permute-start(bf16[64,5120]{1,0:T(8,128)(2,1)S(1)} %pad_maximum_fusion.4), channel_id=1, source_target_pairs={{0,2},{1,3},{2,0},{3,1},{4,6},{5,7},{6,4},{7,5},{8,10},{9,11},{10,... | collective-permute-start | bytes 1966088 | tf_op jit(solution)/shard_map/ppermute | solution.py:31
  174.4 21.9 %collective-permute-start.15 = (bf16[64,5120]{1,0:T(8,128)(2,1)S(1)}, bf16[64,5120]{1,0:T(8,128)(2,1)S(1)}, u32[]{:S(2)}, u32[]{:S(2)}) collective-permute-start(bf16[64,5120]{1,0:T(8,128)(2,1)S(1)} %pad_maximum_fusion.2), channel_id=1, source_target_pairs={{0,4},{4,0},{8,12},{12,8},{16,20},{20,16},{24,28},{28,24},{1,5},{5... | collective-permute-start | bytes 1966088 | tf_op jit(solution)/shard_map/ppermute | solution.py:31
  175.5 20.8 %collective-permute-start.13 = (bf16[64,5120]{1,0:T(8,128)(2,1)S(1)}, bf16[64,5120]{1,0:T(8,128)(2,1)S(1)}, u32[]{:S(2)}, u32[]{:S(2)}) collective-permute-start(bf16[64,5120]{1,0:T(8,128)(2,1)S(1)} %pad_maximum_fusion.1), channel_id=1, source_target_pairs={{0,2},{1,3},{2,0},{3,1},{4,6},{5,7},{6,4},{7,5},{8,10},{9,11},{10,... | collective-permute-start | bytes 1966088 | tf_op jit(solution)/shard_map/ppermute | solution.py:31
  186.9 16.4 %collective-permute-start.34 = (bf16[16,5120]{1,0:T(8,128)(2,1)S(1)}, bf16[16,5120]{1,0:T(8,128)(2,1)S(1)}, u32[]{:S(2)}, u32[]{:S(2)}) collective-permute-start(bf16[16,5120]{1,0:T(8,128)(2,1)S(1)} %get-tuple-element.66), channel_id=1, source_target_pairs={{0,24},{4,28},{8,16},{12,20},{16,8},{20,12},{24,0},{28,4},{1,25},{... | collective-permute-start | bytes 491528 | tf_op jit(solution)/shard_map/ppermute | solution.py:31
  189.5 18.8 %collective-permute-start.33 = (bf16[16,5120]{1,0:T(8,128)(2,1)S(1)}, bf16[16,5120]{1,0:T(8,128)(2,1)S(1)}, u32[]{:S(2)}, u32[]{:S(2)}) collective-permute-start(bf16[16,5120]{1,0:T(8,128)(2,1)S(1)} %get-tuple-element.67), channel_id=1, source_target_pairs={{0,16},{4,20},{8,24},{12,28},{16,0},{20,4},{24,8},{28,12},{1,17},{... | collective-permute-start | bytes 491528 | tf_op jit(solution)/shard_map/ppermute | solution.py:31
  (45 other events, 404.5 us)

commit v3 on v2

--- a/solution.py
+++ b/solution.py
@@ -43,11 +43,17 @@
     sent_pages_ref,
     leaf_keys_ref,
     leaf_values_ref,
+    proj_ref,
     out_ref,
     keys,
     values,
     mask,
+    heads_out,
+    proj,
+    proj_sem,
 ):
+    fetch = pltpu.make_async_copy(proj_ref, proj, proj_sem)
+    fetch.start()
     tokens = queries_ref.shape[0]
     page = own_pages_ref.shape[2]
     pages = own_pages_ref.shape[0]
@@ -94,11 +100,28 @@
         summed = jnp.dot(
             expo.astype(jnp.bfloat16), values[:, group], preferred_element_type=jnp.float32
         )
-        out_ref[:, head] = (summed / total).astype(jnp.bfloat16)
+        heads_out[:, head] = (summed / total).astype(jnp.bfloat16)
+    fetch.wait()
+    span = out_ref.shape[1] // 4
+    for n in range(4):
+        part = pl.ds(n * span, span)
+        out_ref[:, part] = jnp.dot(
+            heads_out[...], proj[:, part], preferred_element_type=jnp.float32
+        )
 
 
 def attend(
-    queries, places, query_segments, leaf_keys, leaf_values, fetched, segments, parents, roots, lengths
+    queries,
+    places,
+    query_segments,
+    leaf_keys,
+    leaf_values,
+    fetched,
+    segments,
+    parents,
+    roots,
+    lengths,
+    out_proj,
 ):
     is_local, entry, own_pages, sent_pages = fetched
     tokens, leaf_tokens = queries.shape[0], leaf_keys.shape[0]
@@ -116,18 +139,21 @@
     heads = queries.shape[1] // HEAD_SIZE
     return pl.pallas_call(
         attend_kernel,
-        in_specs=[scalars] * 2 + [whole] * 9,
+        in_specs=[scalars] * 2 + [whole] * 9 + [pl.BlockSpec(memory_space=pltpu.HBM)],
         out_specs=whole,
-        out_shape=jax.ShapeDtypeStruct(queries.shape, jnp.bfloat16),
+        out_shape=jax.ShapeDtypeStruct((tokens, out_proj.shape[1]), jnp.float32),
         scratch_shapes=[
             pltpu.VMEM((key_count, columns), jnp.bfloat16),
             pltpu.VMEM((key_count, columns), jnp.bfloat16),
             pltpu.VMEM((tokens, key_count), jnp.float32),
+            pltpu.VMEM(queries.shape, jnp.bfloat16),
+            pltpu.VMEM(out_proj.shape, jnp.bfloat16),
+            pltpu.SemaphoreType.DMA(()),
         ],
-        compiler_params=pltpu.CompilerParams(vmem_limit_bytes=20 * 1024 * 1024),
+        compiler_params=pltpu.CompilerParams(vmem_limit_bytes=28 * 1024 * 1024),
         cost_estimate=pl.CostEstimate(
-            flops=4 * tokens * heads * HEAD_SIZE * key_count,
-            bytes_accessed=8 * key_count * columns,
+            flops=4 * tokens * heads * HEAD_SIZE * key_count + 2 * tokens * out_proj.size,
+            bytes_accessed=8 * key_count * columns + 2 * out_proj.size,
             transcendentals=tokens * heads * key_count,
         ),
         name="attend",
@@ -143,6 +169,7 @@
         sent_pages,
         leaf_keys,
         leaf_values,
+        out_proj,
     )
 
 
@@ -252,70 +279,53 @@
     return blocks
 
 
-def feed_forward_kernel(
-    steps_in, x_ref, g0_ref, g1_ref, u0_ref, u1_ref, d0_ref, d1_ref, out_ref, acc, hidden
-):
-    step = pl.program_id(0)
-    wide = jnp.float32
-
-    @pl.when(step < steps_in)
-    def _():
-        x = x_ref[...]
-        parts = [
-            lax.dot_general(x, w[...], (((1,), (1,)), ((), ())), preferred_element_type=wide)
-            for w in (g0_ref, g1_ref, u0_ref, u1_ref)
-        ]
-
-        @pl.when(step == 0)
-        def _():
-            for n, part in enumerate(parts):
-                acc[n] = part
-
-        @pl.when(step > 0)
-        def _():
-            for n, part in enumerate(parts):
-                acc[n] += part
-
-    @pl.when(step == steps_in - 1)
-    def _():
-        for n in range(2):
-            gate = acc[n]
-            hidden[n] = (gate / (1.0 + jnp.exp(-gate)) * acc[2 + n]).astype(jnp.bfloat16)
-
-    @pl.when(step >= steps_in)
-    def _():
-        total = jnp.dot(hidden[0], d0_ref[...], preferred_element_type=wide)
-        total += jnp.dot(hidden[1], d1_ref[...], preferred_element_type=wide)
-        out_ref[...] = total.astype(jnp.bfloat16)
+def feed_forward_kernel(x_ref, g0, g1, u0, u1, d0, d1, out_ref, wide_rows, down_rows, hidden, sems):
+    sources = [g0, u0, g1, u1, d0, d1]
+    targets = [wide_rows.at[n] for n in range(4)] + [down_rows.at[n] for n in range(2)]
+    copies = [
+        pltpu.make_async_copy(source, target, sems.at[n])
+        for n, (source, target) in enumerate(zip(sources, targets))
+    ]
+    for copy in copies:
+        copy.start()
+    flip = (((1,), (1,)), ((), ()))
+    for n in range(2):
+        copies[2 * n].wait()
+        gate = lax.dot_general(
+            x_ref[...], wide_rows[2 * n], flip, preferred_element_type=jnp.float32
+        )
+        copies[2 * n + 1].wait()
+        upper = lax.dot_general(
+            x_ref[...], wide_rows[2 * n + 1], flip, preferred_element_type=jnp.float32
+        )
+        hidden[n] = (gate / (1.0 + jnp.exp(-gate)) * upper).astype(jnp.bfloat16)
+    copies[4].wait()
+    copies[5].wait()
+    span = out_ref.shape[1] // 4
+    for n in range(4):
+        part = pl.ds(n * span, span)
+        total = jnp.dot(hidden[0], down_rows[0, :, part], preferred_element_type=jnp.float32)
+        total += jnp.dot(hidden[1], down_rows[1, :, part], preferred_element_type=jnp.float32)
+        out_ref[:, part] = total.astype(jnp.bfloat16)
 
 
 def feed_forward(tokens, gates, uppers, downs):
     rows, width = tokens.shape
     units = gates[0].shape[0]
-    steps_in, steps_out = 4, 4
-    depth, span = width // steps_in, width // steps_out
-
-    def inner(i):
-        return jnp.minimum(i, steps_in - 1)
-
-    def outer(i):
-        return jnp.maximum(i - steps_in, 0)
-
-    weight = pl.BlockSpec((units, depth), lambda i: (0, inner(i)))
-    down = pl.BlockSpec((units, span), lambda i: (0, outer(i)))
+    far = pl.BlockSpec(memory_space=pltpu.HBM)
+    near = pl.BlockSpec(memory_space=pltpu.VMEM)
     return pl.pallas_call(
-        lambda *refs: feed_forward_kernel(steps_in, *refs),
-        grid=(steps_in + steps_out,),
-        in_specs=[pl.BlockSpec((rows, depth), lambda i: (0, inner(i)))]
-        + [weight] * 4
-        + [down] * 2,
-        out_specs=pl.BlockSpec((rows, span), lambda i: (0, outer(i))),
+        feed_forward_kernel,
+        in_specs=[near] + [far] * 6,
+        out_specs=near,
         out_shape=jax.ShapeDtypeStruct((rows, width), jnp.bfloat16),
         scratch_shapes=[
-            pltpu.VMEM((4, rows, units), jnp.float32),
+            pltpu.VMEM((4, units, width), jnp.bfloat16),
+            pltpu.VMEM((2, units, width), jnp.bfloat16),
             pltpu.VMEM((2, rows, units), jnp.bfloat16),
+            pltpu.SemaphoreType.DMA((6,)),
         ],
-        compiler_params=pltpu.CompilerParams(vmem_limit_bytes=24 * 1024 * 1024),
+        compiler_params=pltpu.CompilerParams(vmem_limit_bytes=40 * 1024 * 1024),
         cost_estimate=pl.CostEstimate(
             flops=12 * rows * width * units,
             bytes_accessed=12 * width * units + 4 * rows * width,
@@ -367,7 +377,7 @@
     asked, fetched, gates, uppers, downs = lax.optimization_barrier(
         (picked(queries), fetched, gates, uppers, downs)
     )
-    attention = attend(
+    projected = attend(
         asked,
         places,
         picked(segment_ids),
@@ -378,8 +388,8 @@
         req_parent[0],
         mid_parent[0],
         node_len[0],
-    )
-    projected = jnp.dot(attention, out_proj, preferred_element_type=jnp.float32)
+        out_proj,
+    )
     span = members * rows
     evens = [sum_cores(projected[c * span : (c + 1) * span], rows) for c in range(CHUNKS)]
     streams, mixed = [], []

time: 233 us -> 220 us (0.944)
  matrix products: 16.3 us -> 9.71 us
  Pallas kernels: 35.1 us -> 31.1 us
  other arithmetic: 11.8 us -> 8.15 us
  local copies, waits for them, and re-layouts: 26.4 us -> 28.8 us
    dot_general x1 -> x0, matrix products: 6.6 us -> none  [body(): projected = jnp.dot(attention, out_proj, preferred_element_type=jnp.float32)]
    pallas_call x3, Pallas kernels: 35.1 us -> 31.1 us  [the longest x2 22.3 us: feed_forward(): pl.pallas_call(feed_forward_kernel, in_specs=[near] + [far] * 6, out_spec...]
    unnamed x77 -> x49, local copies, waits for them, and re-layouts: 12 us -> 13.6 us
  transfers between devices with their start and end apart: 40 -> 40, of which waited for: 19 -> 19; matrix products, arithmetic and copies ran while one was open for 12% -> 13% of each run, Pallas kernels for 12% -> 10%
where the time goes in v3:
time: 220 us; the launch traced here: 219 us
  waiting for transfers between devices  83 us (38%)
  starting transfers between devices  57.2 us (26%)
  Pallas kernels  31.1 us (14%)
  local copies, waits for them, and re-layouts  28.8 us (13%)
  matrix products  9.71 us (4%)
  other arithmetic  8.15 us (4%)
    ppermute x39, waiting for transfers between devices, swap(): lax.ppermute(array, axis, [(i, i ^ step) for i in range(lax.axis_size(axi...  71.5 us
    ppermute x39, starting transfers between devices, swap(): lax.ppermute(array, axis, [(i, i ^ step) for i in range(lax.axis_size(axi...  50.1 us
    pallas_call x2, Pallas kernels, feed_forward(): pl.pallas_call(feed_forward_kernel, in_specs=[near] + [far] * 6, out_spec...  22.3 us
    unnamed x49, local copies, waits for them, and re-layouts  13.6 us
    all_to_all x1, waiting for transfers between devices, fetch_prefix(): lax.all_to_all(outgoing, 'req', split_axis=0, concat_axis=0, tiled=True)  11.5 us
    dot_general x1, matrix products, body(): jnp.dot(next_normed, qkv_proj, preferred_element_type=jnp.float32)  9.71 us
    pallas_call x1, Pallas kernels, attend(): pl.pallas_call(attend_kernel, in_specs=[scalars] * 2 + [whole] * 9 + [pl....  8.84 us
    gather x2, local copies, waits for them, and re-layouts, fetch_prefix(): local = jnp.swapaxes(key_value_pages[own_slots], 1, 2)  7.73 us
  transfers between devices with their start and end apart: 40, of which 19 were waited for; matrix products, arithmetic and copies ran while one was open for 13% of the time, Pallas kernels for 10%

profile of v3, /device:TPU:0, one launch (start us, length us, event | category | flops | bytes accessed | tf_op | source)
XLA Modules:
  0.0 219.3 jit_solution(14429781992259307152)
XLA Ops:
  4.7 2.7 %gather_fusion.1 = bf16[16,64,2,256]{3,2,1,0:T(2,128)(2,1)S(1)} fusion(bf16[32,64,2,256]{3,2,1,0:T(2,128)(2,1)S(1)} %copy-done, s32[1024]{0:T(1024)S(1)} %get-tuple-element.80), kind=kCustom, calls=%fused_computation.1 | custom fusion | bytes 2097216 | tf_op jit(solution)/shard_map/gather | solution.py:189
  8.6 7.0 %all-to-all-start = ((bf16[16,2,64,256]{3,2,1,0:T(8,128)(2,1)}), bf16[16,2,64,256]{3,2,1,0:T(8,128)(2,1)S(1)}, u32[]{:S(2)}, u32[]{:S(2)}) async-start(bf16[16,2,64,256]{3,2,1,0:T(8,128)(2,1)} %bitcast.40), calls=%async_computation | async-start | bytes 2097152 | tf_op jit(solution)/shard_map/all_to_all | solution.py:190
  16.8 6.0 %gather_fusion = bf16[24,64,2,256]{3,2,1,0:T(2,128)(2,1)} fusion(bf16[32,64,2,256]{3,2,1,0:T(2,128)(2,1)S(1)} %copy-done, s32[1024]{0:T(1024)S(1)} %get-tuple-element.81), kind=kCustom, calls=%fused_computation | custom fusion | bytes 3145824 | tf_op jit(solution)/shard_map/gather | solution.py:195
  30.5 11.5 %all-to-all-done.sent_pages_ref = bf16[16,2,64,256]{3,2,1,0:T(8,128)(2,1)S(1)} async-done(((bf16[16,2,64,256]{3,2,1,0:T(8,128)(2,1)}), bf16[16,2,64,256]{3,2,1,0:T(8,128)(2,1)S(1)}, u32[]{:S(2)}, u32[]{:S(2)}) %all-to-all-start) | async-done | bytes 1048608 | tf_op jit(solution)/shard_map/all_to_all | solution.py:190
  42.0 4.7 %copy-done.2 = bf16[1280,5120]{1,0:T(8,128)(2,1)S(1)} copy-done((bf16[1280,5120]{1,0:T(8,128)(2,1)S(1)}, bf16[1280,5120]{1,0:T(8,128)(2,1)}, u32[]{:S(2)}) %copy-start.2) | copy-done | bytes 13107224
  46.7 8.8 %attend.1 = f32[128,5120]{1,0:T(8,128)S(1)} custom-call(s32[24]{0:T(128)S(1)} %fusion.26.local_ref, s32[24]{0:T(128)S(1)} %fusion.32.entry_ref, bf16[128,1280]{1,0:T(8,128)(2,1)S(1)} %constant_dynamic-update-slice_fusion.queries_ref, s32[128,6]{1,0:T(8,128)S(1)} %fusion.24.limits_ref, s32[128,1]{1,0:T(8,128)S(1)} %copy.56.query_segments_ref, ...), custom_call_target="tpu_custom_call" | custom-call | flops 2768240640 | bytes 16515072 | tf_op jit(solution)/shard_map/attend/pallas_call | solution.py:140
  60.0 4.8 %collective-permute-done.4 = bf16[16,5120]{1,0:T(8,128)(2,1)S(1)} collective-permute-done((bf16[16,5120]{1,0:T(8,128)(2,1)S(1)}, bf16[16,5120]{1,0:T(8,128)(2,1)S(1)}, u32[]{:S(2)}, u32[]{:S(2)}) %collective-permute-start.4) | collective-permute-done | bytes 163872 | tf_op jit(solution)/shard_map/ppermute | solution.py:31
  64.8 2.7 %collective-permute-done.20 = bf16[16,5120]{1,0:T(8,128)(2,1)S(1)} collective-permute-done((bf16[16,5120]{1,0:T(8,128)(2,1)S(1)}, bf16[16,5120]{1,0:T(8,128)(2,1)S(1)}, u32[]{:S(2)}, u32[]{:S(2)}) %collective-permute-start.20) | collective-permute-done | bytes 163872 | tf_op jit(solution)/shard_map/ppermute | solution.py:31
  69.7 2.7 %collective-permute-start.22 = (bf16[16,5120]{1,0:T(8,128)(2,1)S(1)}, bf16[16,5120]{1,0:T(8,128)(2,1)}, u32[]{:S(2)}, u32[]{:S(2)}) collective-permute-start(bf16[16,5120]{1,0:T(8,128)(2,1)S(1)} %get-tuple-element.71), channel_id=1, source_target_pairs={{0,16},{4,20},{8,24},{12,28},{16,0},{20,4},{24,8},{28,12},{1,17},{... | collective-permute-start | bytes 491528 | tf_op jit(solution)/shard_map/ppermute | solution.py:31
  74.1 2.7 %collective-permute-start.6 = (bf16[16,5120]{1,0:T(8,128)(2,1)S(1)}, bf16[16,5120]{1,0:T(8,128)(2,1)S(1)}, u32[]{:S(2)}, u32[]{:S(2)}) collective-permute-start(bf16[16,5120]{1,0:T(8,128)(2,1)S(1)} %get-tuple-element.31), channel_id=1, source_target_pairs={{0,16},{4,20},{8,24},{12,28},{16,0},{20,4},{24,8},{28,12},{1,17},{... | collective-permute-start | bytes 491528 | tf_op jit(solution)/shard_map/ppermute | solution.py:31
  76.8 2.9 %collective-permute-done.21 = bf16[16,5120]{1,0:T(8,128)(2,1)} collective-permute-done((bf16[16,5120]{1,0:T(8,128)(2,1)S(1)}, bf16[16,5120]{1,0:T(8,128)(2,1)}, u32[]{:S(2)}, u32[]{:S(2)}) %collective-permute-start.21) | collective-permute-done | bytes 163872 | tf_op jit(solution)/shard_map/ppermute | solution.py:31
  82.0 2.9 %collective-permute-done.22 = bf16[16,5120]{1,0:T(8,128)(2,1)} collective-permute-done((bf16[16,5120]{1,0:T(8,128)(2,1)S(1)}, bf16[16,5120]{1,0:T(8,128)(2,1)}, u32[]{:S(2)}, u32[]{:S(2)}) %collective-permute-start.22) | collective-permute-done | bytes 163872 | tf_op jit(solution)/shard_map/ppermute | solution.py:31
  89.1 9.7 %collective-permute-done.6 = bf16[16,5120]{1,0:T(8,128)(2,1)S(1)} collective-permute-done((bf16[16,5120]{1,0:T(8,128)(2,1)S(1)}, bf16[16,5120]{1,0:T(8,128)(2,1)S(1)}, u32[]{:S(2)}, u32[]{:S(2)}) %collective-permute-start.6) | collective-permute-done | bytes 163872 | tf_op jit(solution)/shard_map/ppermute | solution.py:31
  106.0 12.0 %collective-permute-done.9 = bf16[64,5120]{1,0:T(8,128)(2,1)S(1)} collective-permute-done((bf16[64,5120]{1,0:T(8,128)(2,1)S(1)}, bf16[64,5120]{1,0:T(8,128)(2,1)S(1)}, u32[]{:S(2)}, u32[]{:S(2)}) %collective-permute-start.9) | collective-permute-done | bytes 655392 | tf_op jit(solution)/shard_map/ppermute | solution.py:31
  120.2 3.4 %collective-permute-done.26 = bf16[32,5120]{1,0:T(8,128)(2,1)S(1)} collective-permute-done((bf16[32,5120]{1,0:T(8,128)(2,1)S(1)}, bf16[32,5120]{1,0:T(8,128)(2,1)S(1)}, u32[]{:S(2)}, u32[]{:S(2)}) %collective-permute-start.26) | collective-permute-done | bytes 327712 | tf_op jit(solution)/shard_map/ppermute | solution.py:31
  125.0 11.1 %feed_forward.3 = bf16[256,5120]{1,0:T(8,128)(2,1)S(1)} custom-call(bf16[256,5120]{1,0:T(8,128)(2,1)S(1)} %constant_dynamic-update-slice_fusion.16.x_ref, bf16[432,5120]{1,0:T(8,128)(2,1)S(1)} %bitcast.33, bf16[432,5120]{1,0:T(8,128)(2,1)} %collective-permute-done.g1, bf16[432,5120]{1,0:T(8,128)(2,1)} %bitcast.38, ...), custom_call_target="tpu_custom_call" | custom-call | flops 6794772480 | bytes 31784960 | tf_op jit(solution)/shard_map/feed_forward/pallas_call | solution.py:317
  137.9 11.2 %feed_forward.2 = bf16[256,5120]{1,0:T(8,128)(2,1)S(1)} custom-call(bf16[256,5120]{1,0:T(8,128)(2,1)S(1)} %constant_dynamic-update-slice_fusion.8.x_ref, bf16[432,5120]{1,0:T(8,128)(2,1)S(1)} %bitcast.34, bf16[432,5120]{1,0:T(8,128)(2,1)} %collective-permute-done.g1, bf16[432,5120]{1,0:T(8,128)(2,1)} %bitcast.39, ...), custom_call_target="tpu_custom_call" | custom-call | flops 6794772480 | bytes 31784960 | tf_op jit(solution)/shard_map/feed_forward/pallas_call | solution.py:317
  153.6 6.2 %collective-permute-done.12 = bf16[32,5120]{1,0:T(8,128)(2,1)S(1)} collective-permute-done((bf16[32,5120]{1,0:T(8,128)(2,1)S(1)}, bf16[32,5120]{1,0:T(8,128)(2,1)S(1)}, u32[]{:S(2)}, u32[]{:S(2)}) %collective-permute-start.12) | collective-permute-done | bytes 327712 | tf_op jit(solution)/shard_map/ppermute | solution.py:31
  163.7 8.3 %collective-permute-done.31 = bf16[64,5120]{1,0:T(8,128)(2,1)S(1)} collective-permute-done((bf16[64,5120]{1,0:T(8,128)(2,1)S(1)}, bf16[64,5120]{1,0:T(8,128)(2,1)S(1)}, u32[]{:S(2)}, u32[]{:S(2)}) %collective-permute-start.31) | collective-permute-done | bytes 655392 | tf_op jit(solution)/shard_map/ppermute | solution.py:31
  175.1 8.2 %collective-permute-start.33 = (bf16[16,5120]{1,0:T(8,128)(2,1)S(1)}, bf16[16,5120]{1,0:T(8,128)(2,1)S(1)}, u32[]{:S(2)}, u32[]{:S(2)}) collective-permute-start(bf16[16,5120]{1,0:T(8,128)(2,1)S(1)} %get-tuple-element.67), channel_id=1, source_target_pairs={{0,16},{4,20},{8,24},{12,28},{16,0},{20,4},{24,8},{28,12},{1,17},{... | collective-permute-start | bytes 491528 | tf_op jit(solution)/shard_map/ppermute | solution.py:31
  185.4 4.9 %collective-permute-start.17 = (bf16[16,5120]{1,0:T(8,128)(2,1)S(1)}, bf16[16,5120]{1,0:T(8,128)(2,1)S(1)}, u32[]{:S(2)}, u32[]{:S(2)}) collective-permute-start(bf16[16,5120]{1,0:T(8,128)(2,1)S(1)} %get-tuple-element.64), channel_id=1, source_target_pairs={{0,16},{4,20},{8,24},{12,28},{16,0},{20,4},{24,8},{28,12},{1,17},{... | collective-permute-start | bytes 491528 | tf_op jit(solution)/shard_map/ppermute | solution.py:31
  190.7 5.2 %collective-permute-done.33 = bf16[16,5120]{1,0:T(8,128)(2,1)S(1)} collective-permute-done((bf16[16,5120]{1,0:T(8,128)(2,1)S(1)}, bf16[16,5120]{1,0:T(8,128)(2,1)S(1)}, u32[]{:S(2)}, u32[]{:S(2)}) %collective-permute-start.33) | collective-permute-done | bytes 163872 | tf_op jit(solution)/shard_map/ppermute | solution.py:31
  196.1 3.2 %collective-permute-done.17 = bf16[16,5120]{1,0:T(8,128)(2,1)S(1)} collective-permute-done((bf16[16,5120]{1,0:T(8,128)(2,1)S(1)}, bf16[16,5120]{1,0:T(8,128)(2,1)S(1)}, u32[]{:S(2)}, u32[]{:S(2)}) %collective-permute-start.17) | collective-permute-done | bytes 163872 | tf_op jit(solution)/shard_map/ppermute | solution.py:31
  209.5 9.7 %fusion = bf16[128,1792]{1,0:T(8,128)(2,1)} fusion(bf16[128,5120]{1,0:T(8,128)(2,1)S(1)} %select_dynamic-update-slice_fusion, bf16[5120,1792]{1,0:T(8,128)(2,1)} %param.36, f32[1792]{0:T(1024)S(1)} %copy-done.9), kind=kOutput, calls=%fused_computation.3 | convolution fusion | flops 2349268992 | bytes 20126720 | tf_op jit(solution)/shard_map/dot_general | solution.py:414
  (192 shorter events, 65.4 us)
Async XLA Ops:
  0.6 41.3 %collective-permute-start = (bf16[432,5120]{1,0:T(8,128)(2,1)}, bf16[432,5120]{1,0:T(8,128)(2,1)}, u32[]{:S(2)}, u32[]{:S(2)}) collective-permute-start(bf16[432,5120]{1,0:T(8,128)(2,1)} %bitcast.30), channel_id=1, source_target_pairs={{0,1},{1,0},{2,3},{3,2},{4,5},{5,4},{6,7},{7,6},{8,9},{9,8},{10,11... | collective-permute-start | bytes 13271048 | tf_op jit(solution)/shard_map/ppermute | solution.py:31
  1.2 40.8 %collective-permute-start.1 = (bf16[432,5120]{1,0:T(8,128)(2,1)}, bf16[432,5120]{1,0:T(8,128)(2,1)}, u32[]{:S(2)}, u32[]{:S(2)}) collective-permute-start(bf16[432,5120]{1,0:T(8,128)(2,1)} %bitcast.37), channel_id=1, source_target_pairs={{0,1},{1,0},{2,3},{3,2},{4,5},{5,4},{6,7},{7,6},{8,9},{9,8},{10,11... | collective-permute-start | bytes 13271048 | tf_op jit(solution)/shard_map/ppermute | solution.py:31
  1.2 40.7 %collective-permute-start.2 = (bf16[432,5120]{1,0:T(8,128)(2,1)}, bf16[432,5120]{1,0:T(8,128)(2,1)}, u32[]{:S(2)}, u32[]{:S(2)}) collective-permute-start(bf16[432,5120]{1,0:T(8,128)(2,1)} %d0.1), channel_id=1, source_target_pairs={{0,1},{1,0},{2,3},{3,2},{4,5},{5,4},{6,7},{7,6},{8,9},{9,8},{10,11... | collective-permute-start | bytes 13271048 | tf_op jit(solution)/shard_map/ppermute | solution.py:31
  8.6 33.4 %all-to-all-start = ((bf16[16,2,64,256]{3,2,1,0:T(8,128)(2,1)}), bf16[16,2,64,256]{3,2,1,0:T(8,128)(2,1)S(1)}, u32[]{:S(2)}, u32[]{:S(2)}) async-start(bf16[16,2,64,256]{3,2,1,0:T(8,128)(2,1)} %bitcast.40), calls=%async_computation | async-start | bytes 2097152 | tf_op jit(solution)/shard_map/all_to_all | solution.py:190
  69.7 15.2 %collective-permute-start.22 = (bf16[16,5120]{1,0:T(8,128)(2,1)S(1)}, bf16[16,5120]{1,0:T(8,128)(2,1)}, u32[]{:S(2)}, u32[]{:S(2)}) collective-permute-start(bf16[16,5120]{1,0:T(8,128)(2,1)S(1)} %get-tuple-element.71), channel_id=1, source_target_pairs={{0,16},{4,20},{8,24},{12,28},{16,0},{20,4},{24,8},{28,12},{1,17},{... | collective-permute-start | bytes 491528 | tf_op jit(solution)/shard_map/ppermute | solution.py:31
  74.1 15.0 %collective-permute-start.5 = (bf16[16,5120]{1,0:T(8,128)(2,1)S(1)}, bf16[16,5120]{1,0:T(8,128)(2,1)S(1)}, u32[]{:S(2)}, u32[]{:S(2)}) collective-permute-start(bf16[16,5120]{1,0:T(8,128)(2,1)S(1)} %get-tuple-element.31), channel_id=1, source_target_pairs={{0,8},{4,12},{8,0},{12,4},{16,24},{20,28},{24,16},{28,20},{1,9},{5... | collective-permute-start | bytes 491528 | tf_op jit(solution)/shard_map/ppermute | solution.py:31
  74.1 24.7 %collective-permute-start.6 = (bf16[16,5120]{1,0:T(8,128)(2,1)S(1)}, bf16[16,5120]{1,0:T(8,128)(2,1)S(1)}, u32[]{:S(2)}, u32[]{:S(2)}) collective-permute-start(bf16[16,5120]{1,0:T(8,128)(2,1)S(1)} %get-tuple-element.31), channel_id=1, source_target_pairs={{0,16},{4,20},{8,24},{12,28},{16,0},{20,4},{24,8},{28,12},{1,17},{... | collective-permute-start | bytes 491528 | tf_op jit(solution)/shard_map/ppermute | solution.py:31
  79.7 19.1 %collective-permute-start.7 = (bf16[16,5120]{1,0:T(8,128)(2,1)S(1)}, bf16[16,5120]{1,0:T(8,128)(2,1)S(1)}, u32[]{:S(2)}, u32[]{:S(2)}) collective-permute-start(bf16[16,5120]{1,0:T(8,128)(2,1)S(1)} %get-tuple-element.31), channel_id=1, source_target_pairs={{0,24},{4,28},{8,16},{12,20},{16,8},{20,12},{24,0},{28,4},{1,25},{... | collective-permute-start | bytes 491528 | tf_op jit(solution)/shard_map/ppermute | solution.py:31
  86.0 19.1 %collective-permute-start.24 = (bf16[64,5120]{1,0:T(8,128)(2,1)S(1)}, bf16[64,5120]{1,0:T(8,128)(2,1)S(1)}, u32[]{:S(2)}, u32[]{:S(2)}) collective-permute-start(bf16[64,5120]{1,0:T(8,128)(2,1)S(1)} %pad_maximum_fusion.3), channel_id=1, source_target_pairs={{0,2},{1,3},{2,0},{3,1},{4,6},{5,7},{6,4},{7,5},{8,10},{9,11},{10,... | collective-permute-start | bytes 1966088 | tf_op jit(solution)/shard_map/ppermute | solution.py:31
  87.5 16.9 %collective-permute-start.25 = (bf16[64,5120]{1,0:T(8,128)(2,1)S(1)}, bf16[64,5120]{1,0:T(8,128)(2,1)S(1)}, u32[]{:S(2)}, u32[]{:S(2)}) collective-permute-start(bf16[64,5120]{1,0:T(8,128)(2,1)S(1)} %pad_maximum_fusion.3), channel_id=1, source_target_pairs={{0,4},{4,0},{8,12},{12,8},{16,20},{20,16},{24,28},{28,24},{1,5},{5... | collective-permute-start | bytes 1966088 | tf_op jit(solution)/shard_map/ppermute | solution.py:31
  98.8 19.9 %collective-permute-start.8 = (bf16[64,5120]{1,0:T(8,128)(2,1)S(1)}, bf16[64,5120]{1,0:T(8,128)(2,1)S(1)}, u32[]{:S(2)}, u32[]{:S(2)}) collective-permute-start(bf16[64,5120]{1,0:T(8,128)(2,1)S(1)} %pad_maximum_fusion), channel_id=1, source_target_pairs={{0,2},{1,3},{2,0},{3,1},{4,6},{5,7},{6,4},{7,5},{8,10},{9,11},{10,... | collective-permute-start | bytes 1966088 | tf_op jit(solution)/shard_map/ppermute | solution.py:31
  100.3 17.7 %collective-permute-start.9 = (bf16[64,5120]{1,0:T(8,128)(2,1)S(1)}, bf16[64,5120]{1,0:T(8,128)(2,1)S(1)}, u32[]{:S(2)}, u32[]{:S(2)}) collective-permute-start(bf16[64,5120]{1,0:T(8,128)(2,1)S(1)} %pad_maximum_fusion), channel_id=1, source_target_pairs={{0,4},{4,0},{8,12},{12,8},{16,20},{20,16},{24,28},{28,24},{1,5},{5... | collective-permute-start | bytes 1966088 | tf_op jit(solution)/shard_map/ppermute | solution.py:31
  104.5 19.0 %collective-permute-start.26 = (bf16[32,5120]{1,0:T(8,128)(2,1)S(1)}, bf16[32,5120]{1,0:T(8,128)(2,1)S(1)}, u32[]{:S(2)}, u32[]{:S(2)}) collective-permute-start(bf16[32,5120]{1,0:T(8,128)(2,1)S(1)} %slice.257), channel_id=1, source_target_pairs={{0,2},{1,3},{2,0},{3,1},{4,6},{5,7},{6,4},{7,5},{8,10},{9,11},{10,... | collective-permute-start | bytes 983048 | tf_op jit(solution)/shard_map/ppermute | solution.py:31
  105.1 19.8 %collective-permute-start.27 = (bf16[32,5120]{1,0:T(8,128)(2,1)S(1)}, bf16[32,5120]{1,0:T(8,128)(2,1)S(1)}, u32[]{:S(2)}, u32[]{:S(2)}) collective-permute-start(bf16[32,5120]{1,0:T(8,128)(2,1)S(1)} %slice.258), channel_id=1, source_target_pairs={{0,4},{4,0},{8,12},{12,8},{16,20},{20,16},{24,28},{28,24},{1,5},{5... | collective-permute-start | bytes 983048 | tf_op jit(solution)/shard_map/ppermute | solution.py:31
  118.0 19.8 %collective-permute-start.10 = (bf16[32,5120]{1,0:T(8,128)(2,1)S(1)}, bf16[32,5120]{1,0:T(8,128)(2,1)S(1)}, u32[]{:S(2)}, u32[]{:S(2)}) collective-permute-start(bf16[32,5120]{1,0:T(8,128)(2,1)S(1)} %slice.238), channel_id=1, source_target_pairs={{0,2},{1,3},{2,0},{3,1},{4,6},{5,7},{6,4},{7,5},{8,10},{9,11},{10,... | collective-permute-start | bytes 983048 | tf_op jit(solution)/shard_map/ppermute | solution.py:31
  118.7 19.1 %collective-permute-start.11 = (bf16[32,5120]{1,0:T(8,128)(2,1)S(1)}, bf16[32,5120]{1,0:T(8,128)(2,1)S(1)}, u32[]{:S(2)}, u32[]{:S(2)}) collective-permute-start(bf16[32,5120]{1,0:T(8,128)(2,1)S(1)} %slice.239), channel_id=1, source_target_pairs={{0,4},{4,0},{8,12},{12,8},{16,20},{20,16},{24,28},{28,24},{1,5},{5... | collective-permute-start | bytes 983048 | tf_op jit(solution)/shard_map/ppermute | solution.py:31
  136.2 15.5 %collective-permute-start.28 = (bf16[32,5120]{1,0:T(8,128)(2,1)S(1)}, bf16[32,5120]{1,0:T(8,128)(2,1)S(1)}, u32[]{:S(2)}, u32[]{:S(2)}) collective-permute-start(bf16[32,5120]{1,0:T(8,128)(2,1)S(1)} %get-tuple-element.53), channel_id=1, source_target_pairs={{0,4},{4,0},{8,12},{12,8},{16,20},{20,16},{24,28},{28,24},{1,5},{5... | collective-permute-start | bytes 983048 | tf_op jit(solution)/shard_map/ppermute | solution.py:31
  137.2 14.5 %collective-permute-start.30 = (bf16[32,5120]{1,0:T(8,128)(2,1)S(1)}, bf16[32,5120]{1,0:T(8,128)(2,1)S(1)}, u32[]{:S(2)}, u32[]{:S(2)}) collective-permute-start(bf16[32,5120]{1,0:T(8,128)(2,1)S(1)} %get-tuple-element.52), channel_id=1, source_target_pairs={{0,2},{1,3},{2,0},{3,1},{4,6},{5,7},{6,4},{7,5},{8,10},{9,11},{10,... | collective-permute-start | bytes 983048 | tf_op jit(solution)/shard_map/ppermute | solution.py:31
  151.9 20.1 %collective-permute-start.31 = (bf16[64,5120]{1,0:T(8,128)(2,1)S(1)}, bf16[64,5120]{1,0:T(8,128)(2,1)S(1)}, u32[]{:S(2)}, u32[]{:S(2)}) collective-permute-start(bf16[64,5120]{1,0:T(8,128)(2,1)S(1)} %pad_maximum_fusion.5), channel_id=1, source_target_pairs={{0,4},{4,0},{8,12},{12,8},{16,20},{20,16},{24,28},{28,24},{1,5},{5... | collective-permute-start | bytes 1966088 | tf_op jit(solution)/shard_map/ppermute | solution.py:31
  153.0 20.1 %collective-permute-start.29 = (bf16[64,5120]{1,0:T(8,128)(2,1)S(1)}, bf16[64,5120]{1,0:T(8,128)(2,1)S(1)}, u32[]{:S(2)}, u32[]{:S(2)}) collective-permute-start(bf16[64,5120]{1,0:T(8,128)(2,1)S(1)} %pad_maximum_fusion.4), channel_id=1, source_target_pairs={{0,2},{1,3},{2,0},{3,1},{4,6},{5,7},{6,4},{7,5},{8,10},{9,11},{10,... | collective-permute-start | bytes 1966088 | tf_op jit(solution)/shard_map/ppermute | solution.py:31
  161.1 22.2 %collective-permute-start.15 = (bf16[64,5120]{1,0:T(8,128)(2,1)S(1)}, bf16[64,5120]{1,0:T(8,128)(2,1)S(1)}, u32[]{:S(2)}, u32[]{:S(2)}) collective-permute-start(bf16[64,5120]{1,0:T(8,128)(2,1)S(1)} %pad_maximum_fusion.2), channel_id=1, source_target_pairs={{0,4},{4,0},{8,12},{12,8},{16,20},{20,16},{24,28},{28,24},{1,5},{5... | collective-permute-start | bytes 1966088 | tf_op jit(solution)/shard_map/ppermute | solution.py:31
  162.2 21.1 %collective-permute-start.13 = (bf16[64,5120]{1,0:T(8,128)(2,1)S(1)}, bf16[64,5120]{1,0:T(8,128)(2,1)S(1)}, u32[]{:S(2)}, u32[]{:S(2)}) collective-permute-start(bf16[64,5120]{1,0:T(8,128)(2,1)S(1)} %pad_maximum_fusion.1), channel_id=1, source_target_pairs={{0,2},{1,3},{2,0},{3,1},{4,6},{5,7},{6,4},{7,5},{8,10},{9,11},{10,... | collective-permute-start | bytes 1966088 | tf_op jit(solution)/shard_map/ppermute | solution.py:31
  173.4 16.9 %collective-permute-start.34 = (bf16[16,5120]{1,0:T(8,128)(2,1)S(1)}, bf16[16,5120]{1,0:T(8,128)(2,1)S(1)}, u32[]{:S(2)}, u32[]{:S(2)}) collective-permute-start(bf16[16,5120]{1,0:T(8,128)(2,1)S(1)} %get-tuple-element.66), channel_id=1, source_target_pairs={{0,24},{4,28},{8,16},{12,20},{16,8},{20,12},{24,0},{28,4},{1,25},{... | collective-permute-start | bytes 491528 | tf_op jit(solution)/shard_map/ppermute | solution.py:31
  175.1 20.8 %collective-permute-start.33 = (bf16[16,5120]{1,0:T(8,128)(2,1)S(1)}, bf16[16,5120]{1,0:T(8,128)(2,1)S(1)}, u32[]{:S(2)}, u32[]{:S(2)}) collective-permute-start(bf16[16,5120]{1,0:T(8,128)(2,1)S(1)} %get-tuple-element.67), channel_id=1, source_target_pairs={{0,16},{4,20},{8,24},{12,28},{16,0},{20,4},{24,8},{28,12},{1,17},{... | collective-permute-start | bytes 491528 | tf_op jit(solution)/shard_map/ppermute | solution.py:31
  (31 other events, 342.9 us)

commit v4 on v3

--- a/solution.py
+++ b/solution.py
@@ -150,7 +150,7 @@
             pltpu.VMEM(out_proj.shape, jnp.bfloat16),
             pltpu.SemaphoreType.DMA(()),
         ],
-        compiler_params=pltpu.CompilerParams(vmem_limit_bytes=28 * 1024 * 1024),
+        compiler_params=pltpu.CompilerParams(vmem_limit_bytes=51 * 1024 * 1024),
         cost_estimate=pl.CostEstimate(
             flops=4 * tokens * heads * HEAD_SIZE * key_count + 2 * tokens * out_proj.size,
             bytes_accessed=8 * key_count * columns + 2 * out_proj.size,
@@ -231,15 +231,17 @@
             by_y[l] = jnp.concatenate([by_y[l][:half] + first, by_y[l][half:]], 0)
             by_x[k] = jnp.concatenate([by_x[k][:half], by_x[k][half:] + second], 0)
             at += 1
+    by_x = {k: part.astype(jnp.bfloat16) for k, part in by_x.items()}
+    by_y = {l: part.astype(jnp.bfloat16) for l, part in by_y.items()}
     for k in range(1, across):
-        column = column + swap(by_x[k].astype(jnp.bfloat16), "mlp", 2 * k).astype(wide)
+        column = column + swap(by_x[k], "mlp", 2 * k).astype(wide)
     for l in range(1, inner):
-        column = column + swap(by_y[l].astype(jnp.bfloat16), "req", l).astype(wide)
+        column = column + swap(by_y[l], "req", l).astype(wide)
     total = column[:rows]
     for k in range(1, OUTER):
         part = column[k * rows : (k + 1) * rows].astype(jnp.bfloat16)
         total = total + swap(part, "req", k * inner).astype(wide)
-    return total
+    return total, (by_x, by_y)
 
 
 def sum_cores(projected, rows):
@@ -333,6 +335,27 @@
         ),
         name="feed_forward",
     )(tokens, *gates, *uppers, *downs)
+
+
+def hold_kernel(source_ref, out_ref, sem):
+    copy = pltpu.make_async_copy(source_ref, out_ref, sem)
+    copy.start()
+    copy.wait()
+
+
+def hold(array):
+    return pl.pallas_call(
+        hold_kernel,
+        in_specs=[pl.BlockSpec(memory_space=pltpu.HBM)],
+        out_specs=pl.BlockSpec(memory_space=pltpu.VMEM),
+        out_shape=pltpu.VMEM(array.shape, array.dtype),
+        scratch_shapes=[pltpu.SemaphoreType.DMA(())],
+        compiler_params=pltpu.CompilerParams(vmem_limit_bytes=2 * 1024 * 1024),
+        cost_estimate=pl.CostEstimate(
+            flops=0, bytes_accessed=4 * array.size, transcendentals=0
+        ),
+        name="hold",
+    )(array)
 
 
 def body(
@@ -400,18 +423,20 @@
     for chunk in range(CHUNKS):
         tokens = gather_tokens(rms_norm(streams[chunk], norm_gain))
         mixed.append(feed_forward(tokens, gates, uppers, downs))
-    layer_rows, next_rows = [], []
+    layer_rows, next_rows, sent = [], [], []
     for chunk in range(CHUNKS):
-        summed = scatter_sum(mixed[chunk], rows)
+        summed, sides = scatter_sum(mixed[chunk], rows)
+        sent.append(sides)
         layer = (streams[chunk].astype(jnp.float32) + summed).astype(jnp.bfloat16)
         layer_rows.append(layer)
         next_rows.append(gather_heads(rms_norm(layer, next_gain)))
     layer_out = jnp.concatenate(layer_rows, 0)
+    held = hold(lax.optimization_barrier((qkv_proj, sent))[0])
     next_normed = jnp.concatenate(
         [next_rows[c][j] for j in range(members) for c in range(CHUNKS)], 0
     )
     qkv_out = (
-        jnp.dot(next_normed, qkv_proj, preferred_element_type=jnp.float32) + qkv_bias
+        jnp.dot(next_normed, held, preferred_element_type=jnp.float32) + qkv_bias
     ).astype(jnp.bfloat16)
     return (layer_out, qkv_out)
 

time: 220 us -> 212 us (0.964)
  matrix products: 9.71 us -> 3.45 us
  waiting for transfers between devices: 83 us -> 79.2 us
  Pallas kernels: 31.1 us -> 34.2 us
    ppermute x39, waiting for transfers between devices: 71.5 us -> 63.5 us  [swap(): lax.ppermute(array, axis, [(i, i ^ step) for i in range(lax.axis_size(axi...]
    dot_general x1, matrix products: 9.71 us -> 3.45 us  [body(): jnp.dot(next_normed, held, preferred_element_type=jnp.float32) + qkv_bias]
    all_to_all x1, waiting for transfers between devices: 11.5 us -> 15.6 us  [fetch_prefix(): lax.all_to_all(outgoing, 'req', split_axis=0, concat_axis=0, tiled=True)]
    unnamed x49 -> x57, local copies, waits for them, and re-layouts: 13.6 us -> 11.2 us
  transfers between devices with their start and end apart: 40 -> 40, of which waited for: 19 -> 19; matrix products, arithmetic and copies ran while one was open for 13% -> 11% of each run, Pallas kernels for 10% -> 11%
where the time goes in v4:
time: 212 us
  waiting for transfers between devices  79.2 us (37%)
  starting transfers between devices  57 us (27%)
  Pallas kernels  34.2 us (16%)
  local copies, waits for them, and re-layouts  28.2 us (13%)
  other arithmetic  8.16 us (4%)
  matrix products  3.45 us (2%)
    ppermute x39, waiting for transfers between devices, swap(): lax.ppermute(array, axis, [(i, i ^ step) for i in range(lax.axis_size(axi...  63.5 us
    ppermute x39, starting transfers between devices, swap(): lax.ppermute(array, axis, [(i, i ^ step) for i in range(lax.axis_size(axi...  50 us
    pallas_call x2, Pallas kernels, feed_forward(): pl.pallas_call(feed_forward_kernel, in_specs=[near] + [far] * 6, out_spec...  22.3 us
    all_to_all x1, waiting for transfers between devices, fetch_prefix(): lax.all_to_all(outgoing, 'req', split_axis=0, concat_axis=0, tiled=True)  15.6 us
    unnamed x57, local copies, waits for them, and re-layouts  11.2 us
    pallas_call x1, Pallas kernels, attend(): pl.pallas_call(attend_kernel, in_specs=[scalars] * 2 + [whole] * 9 + [pl....  10.3 us
    gather x2, local copies, waits for them, and re-layouts, fetch_prefix(): local = jnp.swapaxes(key_value_pages[own_slots], 1, 2)  8.92 us
    all_to_all x1, starting transfers between devices, fetch_prefix(): lax.all_to_all(outgoing, 'req', split_axis=0, concat_axis=0, tiled=True)  7.04 us
  transfers between devices with their start and end apart: 40, of which 19 were waited for; matrix products, arithmetic and copies ran while one was open for 11% of the time, Pallas kernels for 11%

profile of v4, /device:TPU:0, one launch (start us, length us, event | category | flops | bytes accessed | tf_op | source)
XLA Modules:
  0.0 211.6 jit_solution(7533500350565486164)
XLA Ops:
  4.7 2.7 %gather_fusion.1 = bf16[16,64,2,256]{3,2,1,0:T(2,128)(2,1)S(1)} fusion(bf16[32,64,2,256]{3,2,1,0:T(2,128)(2,1)S(1)} %copy-done, s32[1024]{0:T(1024)S(1)} %get-tuple-element.82), kind=kCustom, calls=%fused_computation.1 | custom fusion | bytes 2097216 | tf_op jit(solution)/shard_map/gather | solution.py:189
  8.6 7.0 %all-to-all-start = ((bf16[16,2,64,256]{3,2,1,0:T(8,128)(2,1)}), bf16[16,2,64,256]{3,2,1,0:T(8,128)(2,1)S(1)}, u32[]{:S(2)}, u32[]{:S(2)}) async-start(bf16[16,2,64,256]{3,2,1,0:T(8,128)(2,1)} %bitcast.40), calls=%async_computation | async-start | bytes 2097152 | tf_op jit(solution)/shard_map/all_to_all | solution.py:190
  16.8 6.0 %gather_fusion = bf16[24,64,2,256]{3,2,1,0:T(2,128)(2,1)} fusion(bf16[32,64,2,256]{3,2,1,0:T(2,128)(2,1)S(1)} %copy-done, s32[1024]{0:T(1024)S(1)} %get-tuple-element.83), kind=kCustom, calls=%fused_computation | custom fusion | bytes 3145824 | tf_op jit(solution)/shard_map/gather | solution.py:195
  22.8 2.9 %copy.60 = bf16[24,64,2,256]{3,1,2,0:T(8,128)(2,1)} copy(bf16[24,64,2,256]{3,2,1,0:T(2,128)(2,1)} %gather_fusion) | data formatting | bytes 3145728 | tf_op jit(solution)/shard_map/gather | solution.py:195
  26.3 15.6 %all-to-all-done.sent_pages_ref = bf16[16,2,64,256]{3,2,1,0:T(8,128)(2,1)S(1)} async-done(((bf16[16,2,64,256]{3,2,1,0:T(8,128)(2,1)}), bf16[16,2,64,256]{3,2,1,0:T(8,128)(2,1)S(1)}, u32[]{:S(2)}, u32[]{:S(2)}) %all-to-all-start) | async-done | bytes 1048608 | tf_op jit(solution)/shard_map/all_to_all | solution.py:190
  42.0 10.3 %attend.1 = f32[128,5120]{1,0:T(8,128)} custom-call(s32[24]{0:T(128)S(1)} %fusion.26.local_ref, s32[24]{0:T(128)S(1)} %fusion.32.entry_ref, bf16[128,1280]{1,0:T(8,128)(2,1)S(1)} %constant_dynamic-update-slice_fusion.queries_ref, s32[128,6]{1,0:T(8,128)S(1)} %fusion.24.limits_ref, s32[128,1]{1,0:T(8,128)S(1)} %copy.56.query_segments_ref, ...), custom_call_target="tpu_custom_call" | custom-call | flops 2768240640 | bytes 16515072 | tf_op jit(solution)/shard_map/attend/pallas_call | solution.py:140
  58.8 4.8 %collective-permute-done.4 = bf16[16,5120]{1,0:T(8,128)(2,1)S(1)} collective-permute-done((bf16[16,5120]{1,0:T(8,128)(2,1)S(1)}, bf16[16,5120]{1,0:T(8,128)(2,1)S(1)}, u32[]{:S(2)}, u32[]{:S(2)}) %collective-permute-start.4) | collective-permute-done | bytes 163872 | tf_op jit(solution)/shard_map/ppermute | solution.py:31
  63.6 2.7 %collective-permute-done.20 = bf16[16,5120]{1,0:T(8,128)(2,1)S(1)} collective-permute-done((bf16[16,5120]{1,0:T(8,128)(2,1)S(1)}, bf16[16,5120]{1,0:T(8,128)(2,1)S(1)}, u32[]{:S(2)}, u32[]{:S(2)}) %collective-permute-start.20) | collective-permute-done | bytes 163872 | tf_op jit(solution)/shard_map/ppermute | solution.py:31
  68.5 2.7 %collective-permute-start.22 = (bf16[16,5120]{1,0:T(8,128)(2,1)S(1)}, bf16[16,5120]{1,0:T(8,128)(2,1)}, u32[]{:S(2)}, u32[]{:S(2)}) collective-permute-start(bf16[16,5120]{1,0:T(8,128)(2,1)S(1)} %get-tuple-element.73), channel_id=1, source_target_pairs={{0,16},{4,20},{8,24},{12,28},{16,0},{20,4},{24,8},{28,12},{1,17},{... | collective-permute-start | bytes 491528 | tf_op jit(solution)/shard_map/ppermute | solution.py:31
  72.8 2.7 %collective-permute-start.6 = (bf16[16,5120]{1,0:T(8,128)(2,1)S(1)}, bf16[16,5120]{1,0:T(8,128)(2,1)S(1)}, u32[]{:S(2)}, u32[]{:S(2)}) collective-permute-start(bf16[16,5120]{1,0:T(8,128)(2,1)S(1)} %get-tuple-element.33), channel_id=1, source_target_pairs={{0,16},{4,20},{8,24},{12,28},{16,0},{20,4},{24,8},{28,12},{1,17},{... | collective-permute-start | bytes 491528 | tf_op jit(solution)/shard_map/ppermute | solution.py:31
  75.5 2.9 %collective-permute-done.21 = bf16[16,5120]{1,0:T(8,128)(2,1)} collective-permute-done((bf16[16,5120]{1,0:T(8,128)(2,1)S(1)}, bf16[16,5120]{1,0:T(8,128)(2,1)}, u32[]{:S(2)}, u32[]{:S(2)}) %collective-permute-start.21) | collective-permute-done | bytes 163872 | tf_op jit(solution)/shard_map/ppermute | solution.py:31
  80.8 2.8 %collective-permute-done.22 = bf16[16,5120]{1,0:T(8,128)(2,1)} collective-permute-done((bf16[16,5120]{1,0:T(8,128)(2,1)S(1)}, bf16[16,5120]{1,0:T(8,128)(2,1)}, u32[]{:S(2)}, u32[]{:S(2)}) %collective-permute-start.22) | collective-permute-done | bytes 163872 | tf_op jit(solution)/shard_map/ppermute | solution.py:31
  87.9 9.7 %collective-permute-done.6 = bf16[16,5120]{1,0:T(8,128)(2,1)S(1)} collective-permute-done((bf16[16,5120]{1,0:T(8,128)(2,1)S(1)}, bf16[16,5120]{1,0:T(8,128)(2,1)S(1)}, u32[]{:S(2)}, u32[]{:S(2)}) %collective-permute-start.6) | collective-permute-done | bytes 163872 | tf_op jit(solution)/shard_map/ppermute | solution.py:31
  104.8 12.0 %collective-permute-done.9 = bf16[64,5120]{1,0:T(8,128)(2,1)S(1)} collective-permute-done((bf16[64,5120]{1,0:T(8,128)(2,1)S(1)}, bf16[64,5120]{1,0:T(8,128)(2,1)S(1)}, u32[]{:S(2)}, u32[]{:S(2)}) %collective-permute-start.9) | collective-permute-done | bytes 655392 | tf_op jit(solution)/shard_map/ppermute | solution.py:31
  119.0 3.3 %collective-permute-done.26 = bf16[32,5120]{1,0:T(8,128)(2,1)S(1)} collective-permute-done((bf16[32,5120]{1,0:T(8,128)(2,1)S(1)}, bf16[32,5120]{1,0:T(8,128)(2,1)S(1)}, u32[]{:S(2)}, u32[]{:S(2)}) %collective-permute-start.26) | collective-permute-done | bytes 327712 | tf_op jit(solution)/shard_map/ppermute | solution.py:31
  123.8 11.1 %feed_forward.3 = bf16[256,5120]{1,0:T(8,128)(2,1)S(1)} custom-call(bf16[256,5120]{1,0:T(8,128)(2,1)S(1)} %constant_dynamic-update-slice_fusion.16.x_ref, bf16[432,5120]{1,0:T(8,128)(2,1)S(1)} %bitcast.33, bf16[432,5120]{1,0:T(8,128)(2,1)} %collective-permute-done.g1, bf16[432,5120]{1,0:T(8,128)(2,1)} %bitcast.37, ...), custom_call_target="tpu_custom_call" | custom-call | flops 6794772480 | bytes 31784960 | tf_op jit(solution)/shard_map/feed_forward/pallas_call | solution.py:319
  136.7 11.2 %feed_forward.2 = bf16[256,5120]{1,0:T(8,128)(2,1)S(1)} custom-call(bf16[256,5120]{1,0:T(8,128)(2,1)S(1)} %constant_dynamic-update-slice_fusion.8.x_ref, bf16[432,5120]{1,0:T(8,128)(2,1)S(1)} %bitcast.34, bf16[432,5120]{1,0:T(8,128)(2,1)} %collective-permute-done.g1, bf16[432,5120]{1,0:T(8,128)(2,1)} %bitcast.38, ...), custom_call_target="tpu_custom_call" | custom-call | flops 6794772480 | bytes 31784960 | tf_op jit(solution)/shard_map/feed_forward/pallas_call | solution.py:319
  152.5 6.2 %collective-permute-done.12 = bf16[32,5120]{1,0:T(8,128)(2,1)S(1)} collective-permute-done((bf16[32,5120]{1,0:T(8,128)(2,1)S(1)}, bf16[32,5120]{1,0:T(8,128)(2,1)S(1)}, u32[]{:S(2)}, u32[]{:S(2)}) %collective-permute-start.12) | collective-permute-done | bytes 327712 | tf_op jit(solution)/shard_map/ppermute | solution.py:31
  162.5 6.2 %copy-done.2 = bf16[5120,1792]{1,0:T(8,128)(2,1)S(1)} copy-done((bf16[5120,1792]{1,0:T(8,128)(2,1)S(1)}, bf16[5120,1792]{1,0:T(8,128)(2,1)}, u32[]{:S(2)}) %copy-start.2) | copy-done | bytes 18350104
  175.0 7.1 %collective-permute-start.33 = (bf16[16,5120]{1,0:T(8,128)(2,1)S(1)}, bf16[16,5120]{1,0:T(8,128)(2,1)S(1)}, u32[]{:S(2)}, u32[]{:S(2)}) collective-permute-start(bf16[16,5120]{1,0:T(8,128)(2,1)S(1)} %get-tuple-element.69), channel_id=1, source_target_pairs={{0,16},{4,20},{8,24},{12,28},{16,0},{20,4},{24,8},{28,12},{1,17},{... | collective-permute-start | bytes 491528 | tf_op jit(solution)/shard_map/ppermute | solution.py:31
  184.2 4.9 %collective-permute-start.17 = (bf16[16,5120]{1,0:T(8,128)(2,1)S(1)}, bf16[16,5120]{1,0:T(8,128)(2,1)S(1)}, u32[]{:S(2)}, u32[]{:S(2)}) collective-permute-start(bf16[16,5120]{1,0:T(8,128)(2,1)S(1)} %get-tuple-element.66), channel_id=1, source_target_pairs={{0,16},{4,20},{8,24},{12,28},{16,0},{20,4},{24,8},{28,12},{1,17},{... | collective-permute-start | bytes 491528 | tf_op jit(solution)/shard_map/ppermute | solution.py:31
  189.5 4.9 %collective-permute-done.33 = bf16[16,5120]{1,0:T(8,128)(2,1)S(1)} collective-permute-done((bf16[16,5120]{1,0:T(8,128)(2,1)S(1)}, bf16[16,5120]{1,0:T(8,128)(2,1)S(1)}, u32[]{:S(2)}, u32[]{:S(2)}) %collective-permute-start.33) | collective-permute-done | bytes 163872 | tf_op jit(solution)/shard_map/ppermute | solution.py:31
  194.7 3.2 %collective-permute-done.17 = bf16[16,5120]{1,0:T(8,128)(2,1)S(1)} collective-permute-done((bf16[16,5120]{1,0:T(8,128)(2,1)S(1)}, bf16[16,5120]{1,0:T(8,128)(2,1)S(1)}, u32[]{:S(2)}, u32[]{:S(2)}) %collective-permute-start.17) | collective-permute-done | bytes 163872 | tf_op jit(solution)/shard_map/ppermute | solution.py:31
  208.1 3.5 %fusion = bf16[128,1792]{1,0:T(8,128)(2,1)} fusion(bf16[128,5120]{1,0:T(8,128)(2,1)S(1)} %select_dynamic-update-slice_fusion, bf16[5120,1792]{1,0:T(8,128)(2,1)S(1)} %hold.1, f32[1792]{0:T(1024)S(1)} %copy-done.13), kind=kOutput, calls=%fused_computation.3 | convolution fusion | flops 2349268992 | bytes 20126720 | tf_op jit(solution)/shard_map/dot_general | solution.py:439
  (201 shorter events, 63.7 us)
Async XLA Ops:
  0.6 41.3 %collective-permute-start = (bf16[432,5120]{1,0:T(8,128)(2,1)}, bf16[432,5120]{1,0:T(8,128)(2,1)}, u32[]{:S(2)}, u32[]{:S(2)}) collective-permute-start(bf16[432,5120]{1,0:T(8,128)(2,1)} %bitcast.30), channel_id=1, source_target_pairs={{0,1},{1,0},{2,3},{3,2},{4,5},{5,4},{6,7},{7,6},{8,9},{9,8},{10,11... | collective-permute-start | bytes 13271048 | tf_op jit(solution)/shard_map/ppermute | solution.py:31
  1.2 40.8 %collective-permute-start.1 = (bf16[432,5120]{1,0:T(8,128)(2,1)}, bf16[432,5120]{1,0:T(8,128)(2,1)}, u32[]{:S(2)}, u32[]{:S(2)}) collective-permute-start(bf16[432,5120]{1,0:T(8,128)(2,1)} %bitcast.36), channel_id=1, source_target_pairs={{0,1},{1,0},{2,3},{3,2},{4,5},{5,4},{6,7},{7,6},{8,9},{9,8},{10,11... | collective-permute-start | bytes 13271048 | tf_op jit(solution)/shard_map/ppermute | solution.py:31
  1.2 40.7 %collective-permute-start.2 = (bf16[432,5120]{1,0:T(8,128)(2,1)}, bf16[432,5120]{1,0:T(8,128)(2,1)}, u32[]{:S(2)}, u32[]{:S(2)}) collective-permute-start(bf16[432,5120]{1,0:T(8,128)(2,1)} %d0.1), channel_id=1, source_target_pairs={{0,1},{1,0},{2,3},{3,2},{4,5},{5,4},{6,7},{7,6},{8,9},{9,8},{10,11... | collective-permute-start | bytes 13271048 | tf_op jit(solution)/shard_map/ppermute | solution.py:31
  8.6 33.4 %all-to-all-start = ((bf16[16,2,64,256]{3,2,1,0:T(8,128)(2,1)}), bf16[16,2,64,256]{3,2,1,0:T(8,128)(2,1)S(1)}, u32[]{:S(2)}, u32[]{:S(2)}) async-start(bf16[16,2,64,256]{3,2,1,0:T(8,128)(2,1)} %bitcast.40), calls=%async_computation | async-start | bytes 2097152 | tf_op jit(solution)/shard_map/all_to_all | solution.py:190
  68.5 15.2 %collective-permute-start.22 = (bf16[16,5120]{1,0:T(8,128)(2,1)S(1)}, bf16[16,5120]{1,0:T(8,128)(2,1)}, u32[]{:S(2)}, u32[]{:S(2)}) collective-permute-start(bf16[16,5120]{1,0:T(8,128)(2,1)S(1)} %get-tuple-element.73), channel_id=1, source_target_pairs={{0,16},{4,20},{8,24},{12,28},{16,0},{20,4},{24,8},{28,12},{1,17},{... | collective-permute-start | bytes 491528 | tf_op jit(solution)/shard_map/ppermute | solution.py:31
  72.8 15.0 %collective-permute-start.5 = (bf16[16,5120]{1,0:T(8,128)(2,1)S(1)}, bf16[16,5120]{1,0:T(8,128)(2,1)S(1)}, u32[]{:S(2)}, u32[]{:S(2)}) collective-permute-start(bf16[16,5120]{1,0:T(8,128)(2,1)S(1)} %get-tuple-element.33), channel_id=1, source_target_pairs={{0,8},{4,12},{8,0},{12,4},{16,24},{20,28},{24,16},{28,20},{1,9},{5... | collective-permute-start | bytes 491528 | tf_op jit(solution)/shard_map/ppermute | solution.py:31
  72.8 24.7 %collective-permute-start.6 = (bf16[16,5120]{1,0:T(8,128)(2,1)S(1)}, bf16[16,5120]{1,0:T(8,128)(2,1)S(1)}, u32[]{:S(2)}, u32[]{:S(2)}) collective-permute-start(bf16[16,5120]{1,0:T(8,128)(2,1)S(1)} %get-tuple-element.33), channel_id=1, source_target_pairs={{0,16},{4,20},{8,24},{12,28},{16,0},{20,4},{24,8},{28,12},{1,17},{... | collective-permute-start | bytes 491528 | tf_op jit(solution)/shard_map/ppermute | solution.py:31
  78.5 19.1 %collective-permute-start.7 = (bf16[16,5120]{1,0:T(8,128)(2,1)S(1)}, bf16[16,5120]{1,0:T(8,128)(2,1)S(1)}, u32[]{:S(2)}, u32[]{:S(2)}) collective-permute-start(bf16[16,5120]{1,0:T(8,128)(2,1)S(1)} %get-tuple-element.33), channel_id=1, source_target_pairs={{0,24},{4,28},{8,16},{12,20},{16,8},{20,12},{24,0},{28,4},{1,25},{... | collective-permute-start | bytes 491528 | tf_op jit(solution)/shard_map/ppermute | solution.py:31
  84.8 19.1 %collective-permute-start.24 = (bf16[64,5120]{1,0:T(8,128)(2,1)S(1)}, bf16[64,5120]{1,0:T(8,128)(2,1)S(1)}, u32[]{:S(2)}, u32[]{:S(2)}) collective-permute-start(bf16[64,5120]{1,0:T(8,128)(2,1)S(1)} %pad_maximum_fusion.3), channel_id=1, source_target_pairs={{0,2},{1,3},{2,0},{3,1},{4,6},{5,7},{6,4},{7,5},{8,10},{9,11},{10,... | collective-permute-start | bytes 1966088 | tf_op jit(solution)/shard_map/ppermute | solution.py:31
  86.3 16.9 %collective-permute-start.25 = (bf16[64,5120]{1,0:T(8,128)(2,1)S(1)}, bf16[64,5120]{1,0:T(8,128)(2,1)S(1)}, u32[]{:S(2)}, u32[]{:S(2)}) collective-permute-start(bf16[64,5120]{1,0:T(8,128)(2,1)S(1)} %pad_maximum_fusion.3), channel_id=1, source_target_pairs={{0,4},{4,0},{8,12},{12,8},{16,20},{20,16},{24,28},{28,24},{1,5},{5... | collective-permute-start | bytes 1966088 | tf_op jit(solution)/shard_map/ppermute | solution.py:31
  97.6 19.9 %collective-permute-start.8 = (bf16[64,5120]{1,0:T(8,128)(2,1)S(1)}, bf16[64,5120]{1,0:T(8,128)(2,1)S(1)}, u32[]{:S(2)}, u32[]{:S(2)}) collective-permute-start(bf16[64,5120]{1,0:T(8,128)(2,1)S(1)} %pad_maximum_fusion), channel_id=1, source_target_pairs={{0,2},{1,3},{2,0},{3,1},{4,6},{5,7},{6,4},{7,5},{8,10},{9,11},{10,... | collective-permute-start | bytes 1966088 | tf_op jit(solution)/shard_map/ppermute | solution.py:31
  99.1 17.7 %collective-permute-start.9 = (bf16[64,5120]{1,0:T(8,128)(2,1)S(1)}, bf16[64,5120]{1,0:T(8,128)(2,1)S(1)}, u32[]{:S(2)}, u32[]{:S(2)}) collective-permute-start(bf16[64,5120]{1,0:T(8,128)(2,1)S(1)} %pad_maximum_fusion), channel_id=1, source_target_pairs={{0,4},{4,0},{8,12},{12,8},{16,20},{20,16},{24,28},{28,24},{1,5},{5... | collective-permute-start | bytes 1966088 | tf_op jit(solution)/shard_map/ppermute | solution.py:31
  103.3 19.0 %collective-permute-start.26 = (bf16[32,5120]{1,0:T(8,128)(2,1)S(1)}, bf16[32,5120]{1,0:T(8,128)(2,1)S(1)}, u32[]{:S(2)}, u32[]{:S(2)}) collective-permute-start(bf16[32,5120]{1,0:T(8,128)(2,1)S(1)} %slice.257), channel_id=1, source_target_pairs={{0,2},{1,3},{2,0},{3,1},{4,6},{5,7},{6,4},{7,5},{8,10},{9,11},{10,... | collective-permute-start | bytes 983048 | tf_op jit(solution)/shard_map/ppermute | solution.py:31
  103.9 19.8 %collective-permute-start.27 = (bf16[32,5120]{1,0:T(8,128)(2,1)S(1)}, bf16[32,5120]{1,0:T(8,128)(2,1)S(1)}, u32[]{:S(2)}, u32[]{:S(2)}) collective-permute-start(bf16[32,5120]{1,0:T(8,128)(2,1)S(1)} %slice.258), channel_id=1, source_target_pairs={{0,4},{4,0},{8,12},{12,8},{16,20},{20,16},{24,28},{28,24},{1,5},{5... | collective-permute-start | bytes 983048 | tf_op jit(solution)/shard_map/ppermute | solution.py:31
  116.8 19.8 %collective-permute-start.10 = (bf16[32,5120]{1,0:T(8,128)(2,1)S(1)}, bf16[32,5120]{1,0:T(8,128)(2,1)S(1)}, u32[]{:S(2)}, u32[]{:S(2)}) collective-permute-start(bf16[32,5120]{1,0:T(8,128)(2,1)S(1)} %slice.238), channel_id=1, source_target_pairs={{0,2},{1,3},{2,0},{3,1},{4,6},{5,7},{6,4},{7,5},{8,10},{9,11},{10,... | collective-permute-start | bytes 983048 | tf_op jit(solution)/shard_map/ppermute | solution.py:31
  117.5 19.2 %collective-permute-start.11 = (bf16[32,5120]{1,0:T(8,128)(2,1)S(1)}, bf16[32,5120]{1,0:T(8,128)(2,1)S(1)}, u32[]{:S(2)}, u32[]{:S(2)}) collective-permute-start(bf16[32,5120]{1,0:T(8,128)(2,1)S(1)} %slice.239), channel_id=1, source_target_pairs={{0,4},{4,0},{8,12},{12,8},{16,20},{20,16},{24,28},{28,24},{1,5},{5... | collective-permute-start | bytes 983048 | tf_op jit(solution)/shard_map/ppermute | solution.py:31
  135.0 15.5 %collective-permute-start.28 = (bf16[32,5120]{1,0:T(8,128)(2,1)S(1)}, bf16[32,5120]{1,0:T(8,128)(2,1)S(1)}, u32[]{:S(2)}, u32[]{:S(2)}) collective-permute-start(bf16[32,5120]{1,0:T(8,128)(2,1)S(1)} %get-tuple-element.55), channel_id=1, source_target_pairs={{0,4},{4,0},{8,12},{12,8},{16,20},{20,16},{24,28},{28,24},{1,5},{5... | collective-permute-start | bytes 983048 | tf_op jit(solution)/shard_map/ppermute | solution.py:31
  136.0 14.5 %collective-permute-start.30 = (bf16[32,5120]{1,0:T(8,128)(2,1)S(1)}, bf16[32,5120]{1,0:T(8,128)(2,1)S(1)}, u32[]{:S(2)}, u32[]{:S(2)}) collective-permute-start(bf16[32,5120]{1,0:T(8,128)(2,1)S(1)} %get-tuple-element.54), channel_id=1, source_target_pairs={{0,2},{1,3},{2,0},{3,1},{4,6},{5,7},{6,4},{7,5},{8,10},{9,11},{10,... | collective-permute-start | bytes 983048 | tf_op jit(solution)/shard_map/ppermute | solution.py:31
  150.8 21.0 %collective-permute-start.31 = (bf16[64,5120]{1,0:T(8,128)(2,1)S(1)}, bf16[64,5120]{1,0:T(8,128)(2,1)S(1)}, u32[]{:S(2)}, u32[]{:S(2)}) collective-permute-start(bf16[64,5120]{1,0:T(8,128)(2,1)S(1)} %pad_maximum_fusion.5), channel_id=1, source_target_pairs={{0,4},{4,0},{8,12},{12,8},{16,20},{20,16},{24,28},{28,24},{1,5},{5... | collective-permute-start | bytes 1966088 | tf_op jit(solution)/shard_map/ppermute | solution.py:31
  151.8 20.3 %collective-permute-start.29 = (bf16[64,5120]{1,0:T(8,128)(2,1)S(1)}, bf16[64,5120]{1,0:T(8,128)(2,1)S(1)}, u32[]{:S(2)}, u32[]{:S(2)}) collective-permute-start(bf16[64,5120]{1,0:T(8,128)(2,1)S(1)} %pad_maximum_fusion.4), channel_id=1, source_target_pairs={{0,2},{1,3},{2,0},{3,1},{4,6},{5,7},{6,4},{7,5},{8,10},{9,11},{10,... | collective-permute-start | bytes 1966088 | tf_op jit(solution)/shard_map/ppermute | solution.py:31
  159.9 22.2 %collective-permute-start.15 = (bf16[64,5120]{1,0:T(8,128)(2,1)S(1)}, bf16[64,5120]{1,0:T(8,128)(2,1)S(1)}, u32[]{:S(2)}, u32[]{:S(2)}) collective-permute-start(bf16[64,5120]{1,0:T(8,128)(2,1)S(1)} %pad_maximum_fusion.2), channel_id=1, source_target_pairs={{0,4},{4,0},{8,12},{12,8},{16,20},{20,16},{24,28},{28,24},{1,5},{5... | collective-permute-start | bytes 1966088 | tf_op jit(solution)/shard_map/ppermute | solution.py:31
  161.0 21.1 %collective-permute-start.13 = (bf16[64,5120]{1,0:T(8,128)(2,1)S(1)}, bf16[64,5120]{1,0:T(8,128)(2,1)S(1)}, u32[]{:S(2)}, u32[]{:S(2)}) collective-permute-start(bf16[64,5120]{1,0:T(8,128)(2,1)S(1)} %pad_maximum_fusion.1), channel_id=1, source_target_pairs={{0,2},{1,3},{2,0},{3,1},{4,6},{5,7},{6,4},{7,5},{8,10},{9,11},{10,... | collective-permute-start | bytes 1966088 | tf_op jit(solution)/shard_map/ppermute | solution.py:31
  172.4 16.7 %collective-permute-start.34 = (bf16[16,5120]{1,0:T(8,128)(2,1)S(1)}, bf16[16,5120]{1,0:T(8,128)(2,1)S(1)}, u32[]{:S(2)}, u32[]{:S(2)}) collective-permute-start(bf16[16,5120]{1,0:T(8,128)(2,1)S(1)} %get-tuple-element.68), channel_id=1, source_target_pairs={{0,24},{4,28},{8,16},{12,20},{16,8},{20,12},{24,0},{28,4},{1,25},{... | collective-permute-start | bytes 491528 | tf_op jit(solution)/shard_map/ppermute | solution.py:31
  175.0 19.4 %collective-permute-start.33 = (bf16[16,5120]{1,0:T(8,128)(2,1)S(1)}, bf16[16,5120]{1,0:T(8,128)(2,1)S(1)}, u32[]{:S(2)}, u32[]{:S(2)}) collective-permute-start(bf16[16,5120]{1,0:T(8,128)(2,1)S(1)} %get-tuple-element.69), channel_id=1, source_target_pairs={{0,16},{4,20},{8,24},{12,28},{16,0},{20,4},{24,8},{28,12},{1,17},{... | collective-permute-start | bytes 491528 | tf_op jit(solution)/shard_map/ppermute | solution.py:31
  (35 other events, 344.3 us)

commit v5 on v4

--- a/solution.py
+++ b/solution.py
@@ -44,7 +44,8 @@
     leaf_keys_ref,
     leaf_values_ref,
     proj_ref,
-    out_ref,
+    kept_ref,
+    sent_ref,
     keys,
     values,
     mask,
@@ -102,12 +103,13 @@
         )
         heads_out[:, head] = (summed / total).astype(jnp.bfloat16)
     fetch.wait()
-    span = out_ref.shape[1] // 4
+    half = tokens // 2
+    span = kept_ref.shape[1] // 4
     for n in range(4):
         part = pl.ds(n * span, span)
-        out_ref[:, part] = jnp.dot(
-            heads_out[...], proj[:, part], preferred_element_type=jnp.float32
-        )
+        product = jnp.dot(heads_out[...], proj[:, part], preferred_element_type=jnp.float32)
+        kept_ref[:, part] = product[:half]
+        sent_ref[:, part] = product[half:].astype(jnp.bfloat16)
 
 
 def attend(
@@ -140,8 +142,11 @@
     return pl.pallas_call(
         attend_kernel,
         in_specs=[scalars] * 2 + [whole] * 9 + [pl.BlockSpec(memory_space=pltpu.HBM)],
-        out_specs=whole,
-        out_shape=jax.ShapeDtypeStruct((tokens, out_proj.shape[1]), jnp.float32),
+        out_specs=[whole, whole],
+        out_shape=[
+            jax.ShapeDtypeStruct((tokens // 2, out_proj.shape[1]), jnp.float32),
+            jax.ShapeDtypeStruct((tokens // 2, out_proj.shape[1]), jnp.bfloat16),
+        ],
         scratch_shapes=[
             pltpu.VMEM((key_count, columns), jnp.bfloat16),
             pltpu.VMEM((key_count, columns), jnp.bfloat16),
@@ -244,19 +249,11 @@
     return total, (by_x, by_y)
 
 
-def sum_cores(projected, rows):
-    members = lax.axis_size("mlp")
+def sum_heads(kept, sent, rows):
     wide = jnp.float32
-    blocks = [projected[j * rows : (j + 1) * rows] for j in range(members)]
-    odd = jnp.concatenate(blocks[1::2], 0).astype(jnp.bfloat16)
-    return jnp.concatenate(blocks[0::2], 0) + swap(odd, "mlp", 1).astype(wide)
-
-
-def sum_across(even, rows):
-    members = lax.axis_size("mlp")
-    wide = jnp.float32
+    even = kept + swap(sent, "mlp", 1).astype(wide)
     total = even[:rows]
-    for k in range(1, members // 2):
+    for k in range(1, kept.shape[0] // rows):
         part = even[k * rows : (k + 1) * rows].astype(jnp.bfloat16)
         total = total + swap(part, "mlp", 2 * k).astype(wide)
     return total
@@ -390,7 +387,10 @@
     downs = [down_proj, swap(down_proj, "mlp", 1)]
     fetched = fetch_prefix(key_value_pages, page_holder, page_slot)
     starts = [
-        (place ^ j) * owned + chunk * rows for chunk in range(CHUNKS) for j in range(members)
+        (place ^ j) * owned + chunk * rows
+        for core in range(2)
+        for chunk in range(CHUNKS)
+        for j in range(core, members, 2)
     ]
 
     def picked(array):
@@ -400,7 +400,7 @@
     asked, fetched, gates, uppers, downs = lax.optimization_barrier(
         (picked(queries), fetched, gates, uppers, downs)
     )
-    projected = attend(
+    kept, sent_rows = attend(
         asked,
         places,
         picked(segment_ids),
@@ -413,12 +413,12 @@
         node_len[0],
         out_proj,
     )
-    span = members * rows
-    evens = [sum_cores(projected[c * span : (c + 1) * span], rows) for c in range(CHUNKS)]
+    span = members // 2 * rows
     streams, mixed = [], []
     for chunk in range(CHUNKS):
         own = lax.dynamic_slice_in_dim(residual, place * owned + chunk * rows, rows, 0)
-        summed = sum_across(evens[chunk], rows)
+        part = slice(chunk * span, (chunk + 1) * span)
+        summed = sum_heads(kept[part], sent_rows[part], rows)
         streams.append((own.astype(jnp.float32) + summed).astype(jnp.bfloat16))
     for chunk in range(CHUNKS):
         tokens = gather_tokens(rms_norm(streams[chunk], norm_gain))

time: 212 us -> 210 us (level)
  transfers between devices with their start and end apart: 40 -> 40, of which waited for: 19 -> 20; matrix products, arithmetic and copies ran while one was open for 11% -> 11% of each run, Pallas kernels for 11% -> 11%
where the time goes in v5:
time: 210 us; the launch traced here: 209 us
  waiting for transfers between devices  79.8 us (38%)
  starting transfers between devices  56.9 us (27%)
  Pallas kernels  33.7 us (16%)
  local copies, waits for them, and re-layouts  26.1 us (12%)
  other arithmetic  7.92 us (4%)
  matrix products  3.45 us (2%)
    ppermute x39, waiting for transfers between devices, swap(): lax.ppermute(array, axis, [(i, i ^ step) for i in range(lax.axis_size(axi...  64.2 us
    ppermute x39, starting transfers between devices, swap(): lax.ppermute(array, axis, [(i, i ^ step) for i in range(lax.axis_size(axi...  49.9 us
    pallas_call x2, Pallas kernels, feed_forward(): pl.pallas_call(feed_forward_kernel, in_specs=[near] + [far] * 6, out_spec...  22.3 us
    all_to_all x1, waiting for transfers between devices, fetch_prefix(): lax.all_to_all(outgoing, 'req', split_axis=0, concat_axis=0, tiled=True)  15.7 us
    unnamed x57, local copies, waits for them, and re-layouts  10.6 us
    pallas_call x1, Pallas kernels, attend(): pl.pallas_call(attend_kernel, in_specs=[scalars] * 2 + [whole] * 9 + [pl....  9.9 us
    gather x2, local copies, waits for them, and re-layouts, fetch_prefix(): local = jnp.swapaxes(key_value_pages[own_slots], 1, 2)  8.89 us
    all_to_all x1, starting transfers between devices, fetch_prefix(): lax.all_to_all(outgoing, 'req', split_axis=0, concat_axis=0, tiled=True)  7.04 us
  transfers between devices with their start and end apart: 40, of which 20 were waited for; matrix products, arithmetic and copies ran while one was open for 11% of the time, Pallas kernels for 11%

profile of v5, /device:TPU:0, one launch (start us, length us, event | category | flops | bytes accessed | tf_op | source)
XLA Modules:
  0.0 209.3 jit_solution(9041624131132763932)
XLA Ops:
  4.7 2.7 %gather_fusion.1 = bf16[16,64,2,256]{3,2,1,0:T(2,128)(2,1)S(1)} fusion(bf16[32,64,2,256]{3,2,1,0:T(2,128)(2,1)S(1)} %copy-done, s32[1024]{0:T(1024)S(1)} %get-tuple-element.82), kind=kCustom, calls=%fused_computation.1 | custom fusion | bytes 2097216 | tf_op jit(solution)/shard_map/gather | solution.py:194
  8.5 7.0 %all-to-all-start = ((bf16[16,2,64,256]{3,2,1,0:T(8,128)(2,1)}), bf16[16,2,64,256]{3,2,1,0:T(8,128)(2,1)S(1)}, u32[]{:S(2)}, u32[]{:S(2)}) async-start(bf16[16,2,64,256]{3,2,1,0:T(8,128)(2,1)} %bitcast.40), calls=%async_computation | async-start | bytes 2097152 | tf_op jit(solution)/shard_map/all_to_all | solution.py:195
  16.8 6.0 %gather_fusion = bf16[24,64,2,256]{3,2,1,0:T(2,128)(2,1)} fusion(bf16[32,64,2,256]{3,2,1,0:T(2,128)(2,1)S(1)} %copy-done, s32[1024]{0:T(1024)S(1)} %get-tuple-element.83), kind=kCustom, calls=%fused_computation | custom fusion | bytes 3145824 | tf_op jit(solution)/shard_map/gather | solution.py:200
  22.8 2.9 %copy.60 = bf16[24,64,2,256]{3,1,2,0:T(8,128)(2,1)} copy(bf16[24,64,2,256]{3,2,1,0:T(2,128)(2,1)} %gather_fusion) | data formatting | bytes 3145728 | tf_op jit(solution)/shard_map/gather | solution.py:200
  26.3 15.7 %all-to-all-done.sent_pages_ref = bf16[16,2,64,256]{3,2,1,0:T(8,128)(2,1)S(1)} async-done(((bf16[16,2,64,256]{3,2,1,0:T(8,128)(2,1)}), bf16[16,2,64,256]{3,2,1,0:T(8,128)(2,1)S(1)}, u32[]{:S(2)}, u32[]{:S(2)}) %all-to-all-start) | async-done | bytes 1048608 | tf_op jit(solution)/shard_map/all_to_all | solution.py:195
  42.0 9.9 %attend.1 = (f32[64,5120]{1,0:T(8,128)}, bf16[64,5120]{1,0:T(8,128)(2,1)S(1)}) custom-call(s32[24]{0:T(128)S(1)} %fusion.26.local_ref, s32[24]{0:T(128)S(1)} %fusion.32.entry_ref, bf16[128,1280]{1,0:T(8,128)(2,1)S(1)} %constant_dynamic-update-slice_fusion.queries_ref, s32[128,6]{1,0:T(8,128)S(1)} %fusion.24.limits_ref, ...), custom_call_target="tpu_custom_call" | custom-call | flops 2768240640 | bytes 16515072 | tf_op jit(solution)/shard_map/attend/pallas_call | solution.py:142
  56.5 4.9 %collective-permute-done.4 = bf16[16,5120]{1,0:T(8,128)(2,1)S(1)} collective-permute-done((bf16[16,5120]{1,0:T(8,128)(2,1)S(1)}, bf16[16,5120]{1,0:T(8,128)(2,1)S(1)}, u32[]{:S(2)}, u32[]{:S(2)}) %collective-permute-start.4) | collective-permute-done | bytes 163872 | tf_op jit(solution)/shard_map/ppermute | solution.py:31
  61.4 2.7 %collective-permute-done.20 = bf16[16,5120]{1,0:T(8,128)(2,1)S(1)} collective-permute-done((bf16[16,5120]{1,0:T(8,128)(2,1)S(1)}, bf16[16,5120]{1,0:T(8,128)(2,1)S(1)}, u32[]{:S(2)}, u32[]{:S(2)}) %collective-permute-start.20) | collective-permute-done | bytes 163872 | tf_op jit(solution)/shard_map/ppermute | solution.py:31
  66.2 2.7 %collective-permute-start.22 = (bf16[16,5120]{1,0:T(8,128)(2,1)S(1)}, bf16[16,5120]{1,0:T(8,128)(2,1)}, u32[]{:S(2)}, u32[]{:S(2)}) collective-permute-start(bf16[16,5120]{1,0:T(8,128)(2,1)S(1)} %get-tuple-element.73), channel_id=1, source_target_pairs={{0,16},{4,20},{8,24},{12,28},{16,0},{20,4},{24,8},{28,12},{1,17},{... | collective-permute-start | bytes 491528 | tf_op jit(solution)/shard_map/ppermute | solution.py:31
  70.6 2.7 %collective-permute-start.6 = (bf16[16,5120]{1,0:T(8,128)(2,1)S(1)}, bf16[16,5120]{1,0:T(8,128)(2,1)S(1)}, u32[]{:S(2)}, u32[]{:S(2)}) collective-permute-start(bf16[16,5120]{1,0:T(8,128)(2,1)S(1)} %get-tuple-element.37), channel_id=1, source_target_pairs={{0,16},{4,20},{8,24},{12,28},{16,0},{20,4},{24,8},{28,12},{1,17},{... | collective-permute-start | bytes 491528 | tf_op jit(solution)/shard_map/ppermute | solution.py:31
  73.3 2.9 %collective-permute-done.21 = bf16[16,5120]{1,0:T(8,128)(2,1)} collective-permute-done((bf16[16,5120]{1,0:T(8,128)(2,1)S(1)}, bf16[16,5120]{1,0:T(8,128)(2,1)}, u32[]{:S(2)}, u32[]{:S(2)}) %collective-permute-start.21) | collective-permute-done | bytes 163872 | tf_op jit(solution)/shard_map/ppermute | solution.py:31
  78.5 2.8 %collective-permute-done.22 = bf16[16,5120]{1,0:T(8,128)(2,1)} collective-permute-done((bf16[16,5120]{1,0:T(8,128)(2,1)S(1)}, bf16[16,5120]{1,0:T(8,128)(2,1)}, u32[]{:S(2)}, u32[]{:S(2)}) %collective-permute-start.22) | collective-permute-done | bytes 163872 | tf_op jit(solution)/shard_map/ppermute | solution.py:31
  85.6 9.7 %collective-permute-done.6 = bf16[16,5120]{1,0:T(8,128)(2,1)S(1)} collective-permute-done((bf16[16,5120]{1,0:T(8,128)(2,1)S(1)}, bf16[16,5120]{1,0:T(8,128)(2,1)S(1)}, u32[]{:S(2)}, u32[]{:S(2)}) %collective-permute-start.6) | collective-permute-done | bytes 163872 | tf_op jit(solution)/shard_map/ppermute | solution.py:31
  102.5 12.0 %collective-permute-done.9 = bf16[64,5120]{1,0:T(8,128)(2,1)S(1)} collective-permute-done((bf16[64,5120]{1,0:T(8,128)(2,1)S(1)}, bf16[64,5120]{1,0:T(8,128)(2,1)S(1)}, u32[]{:S(2)}, u32[]{:S(2)}) %collective-permute-start.9) | collective-permute-done | bytes 655392 | tf_op jit(solution)/shard_map/ppermute | solution.py:31
  116.7 3.3 %collective-permute-done.26 = bf16[32,5120]{1,0:T(8,128)(2,1)S(1)} collective-permute-done((bf16[32,5120]{1,0:T(8,128)(2,1)S(1)}, bf16[32,5120]{1,0:T(8,128)(2,1)S(1)}, u32[]{:S(2)}, u32[]{:S(2)}) %collective-permute-start.26) | collective-permute-done | bytes 327712 | tf_op jit(solution)/shard_map/ppermute | solution.py:31
  121.5 11.1 %feed_forward.3 = bf16[256,5120]{1,0:T(8,128)(2,1)S(1)} custom-call(bf16[256,5120]{1,0:T(8,128)(2,1)S(1)} %constant_dynamic-update-slice_fusion.16.x_ref, bf16[432,5120]{1,0:T(8,128)(2,1)S(1)} %bitcast.33, bf16[432,5120]{1,0:T(8,128)(2,1)} %collective-permute-done.g1, bf16[432,5120]{1,0:T(8,128)(2,1)} %bitcast.37, ...), custom_call_target="tpu_custom_call" | custom-call | flops 6794772480 | bytes 31784960 | tf_op jit(solution)/shard_map/feed_forward/pallas_call | solution.py:316
  134.5 11.2 %feed_forward.2 = bf16[256,5120]{1,0:T(8,128)(2,1)S(1)} custom-call(bf16[256,5120]{1,0:T(8,128)(2,1)S(1)} %constant_dynamic-update-slice_fusion.8.x_ref, bf16[432,5120]{1,0:T(8,128)(2,1)S(1)} %bitcast.34, bf16[432,5120]{1,0:T(8,128)(2,1)} %collective-permute-done.g1, bf16[432,5120]{1,0:T(8,128)(2,1)} %bitcast.38, ...), custom_call_target="tpu_custom_call" | custom-call | flops 6794772480 | bytes 31784960 | tf_op jit(solution)/shard_map/feed_forward/pallas_call | solution.py:316
  150.3 6.2 %collective-permute-done.12 = bf16[32,5120]{1,0:T(8,128)(2,1)S(1)} collective-permute-done((bf16[32,5120]{1,0:T(8,128)(2,1)S(1)}, bf16[32,5120]{1,0:T(8,128)(2,1)S(1)}, u32[]{:S(2)}, u32[]{:S(2)}) %collective-permute-start.12) | collective-permute-done | bytes 327712 | tf_op jit(solution)/shard_map/ppermute | solution.py:31
  160.3 6.2 %copy-done.2 = bf16[5120,1792]{1,0:T(8,128)(2,1)S(1)} copy-done((bf16[5120,1792]{1,0:T(8,128)(2,1)S(1)}, bf16[5120,1792]{1,0:T(8,128)(2,1)}, u32[]{:S(2)}) %copy-start.2) | copy-done | bytes 18350104
  172.8 7.1 %collective-permute-start.33 = (bf16[16,5120]{1,0:T(8,128)(2,1)S(1)}, bf16[16,5120]{1,0:T(8,128)(2,1)S(1)}, u32[]{:S(2)}, u32[]{:S(2)}) collective-permute-start(bf16[16,5120]{1,0:T(8,128)(2,1)S(1)} %get-tuple-element.69), channel_id=1, source_target_pairs={{0,16},{4,20},{8,24},{12,28},{16,0},{20,4},{24,8},{28,12},{1,17},{... | collective-permute-start | bytes 491528 | tf_op jit(solution)/shard_map/ppermute | solution.py:31
  182.0 4.9 %collective-permute-start.17 = (bf16[16,5120]{1,0:T(8,128)(2,1)S(1)}, bf16[16,5120]{1,0:T(8,128)(2,1)S(1)}, u32[]{:S(2)}, u32[]{:S(2)}) collective-permute-start(bf16[16,5120]{1,0:T(8,128)(2,1)S(1)} %get-tuple-element.64), channel_id=1, source_target_pairs={{0,16},{4,20},{8,24},{12,28},{16,0},{20,4},{24,8},{28,12},{1,17},{... | collective-permute-start | bytes 491528 | tf_op jit(solution)/shard_map/ppermute | solution.py:31
  187.3 4.9 %collective-permute-done.33 = bf16[16,5120]{1,0:T(8,128)(2,1)S(1)} collective-permute-done((bf16[16,5120]{1,0:T(8,128)(2,1)S(1)}, bf16[16,5120]{1,0:T(8,128)(2,1)S(1)}, u32[]{:S(2)}, u32[]{:S(2)}) %collective-permute-start.33) | collective-permute-done | bytes 163872 | tf_op jit(solution)/shard_map/ppermute | solution.py:31
  192.5 3.2 %collective-permute-done.17 = bf16[16,5120]{1,0:T(8,128)(2,1)S(1)} collective-permute-done((bf16[16,5120]{1,0:T(8,128)(2,1)S(1)}, bf16[16,5120]{1,0:T(8,128)(2,1)S(1)}, u32[]{:S(2)}, u32[]{:S(2)}) %collective-permute-start.17) | collective-permute-done | bytes 163872 | tf_op jit(solution)/shard_map/ppermute | solution.py:31
  205.8 3.5 %fusion = bf16[128,1792]{1,0:T(8,128)(2,1)} fusion(bf16[128,5120]{1,0:T(8,128)(2,1)S(1)} %select_dynamic-update-slice_fusion, bf16[5120,1792]{1,0:T(8,128)(2,1)S(1)} %hold.1, f32[1792]{0:T(1024)S(1)} %copy-done.13), kind=kOutput, calls=%fused_computation.3 | convolution fusion | flops 2349268992 | bytes 20126720 | tf_op jit(solution)/shard_map/dot_general | solution.py:439
  (196 shorter events, 61.8 us)
Async XLA Ops:
  0.6 41.3 %collective-permute-start = (bf16[432,5120]{1,0:T(8,128)(2,1)}, bf16[432,5120]{1,0:T(8,128)(2,1)}, u32[]{:S(2)}, u32[]{:S(2)}) collective-permute-start(bf16[432,5120]{1,0:T(8,128)(2,1)} %bitcast.30), channel_id=1, source_target_pairs={{0,1},{1,0},{2,3},{3,2},{4,5},{5,4},{6,7},{7,6},{8,9},{9,8},{10,11... | collective-permute-start | bytes 13271048 | tf_op jit(solution)/shard_map/ppermute | solution.py:31
  1.2 40.8 %collective-permute-start.1 = (bf16[432,5120]{1,0:T(8,128)(2,1)}, bf16[432,5120]{1,0:T(8,128)(2,1)}, u32[]{:S(2)}, u32[]{:S(2)}) collective-permute-start(bf16[432,5120]{1,0:T(8,128)(2,1)} %bitcast.36), channel_id=1, source_target_pairs={{0,1},{1,0},{2,3},{3,2},{4,5},{5,4},{6,7},{7,6},{8,9},{9,8},{10,11... | collective-permute-start | bytes 13271048 | tf_op jit(solution)/shard_map/ppermute | solution.py:31
  1.2 40.7 %collective-permute-start.2 = (bf16[432,5120]{1,0:T(8,128)(2,1)}, bf16[432,5120]{1,0:T(8,128)(2,1)}, u32[]{:S(2)}, u32[]{:S(2)}) collective-permute-start(bf16[432,5120]{1,0:T(8,128)(2,1)} %d0.1), channel_id=1, source_target_pairs={{0,1},{1,0},{2,3},{3,2},{4,5},{5,4},{6,7},{7,6},{8,9},{9,8},{10,11... | collective-permute-start | bytes 13271048 | tf_op jit(solution)/shard_map/ppermute | solution.py:31
  8.5 33.4 %all-to-all-start = ((bf16[16,2,64,256]{3,2,1,0:T(8,128)(2,1)}), bf16[16,2,64,256]{3,2,1,0:T(8,128)(2,1)S(1)}, u32[]{:S(2)}, u32[]{:S(2)}) async-start(bf16[16,2,64,256]{3,2,1,0:T(8,128)(2,1)} %bitcast.40), calls=%async_computation | async-start | bytes 2097152 | tf_op jit(solution)/shard_map/all_to_all | solution.py:195
  66.2 15.2 %collective-permute-start.22 = (bf16[16,5120]{1,0:T(8,128)(2,1)S(1)}, bf16[16,5120]{1,0:T(8,128)(2,1)}, u32[]{:S(2)}, u32[]{:S(2)}) collective-permute-start(bf16[16,5120]{1,0:T(8,128)(2,1)S(1)} %get-tuple-element.73), channel_id=1, source_target_pairs={{0,16},{4,20},{8,24},{12,28},{16,0},{20,4},{24,8},{28,12},{1,17},{... | collective-permute-start | bytes 491528 | tf_op jit(solution)/shard_map/ppermute | solution.py:31
  70.6 15.0 %collective-permute-start.5 = (bf16[16,5120]{1,0:T(8,128)(2,1)S(1)}, bf16[16,5120]{1,0:T(8,128)(2,1)S(1)}, u32[]{:S(2)}, u32[]{:S(2)}) collective-permute-start(bf16[16,5120]{1,0:T(8,128)(2,1)S(1)} %get-tuple-element.37), channel_id=1, source_target_pairs={{0,8},{4,12},{8,0},{12,4},{16,24},{20,28},{24,16},{28,20},{1,9},{5... | collective-permute-start | bytes 491528 | tf_op jit(solution)/shard_map/ppermute | solution.py:31
  70.6 24.7 %collective-permute-start.6 = (bf16[16,5120]{1,0:T(8,128)(2,1)S(1)}, bf16[16,5120]{1,0:T(8,128)(2,1)S(1)}, u32[]{:S(2)}, u32[]{:S(2)}) collective-permute-start(bf16[16,5120]{1,0:T(8,128)(2,1)S(1)} %get-tuple-element.37), channel_id=1, source_target_pairs={{0,16},{4,20},{8,24},{12,28},{16,0},{20,4},{24,8},{28,12},{1,17},{... | collective-permute-start | bytes 491528 | tf_op jit(solution)/shard_map/ppermute | solution.py:31
  76.2 19.1 %collective-permute-start.7 = (bf16[16,5120]{1,0:T(8,128)(2,1)S(1)}, bf16[16,5120]{1,0:T(8,128)(2,1)S(1)}, u32[]{:S(2)}, u32[]{:S(2)}) collective-permute-start(bf16[16,5120]{1,0:T(8,128)(2,1)S(1)} %get-tuple-element.37), channel_id=1, source_target_pairs={{0,24},{4,28},{8,16},{12,20},{16,8},{20,12},{24,0},{28,4},{1,25},{... | collective-permute-start | bytes 491528 | tf_op jit(solution)/shard_map/ppermute | solution.py:31
  82.5 19.1 %collective-permute-start.24 = (bf16[64,5120]{1,0:T(8,128)(2,1)S(1)}, bf16[64,5120]{1,0:T(8,128)(2,1)S(1)}, u32[]{:S(2)}, u32[]{:S(2)}) collective-permute-start(bf16[64,5120]{1,0:T(8,128)(2,1)S(1)} %pad_maximum_fusion.3), channel_id=1, source_target_pairs={{0,2},{1,3},{2,0},{3,1},{4,6},{5,7},{6,4},{7,5},{8,10},{9,11},{10,... | collective-permute-start | bytes 1966088 | tf_op jit(solution)/shard_map/ppermute | solution.py:31
  84.1 16.9 %collective-permute-start.25 = (bf16[64,5120]{1,0:T(8,128)(2,1)S(1)}, bf16[64,5120]{1,0:T(8,128)(2,1)S(1)}, u32[]{:S(2)}, u32[]{:S(2)}) collective-permute-start(bf16[64,5120]{1,0:T(8,128)(2,1)S(1)} %pad_maximum_fusion.3), channel_id=1, source_target_pairs={{0,4},{4,0},{8,12},{12,8},{16,20},{20,16},{24,28},{28,24},{1,5},{5... | collective-permute-start | bytes 1966088 | tf_op jit(solution)/shard_map/ppermute | solution.py:31
  95.3 19.9 %collective-permute-start.8 = (bf16[64,5120]{1,0:T(8,128)(2,1)S(1)}, bf16[64,5120]{1,0:T(8,128)(2,1)S(1)}, u32[]{:S(2)}, u32[]{:S(2)}) collective-permute-start(bf16[64,5120]{1,0:T(8,128)(2,1)S(1)} %pad_maximum_fusion), channel_id=1, source_target_pairs={{0,2},{1,3},{2,0},{3,1},{4,6},{5,7},{6,4},{7,5},{8,10},{9,11},{10,... | collective-permute-start | bytes 1966088 | tf_op jit(solution)/shard_map/ppermute | solution.py:31
  96.9 17.7 %collective-permute-start.9 = (bf16[64,5120]{1,0:T(8,128)(2,1)S(1)}, bf16[64,5120]{1,0:T(8,128)(2,1)S(1)}, u32[]{:S(2)}, u32[]{:S(2)}) collective-permute-start(bf16[64,5120]{1,0:T(8,128)(2,1)S(1)} %pad_maximum_fusion), channel_id=1, source_target_pairs={{0,4},{4,0},{8,12},{12,8},{16,20},{20,16},{24,28},{28,24},{1,5},{5... | collective-permute-start | bytes 1966088 | tf_op jit(solution)/shard_map/ppermute | solution.py:31
  101.1 19.0 %collective-permute-start.26 = (bf16[32,5120]{1,0:T(8,128)(2,1)S(1)}, bf16[32,5120]{1,0:T(8,128)(2,1)S(1)}, u32[]{:S(2)}, u32[]{:S(2)}) collective-permute-start(bf16[32,5120]{1,0:T(8,128)(2,1)S(1)} %slice.219), channel_id=1, source_target_pairs={{0,2},{1,3},{2,0},{3,1},{4,6},{5,7},{6,4},{7,5},{8,10},{9,11},{10,... | collective-permute-start | bytes 983048 | tf_op jit(solution)/shard_map/ppermute | solution.py:31
  101.7 19.8 %collective-permute-start.27 = (bf16[32,5120]{1,0:T(8,128)(2,1)S(1)}, bf16[32,5120]{1,0:T(8,128)(2,1)S(1)}, u32[]{:S(2)}, u32[]{:S(2)}) collective-permute-start(bf16[32,5120]{1,0:T(8,128)(2,1)S(1)} %slice.220), channel_id=1, source_target_pairs={{0,4},{4,0},{8,12},{12,8},{16,20},{20,16},{24,28},{28,24},{1,5},{5... | collective-permute-start | bytes 983048 | tf_op jit(solution)/shard_map/ppermute | solution.py:31
  114.6 19.8 %collective-permute-start.10 = (bf16[32,5120]{1,0:T(8,128)(2,1)S(1)}, bf16[32,5120]{1,0:T(8,128)(2,1)S(1)}, u32[]{:S(2)}, u32[]{:S(2)}) collective-permute-start(bf16[32,5120]{1,0:T(8,128)(2,1)S(1)} %slice.204), channel_id=1, source_target_pairs={{0,2},{1,3},{2,0},{3,1},{4,6},{5,7},{6,4},{7,5},{8,10},{9,11},{10,... | collective-permute-start | bytes 983048 | tf_op jit(solution)/shard_map/ppermute | solution.py:31
  115.2 19.2 %collective-permute-start.11 = (bf16[32,5120]{1,0:T(8,128)(2,1)S(1)}, bf16[32,5120]{1,0:T(8,128)(2,1)S(1)}, u32[]{:S(2)}, u32[]{:S(2)}) collective-permute-start(bf16[32,5120]{1,0:T(8,128)(2,1)S(1)} %slice.205), channel_id=1, source_target_pairs={{0,4},{4,0},{8,12},{12,8},{16,20},{20,16},{24,28},{28,24},{1,5},{5... | collective-permute-start | bytes 983048 | tf_op jit(solution)/shard_map/ppermute | solution.py:31
  132.8 15.5 %collective-permute-start.28 = (bf16[32,5120]{1,0:T(8,128)(2,1)S(1)}, bf16[32,5120]{1,0:T(8,128)(2,1)S(1)}, u32[]{:S(2)}, u32[]{:S(2)}) collective-permute-start(bf16[32,5120]{1,0:T(8,128)(2,1)S(1)} %get-tuple-element.55), channel_id=1, source_target_pairs={{0,4},{4,0},{8,12},{12,8},{16,20},{20,16},{24,28},{28,24},{1,5},{5... | collective-permute-start | bytes 983048 | tf_op jit(solution)/shard_map/ppermute | solution.py:31
  133.8 14.5 %collective-permute-start.30 = (bf16[32,5120]{1,0:T(8,128)(2,1)S(1)}, bf16[32,5120]{1,0:T(8,128)(2,1)S(1)}, u32[]{:S(2)}, u32[]{:S(2)}) collective-permute-start(bf16[32,5120]{1,0:T(8,128)(2,1)S(1)} %get-tuple-element.54), channel_id=1, source_target_pairs={{0,2},{1,3},{2,0},{3,1},{4,6},{5,7},{6,4},{7,5},{8,10},{9,11},{10,... | collective-permute-start | bytes 983048 | tf_op jit(solution)/shard_map/ppermute | solution.py:31
  148.5 21.0 %collective-permute-start.31 = (bf16[64,5120]{1,0:T(8,128)(2,1)S(1)}, bf16[64,5120]{1,0:T(8,128)(2,1)S(1)}, u32[]{:S(2)}, u32[]{:S(2)}) collective-permute-start(bf16[64,5120]{1,0:T(8,128)(2,1)S(1)} %pad_maximum_fusion.5), channel_id=1, source_target_pairs={{0,4},{4,0},{8,12},{12,8},{16,20},{20,16},{24,28},{28,24},{1,5},{5... | collective-permute-start | bytes 1966088 | tf_op jit(solution)/shard_map/ppermute | solution.py:31
  149.6 20.3 %collective-permute-start.29 = (bf16[64,5120]{1,0:T(8,128)(2,1)S(1)}, bf16[64,5120]{1,0:T(8,128)(2,1)S(1)}, u32[]{:S(2)}, u32[]{:S(2)}) collective-permute-start(bf16[64,5120]{1,0:T(8,128)(2,1)S(1)} %pad_maximum_fusion.4), channel_id=1, source_target_pairs={{0,2},{1,3},{2,0},{3,1},{4,6},{5,7},{6,4},{7,5},{8,10},{9,11},{10,... | collective-permute-start | bytes 1966088 | tf_op jit(solution)/shard_map/ppermute | solution.py:31
  157.7 22.2 %collective-permute-start.15 = (bf16[64,5120]{1,0:T(8,128)(2,1)S(1)}, bf16[64,5120]{1,0:T(8,128)(2,1)S(1)}, u32[]{:S(2)}, u32[]{:S(2)}) collective-permute-start(bf16[64,5120]{1,0:T(8,128)(2,1)S(1)} %pad_maximum_fusion.2), channel_id=1, source_target_pairs={{0,4},{4,0},{8,12},{12,8},{16,20},{20,16},{24,28},{28,24},{1,5},{5... | collective-permute-start | bytes 1966088 | tf_op jit(solution)/shard_map/ppermute | solution.py:31
  158.8 21.1 %collective-permute-start.13 = (bf16[64,5120]{1,0:T(8,128)(2,1)S(1)}, bf16[64,5120]{1,0:T(8,128)(2,1)S(1)}, u32[]{:S(2)}, u32[]{:S(2)}) collective-permute-start(bf16[64,5120]{1,0:T(8,128)(2,1)S(1)} %pad_maximum_fusion.1), channel_id=1, source_target_pairs={{0,2},{1,3},{2,0},{3,1},{4,6},{5,7},{6,4},{7,5},{8,10},{9,11},{10,... | collective-permute-start | bytes 1966088 | tf_op jit(solution)/shard_map/ppermute | solution.py:31
  170.1 16.7 %collective-permute-start.34 = (bf16[16,5120]{1,0:T(8,128)(2,1)S(1)}, bf16[16,5120]{1,0:T(8,128)(2,1)S(1)}, u32[]{:S(2)}, u32[]{:S(2)}) collective-permute-start(bf16[16,5120]{1,0:T(8,128)(2,1)S(1)} %get-tuple-element.68), channel_id=1, source_target_pairs={{0,24},{4,28},{8,16},{12,20},{16,8},{20,12},{24,0},{28,4},{1,25},{... | collective-permute-start | bytes 491528 | tf_op jit(solution)/shard_map/ppermute | solution.py:31
  172.8 19.4 %collective-permute-start.33 = (bf16[16,5120]{1,0:T(8,128)(2,1)S(1)}, bf16[16,5120]{1,0:T(8,128)(2,1)S(1)}, u32[]{:S(2)}, u32[]{:S(2)}) collective-permute-start(bf16[16,5120]{1,0:T(8,128)(2,1)S(1)} %get-tuple-element.69), channel_id=1, source_target_pairs={{0,16},{4,20},{8,24},{12,28},{16,0},{20,4},{24,8},{28,12},{1,17},{... | collective-permute-start | bytes 491528 | tf_op jit(solution)/shard_map/ppermute | solution.py:31
  (35 other events, 345.0 us)

commit v6 on v5

--- a/solution.py
+++ b/solution.py
@@ -85,23 +85,27 @@
     seen = (segments_ref[...] == query_segments_ref[...]) & (at <= places_ref[...])
     mask[:, prefix:] = jnp.where(seen, 0.0, -1e30)
     scale = 1.0 / math.sqrt(HEAD_SIZE)
-    for h in range(heads_kv * QUERY_PER_KV):
-        group = pl.ds(h // QUERY_PER_KV * HEAD_SIZE, HEAD_SIZE)
-        head = pl.ds(h * HEAD_SIZE, HEAD_SIZE)
+    for g in range(heads_kv):
+        group = pl.ds(g * HEAD_SIZE, HEAD_SIZE)
+        heads = [pl.ds((g * QUERY_PER_KV + h) * HEAD_SIZE, HEAD_SIZE) for h in range(QUERY_PER_KV)]
         score = lax.dot_general(
-            queries_ref[:, head],
+            jnp.concatenate([queries_ref[:, head] for head in heads], 0),
             keys[:, group],
             (((1,), (1,)), ((), ())),
             preferred_element_type=jnp.float32,
         )
-        score = score * scale + mask[...]
-        top = jnp.max(score, axis=1, keepdims=True)
+        score = score.reshape(QUERY_PER_KV, tokens, -1) * scale + mask[...][None]
+        top = jnp.max(score, axis=2, keepdims=True)
         expo = jnp.exp(score - top)
-        total = jnp.sum(expo, axis=1, keepdims=True)
+        total = jnp.sum(expo, axis=2, keepdims=True)
         summed = jnp.dot(
-            expo.astype(jnp.bfloat16), values[:, group], preferred_element_type=jnp.float32
+            expo.astype(jnp.bfloat16).reshape(QUERY_PER_KV * tokens, -1),
+            values[:, group],
+            preferred_element_type=jnp.float32,
         )
-        heads_out[:, head] = (summed / total).astype(jnp.bfloat16)
+        result = (summed.reshape(QUERY_PER_KV, tokens, -1) / total).astype(jnp.bfloat16)
+        for h, head in enumerate(heads):
+            heads_out[:, head] = result[h]
     fetch.wait()
     half = tokens // 2
     span = kept_ref.shape[1] // 4
@@ -188,9 +192,16 @@
     earlier = jnp.arange(token_count)[None, :] < jnp.arange(token_count)[:, None]
     same = holders[:, :, None] == holders[:, None, :]
     rank = jnp.sum(same & earlier[None, :, :], axis=-1)
-    asked = (holders == myself) & (jnp.arange(groups)[:, None] != myself)
-    picked = asked[:, None, :] & (rank[:, None, :] == jnp.arange(room)[None, :, None])
-    send_slot = jnp.sum(jnp.where(picked, slots[:, None, :], 0), axis=-1)
+    count = page_holder.shape[2]
+    index = jnp.arange(page_holder.shape[1])[:, None] * count + jnp.arange(count)[None, :]
+    asked = (page_holder == myself) & (jnp.arange(groups)[:, None, None] != myself)
+    ends = [jnp.min(jnp.where(asked, index, token_count), axis=(1, 2))]
+    if room > 1:
+        ends.append(jnp.max(jnp.where(asked, index, -1), axis=(1, 2)))
+    send_slot = jnp.stack(
+        [jnp.sum(jnp.where(index == end[:, None, None], page_slot, 0), axis=(1, 2)) for end in ends],
+        1,
+    )
     outgoing = jnp.swapaxes(key_value_pages[send_slot.reshape(-1)], 1, 2)
     incoming = lax.all_to_all(outgoing, "req", split_axis=0, concat_axis=0, tiled=True)
     own_holders = lax.dynamic_index_in_dim(holders, myself, 0, keepdims=False)

time: 210 us -> 209 us (level)
    unnamed x57 -> x60, local copies, waits for them, and re-layouts: 10.6 us -> 10.7 us
  transfers between devices with their start and end apart: 40 -> 40, of which waited for: 20 -> 20; matrix products, arithmetic and copies ran while one was open for 11% -> 12% of each run, Pallas kernels for 11% -> 11%
where the time goes in v6:
time: 209 us
  waiting for transfers between devices  79.5 us (38%)
  starting transfers between devices  57 us (27%)
  Pallas kernels  33.4 us (16%)
  local copies, waits for them, and re-layouts  25.4 us (12%)
  other arithmetic  8.74 us (4%)
  matrix products  3.46 us (2%)
    ppermute x39, waiting for transfers between devices, swap(): lax.ppermute(array, axis, [(i, i ^ step) for i in range(lax.axis_size(axi...  64.2 us
    ppermute x39, starting transfers between devices, swap(): lax.ppermute(array, axis, [(i, i ^ step) for i in range(lax.axis_size(axi...  49.9 us
    pallas_call x2, Pallas kernels, feed_forward(): pl.pallas_call(feed_forward_kernel, in_specs=[near] + [far] * 6, out_spec...  22.3 us
    all_to_all x1, waiting for transfers between devices, fetch_prefix(): lax.all_to_all(outgoing, 'req', split_axis=0, concat_axis=0, tiled=True)  15.3 us
    unnamed x60, local copies, waits for them, and re-layouts  10.7 us
    pallas_call x1, Pallas kernels, attend(): pl.pallas_call(attend_kernel, in_specs=[scalars] * 2 + [whole] * 9 + [pl....  9.59 us
    gather x2, local copies, waits for them, and re-layouts, fetch_prefix(): local = jnp.swapaxes(key_value_pages[own_slots], 1, 2)  8.87 us
    all_to_all x1, starting transfers between devices, fetch_prefix(): lax.all_to_all(outgoing, 'req', split_axis=0, concat_axis=0, tiled=True)  7.05 us
  transfers between devices with their start and end apart: 40, of which 20 were waited for; matrix products, arithmetic and copies ran while one was open for 12% of the time, Pallas kernels for 11%

profile of v6, /device:TPU:0, one launch (start us, length us, event | category | flops | bytes accessed | tf_op | source)
XLA Modules:
  0.0 208.8 jit_solution(12002775272984824395)
XLA Ops:
  8.3 7.1 %all-to-all-start = ((bf16[16,2,64,256]{3,2,1,0:T(8,128)(2,1)}), bf16[16,2,64,256]{3,2,1,0:T(8,128)(2,1)S(1)}, u32[]{:S(2)}, u32[]{:S(2)}) async-start(bf16[16,2,64,256]{3,2,1,0:T(8,128)(2,1)} %bitcast.40), calls=%async_computation | async-start | bytes 2097152 | tf_op jit(solution)/shard_map/all_to_all | solution.py:206
  16.9 6.0 %gather_fusion = bf16[24,64,2,256]{3,2,1,0:T(2,128)(2,1)} fusion(bf16[32,64,2,256]{3,2,1,0:T(2,128)(2,1)S(1)} %copy-done, s32[1024]{0:T(1024)S(1)} %get-tuple-element.87), kind=kCustom, calls=%fused_computation | custom fusion | bytes 3145824 | tf_op jit(solution)/shard_map/gather | solution.py:211
  22.9 2.9 %copy.56 = bf16[24,64,2,256]{3,1,2,0:T(8,128)(2,1)} copy(bf16[24,64,2,256]{3,2,1,0:T(2,128)(2,1)} %gather_fusion) | data formatting | bytes 3145728 | tf_op jit(solution)/shard_map/gather | solution.py:211
  26.4 15.3 %all-to-all-done.sent_pages_ref = bf16[16,2,64,256]{3,2,1,0:T(8,128)(2,1)S(1)} async-done(((bf16[16,2,64,256]{3,2,1,0:T(8,128)(2,1)}), bf16[16,2,64,256]{3,2,1,0:T(8,128)(2,1)S(1)}, u32[]{:S(2)}, u32[]{:S(2)}) %all-to-all-start) | async-done | bytes 1048608 | tf_op jit(solution)/shard_map/all_to_all | solution.py:206
  41.7 9.6 %attend.1 = (f32[64,5120]{1,0:T(8,128)}, bf16[64,5120]{1,0:T(8,128)(2,1)S(1)}) custom-call(s32[24]{0:T(128)S(1)} %fusion.25.local_ref, s32[24]{0:T(128)S(1)} %fusion.30.entry_ref, bf16[128,1280]{1,0:T(8,128)(2,1)S(1)} %constant_dynamic-update-slice_fusion.queries_ref, s32[128,6]{1,0:T(8,128)S(1)} %fusion.24.limits_ref, ...), custom_call_target="tpu_custom_call" | custom-call | flops 2768240640 | bytes 16515072 | tf_op jit(solution)/shard_map/attend/pallas_call | solution.py:146
  55.9 4.9 %collective-permute-done.4 = bf16[16,5120]{1,0:T(8,128)(2,1)S(1)} collective-permute-done((bf16[16,5120]{1,0:T(8,128)(2,1)S(1)}, bf16[16,5120]{1,0:T(8,128)(2,1)S(1)}, u32[]{:S(2)}, u32[]{:S(2)}) %collective-permute-start.4) | collective-permute-done | bytes 163872 | tf_op jit(solution)/shard_map/ppermute | solution.py:31
  60.8 2.7 %collective-permute-done.20 = bf16[16,5120]{1,0:T(8,128)(2,1)S(1)} collective-permute-done((bf16[16,5120]{1,0:T(8,128)(2,1)S(1)}, bf16[16,5120]{1,0:T(8,128)(2,1)S(1)}, u32[]{:S(2)}, u32[]{:S(2)}) %collective-permute-start.20) | collective-permute-done | bytes 163872 | tf_op jit(solution)/shard_map/ppermute | solution.py:31
  65.7 2.7 %collective-permute-start.22 = (bf16[16,5120]{1,0:T(8,128)(2,1)S(1)}, bf16[16,5120]{1,0:T(8,128)(2,1)}, u32[]{:S(2)}, u32[]{:S(2)}) collective-permute-start(bf16[16,5120]{1,0:T(8,128)(2,1)S(1)} %get-tuple-element.77), channel_id=1, source_target_pairs={{0,16},{4,20},{8,24},{12,28},{16,0},{20,4},{24,8},{28,12},{1,17},{... | collective-permute-start | bytes 491528 | tf_op jit(solution)/shard_map/ppermute | solution.py:31
  70.1 2.7 %collective-permute-start.6 = (bf16[16,5120]{1,0:T(8,128)(2,1)S(1)}, bf16[16,5120]{1,0:T(8,128)(2,1)S(1)}, u32[]{:S(2)}, u32[]{:S(2)}) collective-permute-start(bf16[16,5120]{1,0:T(8,128)(2,1)S(1)} %get-tuple-element.41), channel_id=1, source_target_pairs={{0,16},{4,20},{8,24},{12,28},{16,0},{20,4},{24,8},{28,12},{1,17},{... | collective-permute-start | bytes 491528 | tf_op jit(solution)/shard_map/ppermute | solution.py:31
  72.7 2.9 %collective-permute-done.21 = bf16[16,5120]{1,0:T(8,128)(2,1)} collective-permute-done((bf16[16,5120]{1,0:T(8,128)(2,1)S(1)}, bf16[16,5120]{1,0:T(8,128)(2,1)}, u32[]{:S(2)}, u32[]{:S(2)}) %collective-permute-start.21) | collective-permute-done | bytes 163872 | tf_op jit(solution)/shard_map/ppermute | solution.py:31
  78.0 2.8 %collective-permute-done.22 = bf16[16,5120]{1,0:T(8,128)(2,1)} collective-permute-done((bf16[16,5120]{1,0:T(8,128)(2,1)S(1)}, bf16[16,5120]{1,0:T(8,128)(2,1)}, u32[]{:S(2)}, u32[]{:S(2)}) %collective-permute-start.22) | collective-permute-done | bytes 163872 | tf_op jit(solution)/shard_map/ppermute | solution.py:31
  85.1 9.6 %collective-permute-done.6 = bf16[16,5120]{1,0:T(8,128)(2,1)S(1)} collective-permute-done((bf16[16,5120]{1,0:T(8,128)(2,1)S(1)}, bf16[16,5120]{1,0:T(8,128)(2,1)S(1)}, u32[]{:S(2)}, u32[]{:S(2)}) %collective-permute-start.6) | collective-permute-done | bytes 163872 | tf_op jit(solution)/shard_map/ppermute | solution.py:31
  102.0 12.0 %collective-permute-done.9 = bf16[64,5120]{1,0:T(8,128)(2,1)S(1)} collective-permute-done((bf16[64,5120]{1,0:T(8,128)(2,1)S(1)}, bf16[64,5120]{1,0:T(8,128)(2,1)S(1)}, u32[]{:S(2)}, u32[]{:S(2)}) %collective-permute-start.9) | collective-permute-done | bytes 655392 | tf_op jit(solution)/shard_map/ppermute | solution.py:31
  116.2 3.3 %collective-permute-done.26 = bf16[32,5120]{1,0:T(8,128)(2,1)S(1)} collective-permute-done((bf16[32,5120]{1,0:T(8,128)(2,1)S(1)}, bf16[32,5120]{1,0:T(8,128)(2,1)S(1)}, u32[]{:S(2)}, u32[]{:S(2)}) %collective-permute-start.26) | collective-permute-done | bytes 327712 | tf_op jit(solution)/shard_map/ppermute | solution.py:31
  121.0 11.1 %feed_forward.3 = bf16[256,5120]{1,0:T(8,128)(2,1)S(1)} custom-call(bf16[256,5120]{1,0:T(8,128)(2,1)S(1)} %constant_dynamic-update-slice_fusion.16.x_ref, bf16[432,5120]{1,0:T(8,128)(2,1)S(1)} %bitcast.33, bf16[432,5120]{1,0:T(8,128)(2,1)} %collective-permute-done.g1, bf16[432,5120]{1,0:T(8,128)(2,1)} %bitcast.37, ...), custom_call_target="tpu_custom_call" | custom-call | flops 6794772480 | bytes 31784960 | tf_op jit(solution)/shard_map/feed_forward/pallas_call | solution.py:327
  133.9 11.2 %feed_forward.2 = bf16[256,5120]{1,0:T(8,128)(2,1)S(1)} custom-call(bf16[256,5120]{1,0:T(8,128)(2,1)S(1)} %constant_dynamic-update-slice_fusion.8.x_ref, bf16[432,5120]{1,0:T(8,128)(2,1)S(1)} %bitcast.34, bf16[432,5120]{1,0:T(8,128)(2,1)} %collective-permute-done.g1, bf16[432,5120]{1,0:T(8,128)(2,1)} %bitcast.38, ...), custom_call_target="tpu_custom_call" | custom-call | flops 6794772480 | bytes 31784960 | tf_op jit(solution)/shard_map/feed_forward/pallas_call | solution.py:327
  149.7 6.2 %collective-permute-done.12 = bf16[32,5120]{1,0:T(8,128)(2,1)S(1)} collective-permute-done((bf16[32,5120]{1,0:T(8,128)(2,1)S(1)}, bf16[32,5120]{1,0:T(8,128)(2,1)S(1)}, u32[]{:S(2)}, u32[]{:S(2)}) %collective-permute-start.12) | collective-permute-done | bytes 327712 | tf_op jit(solution)/shard_map/ppermute | solution.py:31
  159.7 6.2 %copy-done.2 = bf16[5120,1792]{1,0:T(8,128)(2,1)S(1)} copy-done((bf16[5120,1792]{1,0:T(8,128)(2,1)S(1)}, bf16[5120,1792]{1,0:T(8,128)(2,1)}, u32[]{:S(2)}) %copy-start.2) | copy-done | bytes 18350104
  169.6 2.7 %collective-permute-start.34 = (bf16[16,5120]{1,0:T(8,128)(2,1)S(1)}, bf16[16,5120]{1,0:T(8,128)(2,1)S(1)}, u32[]{:S(2)}, u32[]{:S(2)}) collective-permute-start(bf16[16,5120]{1,0:T(8,128)(2,1)S(1)} %get-tuple-element.72), channel_id=1, source_target_pairs={{0,24},{4,28},{8,16},{12,20},{16,8},{20,12},{24,0},{28,4},{1,25},{... | collective-permute-start | bytes 491528 | tf_op jit(solution)/shard_map/ppermute | solution.py:31
  172.2 7.1 %collective-permute-start.33 = (bf16[16,5120]{1,0:T(8,128)(2,1)S(1)}, bf16[16,5120]{1,0:T(8,128)(2,1)S(1)}, u32[]{:S(2)}, u32[]{:S(2)}) collective-permute-start(bf16[16,5120]{1,0:T(8,128)(2,1)S(1)} %get-tuple-element.73), channel_id=1, source_target_pairs={{0,16},{4,20},{8,24},{12,28},{16,0},{20,4},{24,8},{28,12},{1,17},{... | collective-permute-start | bytes 491528 | tf_op jit(solution)/shard_map/ppermute | solution.py:31
  181.4 5.0 %collective-permute-start.17 = (bf16[16,5120]{1,0:T(8,128)(2,1)S(1)}, bf16[16,5120]{1,0:T(8,128)(2,1)S(1)}, u32[]{:S(2)}, u32[]{:S(2)}) collective-permute-start(bf16[16,5120]{1,0:T(8,128)(2,1)S(1)} %get-tuple-element.68), channel_id=1, source_target_pairs={{0,16},{4,20},{8,24},{12,28},{16,0},{20,4},{24,8},{28,12},{1,17},{... | collective-permute-start | bytes 491528 | tf_op jit(solution)/shard_map/ppermute | solution.py:31
  186.8 4.9 %collective-permute-done.33 = bf16[16,5120]{1,0:T(8,128)(2,1)S(1)} collective-permute-done((bf16[16,5120]{1,0:T(8,128)(2,1)S(1)}, bf16[16,5120]{1,0:T(8,128)(2,1)S(1)}, u32[]{:S(2)}, u32[]{:S(2)}) %collective-permute-start.33) | collective-permute-done | bytes 163872 | tf_op jit(solution)/shard_map/ppermute | solution.py:31
  191.9 3.2 %collective-permute-done.17 = bf16[16,5120]{1,0:T(8,128)(2,1)S(1)} collective-permute-done((bf16[16,5120]{1,0:T(8,128)(2,1)S(1)}, bf16[16,5120]{1,0:T(8,128)(2,1)S(1)}, u32[]{:S(2)}, u32[]{:S(2)}) %collective-permute-start.17) | collective-permute-done | bytes 163872 | tf_op jit(solution)/shard_map/ppermute | solution.py:31
  205.3 3.5 %fusion = bf16[128,1792]{1,0:T(8,128)(2,1)} fusion(bf16[128,5120]{1,0:T(8,128)(2,1)S(1)} %select_dynamic-update-slice_fusion, bf16[5120,1792]{1,0:T(8,128)(2,1)S(1)} %hold.1, f32[1792]{0:T(1024)S(1)} %copy-done.14), kind=kOutput, calls=%fused_computation.3 | convolution fusion | flops 2349268992 | bytes 20126720 | tf_op jit(solution)/shard_map/dot_general | solution.py:450
  (201 shorter events, 61.9 us)
Async XLA Ops:
  0.6 41.1 %collective-permute-start = (bf16[432,5120]{1,0:T(8,128)(2,1)}, bf16[432,5120]{1,0:T(8,128)(2,1)}, u32[]{:S(2)}, u32[]{:S(2)}) collective-permute-start(bf16[432,5120]{1,0:T(8,128)(2,1)} %bitcast.30), channel_id=1, source_target_pairs={{0,1},{1,0},{2,3},{3,2},{4,5},{5,4},{6,7},{7,6},{8,9},{9,8},{10,11... | collective-permute-start | bytes 13271048 | tf_op jit(solution)/shard_map/ppermute | solution.py:31
  1.2 40.5 %collective-permute-start.1 = (bf16[432,5120]{1,0:T(8,128)(2,1)}, bf16[432,5120]{1,0:T(8,128)(2,1)}, u32[]{:S(2)}, u32[]{:S(2)}) collective-permute-start(bf16[432,5120]{1,0:T(8,128)(2,1)} %bitcast.36), channel_id=1, source_target_pairs={{0,1},{1,0},{2,3},{3,2},{4,5},{5,4},{6,7},{7,6},{8,9},{9,8},{10,11... | collective-permute-start | bytes 13271048 | tf_op jit(solution)/shard_map/ppermute | solution.py:31
  1.2 40.5 %collective-permute-start.2 = (bf16[432,5120]{1,0:T(8,128)(2,1)}, bf16[432,5120]{1,0:T(8,128)(2,1)}, u32[]{:S(2)}, u32[]{:S(2)}) collective-permute-start(bf16[432,5120]{1,0:T(8,128)(2,1)} %d0.1), channel_id=1, source_target_pairs={{0,1},{1,0},{2,3},{3,2},{4,5},{5,4},{6,7},{7,6},{8,9},{9,8},{10,11... | collective-permute-start | bytes 13271048 | tf_op jit(solution)/shard_map/ppermute | solution.py:31
  8.3 33.4 %all-to-all-start = ((bf16[16,2,64,256]{3,2,1,0:T(8,128)(2,1)}), bf16[16,2,64,256]{3,2,1,0:T(8,128)(2,1)S(1)}, u32[]{:S(2)}, u32[]{:S(2)}) async-start(bf16[16,2,64,256]{3,2,1,0:T(8,128)(2,1)} %bitcast.40), calls=%async_computation | async-start | bytes 2097152 | tf_op jit(solution)/shard_map/all_to_all | solution.py:206
  65.7 15.2 %collective-permute-start.22 = (bf16[16,5120]{1,0:T(8,128)(2,1)S(1)}, bf16[16,5120]{1,0:T(8,128)(2,1)}, u32[]{:S(2)}, u32[]{:S(2)}) collective-permute-start(bf16[16,5120]{1,0:T(8,128)(2,1)S(1)} %get-tuple-element.77), channel_id=1, source_target_pairs={{0,16},{4,20},{8,24},{12,28},{16,0},{20,4},{24,8},{28,12},{1,17},{... | collective-permute-start | bytes 491528 | tf_op jit(solution)/shard_map/ppermute | solution.py:31
  70.0 15.0 %collective-permute-start.5 = (bf16[16,5120]{1,0:T(8,128)(2,1)S(1)}, bf16[16,5120]{1,0:T(8,128)(2,1)S(1)}, u32[]{:S(2)}, u32[]{:S(2)}) collective-permute-start(bf16[16,5120]{1,0:T(8,128)(2,1)S(1)} %get-tuple-element.41), channel_id=1, source_target_pairs={{0,8},{4,12},{8,0},{12,4},{16,24},{20,28},{24,16},{28,20},{1,9},{5... | collective-permute-start | bytes 491528 | tf_op jit(solution)/shard_map/ppermute | solution.py:31
  70.1 24.7 %collective-permute-start.6 = (bf16[16,5120]{1,0:T(8,128)(2,1)S(1)}, bf16[16,5120]{1,0:T(8,128)(2,1)S(1)}, u32[]{:S(2)}, u32[]{:S(2)}) collective-permute-start(bf16[16,5120]{1,0:T(8,128)(2,1)S(1)} %get-tuple-element.41), channel_id=1, source_target_pairs={{0,16},{4,20},{8,24},{12,28},{16,0},{20,4},{24,8},{28,12},{1,17},{... | collective-permute-start | bytes 491528 | tf_op jit(solution)/shard_map/ppermute | solution.py:31
  75.7 19.1 %collective-permute-start.7 = (bf16[16,5120]{1,0:T(8,128)(2,1)S(1)}, bf16[16,5120]{1,0:T(8,128)(2,1)S(1)}, u32[]{:S(2)}, u32[]{:S(2)}) collective-permute-start(bf16[16,5120]{1,0:T(8,128)(2,1)S(1)} %get-tuple-element.41), channel_id=1, source_target_pairs={{0,24},{4,28},{8,16},{12,20},{16,8},{20,12},{24,0},{28,4},{1,25},{... | collective-permute-start | bytes 491528 | tf_op jit(solution)/shard_map/ppermute | solution.py:31
  82.0 19.1 %collective-permute-start.24 = (bf16[64,5120]{1,0:T(8,128)(2,1)S(1)}, bf16[64,5120]{1,0:T(8,128)(2,1)S(1)}, u32[]{:S(2)}, u32[]{:S(2)}) collective-permute-start(bf16[64,5120]{1,0:T(8,128)(2,1)S(1)} %pad_maximum_fusion.3), channel_id=1, source_target_pairs={{0,2},{1,3},{2,0},{3,1},{4,6},{5,7},{6,4},{7,5},{8,10},{9,11},{10,... | collective-permute-start | bytes 1966088 | tf_op jit(solution)/shard_map/ppermute | solution.py:31
  83.5 17.0 %collective-permute-start.25 = (bf16[64,5120]{1,0:T(8,128)(2,1)S(1)}, bf16[64,5120]{1,0:T(8,128)(2,1)S(1)}, u32[]{:S(2)}, u32[]{:S(2)}) collective-permute-start(bf16[64,5120]{1,0:T(8,128)(2,1)S(1)} %pad_maximum_fusion.3), channel_id=1, source_target_pairs={{0,4},{4,0},{8,12},{12,8},{16,20},{20,16},{24,28},{28,24},{1,5},{5... | collective-permute-start | bytes 1966088 | tf_op jit(solution)/shard_map/ppermute | solution.py:31
  94.8 19.9 %collective-permute-start.8 = (bf16[64,5120]{1,0:T(8,128)(2,1)S(1)}, bf16[64,5120]{1,0:T(8,128)(2,1)S(1)}, u32[]{:S(2)}, u32[]{:S(2)}) collective-permute-start(bf16[64,5120]{1,0:T(8,128)(2,1)S(1)} %pad_maximum_fusion), channel_id=1, source_target_pairs={{0,2},{1,3},{2,0},{3,1},{4,6},{5,7},{6,4},{7,5},{8,10},{9,11},{10,... | collective-permute-start | bytes 1966088 | tf_op jit(solution)/shard_map/ppermute | solution.py:31
  96.3 17.7 %collective-permute-start.9 = (bf16[64,5120]{1,0:T(8,128)(2,1)S(1)}, bf16[64,5120]{1,0:T(8,128)(2,1)S(1)}, u32[]{:S(2)}, u32[]{:S(2)}) collective-permute-start(bf16[64,5120]{1,0:T(8,128)(2,1)S(1)} %pad_maximum_fusion), channel_id=1, source_target_pairs={{0,4},{4,0},{8,12},{12,8},{16,20},{20,16},{24,28},{28,24},{1,5},{5... | collective-permute-start | bytes 1966088 | tf_op jit(solution)/shard_map/ppermute | solution.py:31
  100.5 19.0 %collective-permute-start.26 = (bf16[32,5120]{1,0:T(8,128)(2,1)S(1)}, bf16[32,5120]{1,0:T(8,128)(2,1)S(1)}, u32[]{:S(2)}, u32[]{:S(2)}) collective-permute-start(bf16[32,5120]{1,0:T(8,128)(2,1)S(1)} %slice.219), channel_id=1, source_target_pairs={{0,2},{1,3},{2,0},{3,1},{4,6},{5,7},{6,4},{7,5},{8,10},{9,11},{10,... | collective-permute-start | bytes 983048 | tf_op jit(solution)/shard_map/ppermute | solution.py:31
  101.1 19.8 %collective-permute-start.27 = (bf16[32,5120]{1,0:T(8,128)(2,1)S(1)}, bf16[32,5120]{1,0:T(8,128)(2,1)S(1)}, u32[]{:S(2)}, u32[]{:S(2)}) collective-permute-start(bf16[32,5120]{1,0:T(8,128)(2,1)S(1)} %slice.220), channel_id=1, source_target_pairs={{0,4},{4,0},{8,12},{12,8},{16,20},{20,16},{24,28},{28,24},{1,5},{5... | collective-permute-start | bytes 983048 | tf_op jit(solution)/shard_map/ppermute | solution.py:31
  114.0 19.8 %collective-permute-start.10 = (bf16[32,5120]{1,0:T(8,128)(2,1)S(1)}, bf16[32,5120]{1,0:T(8,128)(2,1)S(1)}, u32[]{:S(2)}, u32[]{:S(2)}) collective-permute-start(bf16[32,5120]{1,0:T(8,128)(2,1)S(1)} %slice.204), channel_id=1, source_target_pairs={{0,2},{1,3},{2,0},{3,1},{4,6},{5,7},{6,4},{7,5},{8,10},{9,11},{10,... | collective-permute-start | bytes 983048 | tf_op jit(solution)/shard_map/ppermute | solution.py:31
  114.7 19.2 %collective-permute-start.11 = (bf16[32,5120]{1,0:T(8,128)(2,1)S(1)}, bf16[32,5120]{1,0:T(8,128)(2,1)S(1)}, u32[]{:S(2)}, u32[]{:S(2)}) collective-permute-start(bf16[32,5120]{1,0:T(8,128)(2,1)S(1)} %slice.205), channel_id=1, source_target_pairs={{0,4},{4,0},{8,12},{12,8},{16,20},{20,16},{24,28},{28,24},{1,5},{5... | collective-permute-start | bytes 983048 | tf_op jit(solution)/shard_map/ppermute | solution.py:31
  132.2 15.5 %collective-permute-start.28 = (bf16[32,5120]{1,0:T(8,128)(2,1)S(1)}, bf16[32,5120]{1,0:T(8,128)(2,1)S(1)}, u32[]{:S(2)}, u32[]{:S(2)}) collective-permute-start(bf16[32,5120]{1,0:T(8,128)(2,1)S(1)} %get-tuple-element.59), channel_id=1, source_target_pairs={{0,4},{4,0},{8,12},{12,8},{16,20},{20,16},{24,28},{28,24},{1,5},{5... | collective-permute-start | bytes 983048 | tf_op jit(solution)/shard_map/ppermute | solution.py:31
  133.2 14.5 %collective-permute-start.30 = (bf16[32,5120]{1,0:T(8,128)(2,1)S(1)}, bf16[32,5120]{1,0:T(8,128)(2,1)S(1)}, u32[]{:S(2)}, u32[]{:S(2)}) collective-permute-start(bf16[32,5120]{1,0:T(8,128)(2,1)S(1)} %get-tuple-element.58), channel_id=1, source_target_pairs={{0,2},{1,3},{2,0},{3,1},{4,6},{5,7},{6,4},{7,5},{8,10},{9,11},{10,... | collective-permute-start | bytes 983048 | tf_op jit(solution)/shard_map/ppermute | solution.py:31
  148.0 21.0 %collective-permute-start.31 = (bf16[64,5120]{1,0:T(8,128)(2,1)S(1)}, bf16[64,5120]{1,0:T(8,128)(2,1)S(1)}, u32[]{:S(2)}, u32[]{:S(2)}) collective-permute-start(bf16[64,5120]{1,0:T(8,128)(2,1)S(1)} %pad_maximum_fusion.5), channel_id=1, source_target_pairs={{0,4},{4,0},{8,12},{12,8},{16,20},{20,16},{24,28},{28,24},{1,5},{5... | collective-permute-start | bytes 1966088 | tf_op jit(solution)/shard_map/ppermute | solution.py:31
  149.0 20.2 %collective-permute-start.29 = (bf16[64,5120]{1,0:T(8,128)(2,1)S(1)}, bf16[64,5120]{1,0:T(8,128)(2,1)S(1)}, u32[]{:S(2)}, u32[]{:S(2)}) collective-permute-start(bf16[64,5120]{1,0:T(8,128)(2,1)S(1)} %pad_maximum_fusion.4), channel_id=1, source_target_pairs={{0,2},{1,3},{2,0},{3,1},{4,6},{5,7},{6,4},{7,5},{8,10},{9,11},{10,... | collective-permute-start | bytes 1966088 | tf_op jit(solution)/shard_map/ppermute | solution.py:31
  157.1 22.2 %collective-permute-start.15 = (bf16[64,5120]{1,0:T(8,128)(2,1)S(1)}, bf16[64,5120]{1,0:T(8,128)(2,1)S(1)}, u32[]{:S(2)}, u32[]{:S(2)}) collective-permute-start(bf16[64,5120]{1,0:T(8,128)(2,1)S(1)} %pad_maximum_fusion.2), channel_id=1, source_target_pairs={{0,4},{4,0},{8,12},{12,8},{16,20},{20,16},{24,28},{28,24},{1,5},{5... | collective-permute-start | bytes 1966088 | tf_op jit(solution)/shard_map/ppermute | solution.py:31
  158.2 21.1 %collective-permute-start.13 = (bf16[64,5120]{1,0:T(8,128)(2,1)S(1)}, bf16[64,5120]{1,0:T(8,128)(2,1)S(1)}, u32[]{:S(2)}, u32[]{:S(2)}) collective-permute-start(bf16[64,5120]{1,0:T(8,128)(2,1)S(1)} %pad_maximum_fusion.1), channel_id=1, source_target_pairs={{0,2},{1,3},{2,0},{3,1},{4,6},{5,7},{6,4},{7,5},{8,10},{9,11},{10,... | collective-permute-start | bytes 1966088 | tf_op jit(solution)/shard_map/ppermute | solution.py:31
  169.6 16.8 %collective-permute-start.34 = (bf16[16,5120]{1,0:T(8,128)(2,1)S(1)}, bf16[16,5120]{1,0:T(8,128)(2,1)S(1)}, u32[]{:S(2)}, u32[]{:S(2)}) collective-permute-start(bf16[16,5120]{1,0:T(8,128)(2,1)S(1)} %get-tuple-element.72), channel_id=1, source_target_pairs={{0,24},{4,28},{8,16},{12,20},{16,8},{20,12},{24,0},{28,4},{1,25},{... | collective-permute-start | bytes 491528 | tf_op jit(solution)/shard_map/ppermute | solution.py:31
  172.2 19.4 %collective-permute-start.33 = (bf16[16,5120]{1,0:T(8,128)(2,1)S(1)}, bf16[16,5120]{1,0:T(8,128)(2,1)S(1)}, u32[]{:S(2)}, u32[]{:S(2)}) collective-permute-start(bf16[16,5120]{1,0:T(8,128)(2,1)S(1)} %get-tuple-element.73), channel_id=1, source_target_pairs={{0,16},{4,20},{8,24},{12,28},{16,0},{20,4},{24,8},{28,12},{1,17},{... | collective-permute-start | bytes 491528 | tf_op jit(solution)/shard_map/ppermute | solution.py:31
  (36 other events, 351.4 us)
